TPU v7x, 32 devices: a whole 2x2x4 slice. The times are simulated.
32 devices in a mesh: section: 4 (over z), seq: 8 (over y, x, core).
Axes of the slice: x: 2, y: 2, z: 4, core: 2. Of those that a mesh axis runs over, the one named last changes fastest.
Arguments:
- inbound_embedding_batches: bfloat16 [2, 128, 4096], replicated, may hold values from -16 to 16
- decoder_embedding_batches: bfloat16 [2, 128, 4096], replicated, may hold values from -16 to 16
- asking_projections: bfloat16 [4, 4096, 4096], P('section', None, 'seq'), may hold values from -0.09375 to 0.09375
- probe_projections: bfloat16 [4, 4096, 4096], P('section', None, 'seq'), may hold values from -0.09375 to 0.09375
- payload_projections: bfloat16 [4, 4096, 4096], P('section', None, 'seq'), may hold values from -0.09375 to 0.09375
- exit_projections: bfloat16 [4, 4096, 4096], P('section', 'seq'), may hold values from -0.1875 to 0.1875
- layer_rescale_weights: float32 [4, 4096], P('section'), may hold values from 0.1 to 1.9
- logit_sharpness: float32 [4, 64], P('section', 'seq'), may hold values from 0.5 to 3
- last_rescale_weights: float32 [4096], replicated, may hold values from 0.1 to 1.9
Outputs:
- section_out: bfloat16 [4, 2, 128, 4096], P('section')
All inputs are finite; a program needn't handle non-finite values.
Results may differ from a plain program's by a relative error of at most 0.025.
Values may be sent and summed in bfloat16 or wider, within the bound.
No kernel may reach another device: no remote copies, remote signals or barrier semaphores. Data moves between devices by JAX's collectives and lax.ppermute only.
A program may use at most 64 MiB of HBM per device.

v0:
```python
import math

import jax
import jax.numpy as jnp
from jax import lax
from jax.sharding import PartitionSpec as P

epsilon = 1e-06


def from_behind(x, axis, by):
    count = lax.axis_size(axis)
    pairs = [(i, i + by) for i in range(count) if 0 <= i + by < count]
    return lax.ppermute(x, axis, pairs)


def normalize(row_block, gain_vector):
    values = row_block.astype(jnp.float32)
    factor = lax.rsqrt(jnp.mean(values * values, axis=-1, keepdims=True) + epsilon)
    return (values * factor * gain_vector).astype(jnp.bfloat16)


def unit_heads(projected):
    return (
        projected * lax.rsqrt(jnp.mean(projected * projected, axis=-1, keepdims=True) + epsilon)
    ).astype(jnp.bfloat16)


def attend(queries, keys_proj, values_proj, logit_divisor):
    length = queries.shape[0]
    key_length = keys_proj.shape[0]
    head_count = logit_divisor.shape[0]
    head_size = queries.shape[1] // head_count
    unit_query = unit_heads(queries.reshape(length, head_count, head_size))
    unit_key = unit_heads(keys_proj.reshape(key_length, head_count, head_size))
    values = values_proj.astype(jnp.bfloat16).reshape(key_length, head_count, head_size)
    scores = jnp.einsum("qhd,khd->hqk", unit_query, unit_key, preferred_element_type=jnp.float32)
    scores = scores * (logit_divisor[:, None, None] / math.sqrt(head_size))
    weights = jnp.exp(scores)
    weights = (weights / jnp.sum(weights, axis=-1, keepdims=True)).astype(jnp.bfloat16)
    blended_payloads = jnp.einsum(
        "hqk,khd->qhd", weights, values, preferred_element_type=jnp.float32
    )
    return blended_payloads.astype(jnp.bfloat16).reshape(length, head_count * head_size)


def shards(
    inbound_embedding_batches,
    decoder_embedding_batches,
    asking_projections,
    probe_projections,
    payload_projections,
    exit_projections,
    layer_rescale_weights,
    logit_sharpness,
    last_rescale_weights,
):
    section_count = lax.axis_size("section")
    seq_count = lax.axis_size("seq")
    present_layer_index = lax.axis_index("section")
    seq_index = lax.axis_index("seq")
    encoders = 3 * section_count // 8
    batches = inbound_embedding_batches.shape[0]
    length = inbound_embedding_batches.shape[1]
    width = inbound_embedding_batches.shape[2]
    share_rows = length // seq_count
    first_own = seq_index * share_rows
    ticks = section_count + batches - 1
    w_query = asking_projections[0]
    w_key = probe_projections[0]
    w_value = payload_projections[0]
    w_output = exit_projections[0]
    logit_divisor = logit_sharpness[0]
    gain_vector = layer_rescale_weights[0]
    is_encoder = present_layer_index < encoders

    def layer(stream, memory_raw):
        rescaled_activations = normalize(stream, gain_vector)
        remote = normalize(memory_raw, last_rescale_weights)
        source_kv = jnp.where(is_encoder, rescaled_activations, remote)
        queries = jnp.dot(rescaled_activations, w_query, preferred_element_type=jnp.float32)
        keys_proj = jnp.dot(source_kv, w_key, preferred_element_type=jnp.float32)
        values_proj = jnp.dot(source_kv, w_value, preferred_element_type=jnp.float32)
        blended_payloads = attend(queries, keys_proj, values_proj, logit_divisor)
        update = lax.psum_scatter(
            jnp.dot(blended_payloads, w_output, preferred_element_type=jnp.float32).astype(
                jnp.bfloat16
            ),
            "seq",
            scatter_dimension=0,
            tiled=True,
        ).astype(jnp.float32)
        own_rows = lax.dynamic_slice_in_dim(stream, first_own, share_rows, 0)
        return (own_rows.astype(jnp.float32) + update).astype(jnp.bfloat16)

    blank = jnp.zeros((length, width), inbound_embedding_batches.dtype)
    holder = jnp.zeros((batches,) + blank.shape, inbound_embedding_batches.dtype)

    def advance(tick_index, state_tuple):
        arrived, carried, stored, finished = state_tuple
        offset = tick_index - present_layer_index
        batch_index = jnp.clip(offset, 0, batches - 1)
        valid = (offset >= 0) & (offset < batches)
        source_rows = lax.dynamic_index_in_dim(
            inbound_embedding_batches, batch_index, 0, keepdims=False
        )
        target_rows = lax.dynamic_index_in_dim(
            decoder_embedding_batches, batch_index, 0, keepdims=False
        )
        memory_kept = jnp.where(present_layer_index == encoders, arrived, carried)
        arrived_rows = arrived
        stream = jnp.where(
            present_layer_index == 0,
            source_rows,
            jnp.where(present_layer_index == encoders, target_rows, arrived_rows),
        )
        share = layer(stream, memory_kept)
        outgoing = lax.all_gather(share, "seq", axis=0, tiled=True)
        written = lax.dynamic_update_index_in_dim(finished, outgoing, batch_index, 0)
        finished = jnp.where(valid, written, finished)
        forward = jnp.where(present_layer_index >= encoders, memory_kept, outgoing)
        arrived, carried = from_behind((outgoing, forward), "section", 1)
        return (arrived, carried, stored, finished)

    final_state = lax.fori_loop(0, ticks, advance, (blank, blank, holder, holder))
    finished = final_state[3]
    return finished[None]


def solution(mesh):
    return jax.shard_map(
        shards,
        mesh=mesh,
        in_specs=(
            P(),
            P(),
            P("section", None, "seq"),
            P("section", None, "seq"),
            P("section", None, "seq"),
            P("section", "seq", None),
            P("section", None),
            P("section", "seq"),
            P(),
        ),
        out_specs=P("section", None, None, None),
        check_vma=False,
    )
```

profile of v0, /device:TPU:25, one launch (start us, length us, event | category | flops | bytes accessed | tf_op | source)
XLA Modules:
  0.0 653.7 jit_solution(16447415044279028495)
XLA Ops:
  9.3 637.5 %while.19 = (s32[]{:T(128)}, bf16[128,4096]{1,0:T(8,128)(2,1)}, bf16[128,4096]{1,0:T(8,128)(2,1)S(1)}, bf16[2,128,4096]{2,1,0:T(8,128)(2,1)}, pred[]{:T(512)}, /...) while((s32[]{:T(128)}, bf16[128,4096]{1,0:T(8,128)(2,1)}, ...), condition=%wide.region_7.8_spmd, body=%wide.region_0.7_spmd.sunk | while | flops 2200178176 | bytes 92264552 | solution.py:125
  13.7 4.2 multiply_reduce_fusion.5
  24.2 37.0 %reduce-scatter.2.cloned.1.call-done = bf16[16,4096]{1,0:T(8,128)(2,1)} async-done(((bf16[128,4096]{1,0:T(8,128)(2,1)}), bf16[16,4096]{1,0:T(8,128)(2,1)}) %reduce-scatter.2.cloned.1.call-update) | async-done | bytes 131088 | tf_op jit(solution)/shard_map/while/body/eval_jaxpr/reduce_scatter | solution.py:85
  62.8 24.4 %all-gather.2.cloned.1.call-done = bf16[128,4096]{1,0:T(8,128)(2,1)} async-done(((bf16[16,4096]{1,0:T(8,128)(2,1)}), bf16[128,4096]{1,0:T(8,128)(2,1)}) %all-gather.2.cloned.1.call-update) | async-done | bytes 1048592 | tf_op jit(solution)/shard_map/while/body/eval_jaxpr/all_gather | solution.py:118
  93.3 21.6 %collective-permute-done.1 = bf16[128,4096]{1,0:T(8,128)(2,1)S(1)} collective-permute-done((bf16[128,4096]{1,0:T(8,128)(2,1)}, bf16[128,4096]{1,0:T(8,128)(2,1)S(1)}, u32[]{:S(2)}, u32[]{:S(2)}) %collective-permute-start.1) | collective-permute-done | bytes 1048608 | tf_op jit(solution)/shard_map/while/body/eval_jaxpr/ppermute | solution.py:14
  114.9 22.6 %collective-permute-done = bf16[128,4096]{1,0:T(8,128)(2,1)} collective-permute-done((bf16[128,4096]{1,0:T(8,128)(2,1)S(1)}, bf16[128,4096]{1,0:T(8,128)(2,1)}, u32[]{:S(2)}, u32[]{:S(2)}) %collective-permute-start) | collective-permute-done | bytes 1048608 | tf_op jit(solution)/shard_map/while/body/eval_jaxpr/ppermute | solution.py:14
  152.3 36.4 %reduce-scatter.2.cloned.1.call-done = bf16[16,4096]{1,0:T(8,128)(2,1)} async-done(((bf16[128,4096]{1,0:T(8,128)(2,1)}), bf16[16,4096]{1,0:T(8,128)(2,1)}) %reduce-scatter.2.cloned.1.call-update) | async-done | bytes 131088 | tf_op jit(solution)/shard_map/while/body/eval_jaxpr/reduce_scatter | solution.py:85
  190.3 24.2 %all-gather.2.cloned.1.call-done = bf16[128,4096]{1,0:T(8,128)(2,1)} async-done(((bf16[16,4096]{1,0:T(8,128)(2,1)}), bf16[128,4096]{1,0:T(8,128)(2,1)}) %all-gather.2.cloned.1.call-update) | async-done | bytes 1048592 | tf_op jit(solution)/shard_map/while/body/eval_jaxpr/all_gather | solution.py:118
  220.6 21.6 %collective-permute-done.1 = bf16[128,4096]{1,0:T(8,128)(2,1)S(1)} collective-permute-done((bf16[128,4096]{1,0:T(8,128)(2,1)}, bf16[128,4096]{1,0:T(8,128)(2,1)S(1)}, u32[]{:S(2)}, u32[]{:S(2)}) %collective-permute-start.1) | collective-permute-done | bytes 1048608 | tf_op jit(solution)/shard_map/while/body/eval_jaxpr/ppermute | solution.py:14
  242.2 22.6 %collective-permute-done = bf16[128,4096]{1,0:T(8,128)(2,1)} collective-permute-done((bf16[128,4096]{1,0:T(8,128)(2,1)S(1)}, bf16[128,4096]{1,0:T(8,128)(2,1)}, u32[]{:S(2)}, u32[]{:S(2)}) %collective-permute-start) | collective-permute-done | bytes 1048608 | tf_op jit(solution)/shard_map/while/body/eval_jaxpr/ppermute | solution.py:14
  279.6 36.4 %reduce-scatter.2.cloned.1.call-done = bf16[16,4096]{1,0:T(8,128)(2,1)} async-done(((bf16[128,4096]{1,0:T(8,128)(2,1)}), bf16[16,4096]{1,0:T(8,128)(2,1)}) %reduce-scatter.2.cloned.1.call-update) | async-done | bytes 131088 | tf_op jit(solution)/shard_map/while/body/eval_jaxpr/reduce_scatter | solution.py:85
  317.6 24.2 %all-gather.2.cloned.1.call-done = bf16[128,4096]{1,0:T(8,128)(2,1)} async-done(((bf16[16,4096]{1,0:T(8,128)(2,1)}), bf16[128,4096]{1,0:T(8,128)(2,1)}) %all-gather.2.cloned.1.call-update) | async-done | bytes 1048592 | tf_op jit(solution)/shard_map/while/body/eval_jaxpr/all_gather | solution.py:118
  347.9 21.6 %collective-permute-done.1 = bf16[128,4096]{1,0:T(8,128)(2,1)S(1)} collective-permute-done((bf16[128,4096]{1,0:T(8,128)(2,1)}, bf16[128,4096]{1,0:T(8,128)(2,1)S(1)}, u32[]{:S(2)}, u32[]{:S(2)}) %collective-permute-start.1) | collective-permute-done | bytes 1048608 | tf_op jit(solution)/shard_map/while/body/eval_jaxpr/ppermute | solution.py:14
  369.5 22.6 %collective-permute-done = bf16[128,4096]{1,0:T(8,128)(2,1)} collective-permute-done((bf16[128,4096]{1,0:T(8,128)(2,1)S(1)}, bf16[128,4096]{1,0:T(8,128)(2,1)}, u32[]{:S(2)}, u32[]{:S(2)}) %collective-permute-start) | collective-permute-done | bytes 1048608 | tf_op jit(solution)/shard_map/while/body/eval_jaxpr/ppermute | solution.py:14
  396.3 4.2 multiply_reduce_fusion.5
  406.9 36.4 %reduce-scatter.2.cloned.1.call-done = bf16[16,4096]{1,0:T(8,128)(2,1)} async-done(((bf16[128,4096]{1,0:T(8,128)(2,1)}), bf16[16,4096]{1,0:T(8,128)(2,1)}) %reduce-scatter.2.cloned.1.call-update) | async-done | bytes 131088 | tf_op jit(solution)/shard_map/while/body/eval_jaxpr/reduce_scatter | solution.py:85
  444.9 24.3 %all-gather.2.cloned.1.call-done = bf16[128,4096]{1,0:T(8,128)(2,1)} async-done(((bf16[16,4096]{1,0:T(8,128)(2,1)}), bf16[128,4096]{1,0:T(8,128)(2,1)}) %all-gather.2.cloned.1.call-update) | async-done | bytes 1048592 | tf_op jit(solution)/shard_map/while/body/eval_jaxpr/all_gather | solution.py:118
  475.4 21.6 %collective-permute-done.1 = bf16[128,4096]{1,0:T(8,128)(2,1)S(1)} collective-permute-done((bf16[128,4096]{1,0:T(8,128)(2,1)}, bf16[128,4096]{1,0:T(8,128)(2,1)S(1)}, u32[]{:S(2)}, u32[]{:S(2)}) %collective-permute-start.1) | collective-permute-done | bytes 1048608 | tf_op jit(solution)/shard_map/while/body/eval_jaxpr/ppermute | solution.py:14
  497.0 22.6 %collective-permute-done = bf16[128,4096]{1,0:T(8,128)(2,1)} collective-permute-done((bf16[128,4096]{1,0:T(8,128)(2,1)S(1)}, bf16[128,4096]{1,0:T(8,128)(2,1)}, u32[]{:S(2)}, u32[]{:S(2)}) %collective-permute-start) | collective-permute-done | bytes 1048608 | tf_op jit(solution)/shard_map/while/body/eval_jaxpr/ppermute | solution.py:14
  523.8 4.2 multiply_reduce_fusion.5
  534.4 36.4 %reduce-scatter.2.cloned.1.call-done = bf16[16,4096]{1,0:T(8,128)(2,1)} async-done(((bf16[128,4096]{1,0:T(8,128)(2,1)}), bf16[16,4096]{1,0:T(8,128)(2,1)}) %reduce-scatter.2.cloned.1.call-update) | async-done | bytes 131088 | tf_op jit(solution)/shard_map/while/body/eval_jaxpr/reduce_scatter | solution.py:85
  572.4 24.2 %all-gather.2.cloned.1.call-done = bf16[128,4096]{1,0:T(8,128)(2,1)} async-done(((bf16[16,4096]{1,0:T(8,128)(2,1)}), bf16[128,4096]{1,0:T(8,128)(2,1)}) %all-gather.2.cloned.1.call-update) | async-done | bytes 1048592 | tf_op jit(solution)/shard_map/while/body/eval_jaxpr/all_gather | solution.py:118
  602.7 21.6 %collective-permute-done.1 = bf16[128,4096]{1,0:T(8,128)(2,1)S(1)} collective-permute-done((bf16[128,4096]{1,0:T(8,128)(2,1)}, bf16[128,4096]{1,0:T(8,128)(2,1)S(1)}, u32[]{:S(2)}, u32[]{:S(2)}) %collective-permute-start.1) | collective-permute-done | bytes 1048608 | tf_op jit(solution)/shard_map/while/body/eval_jaxpr/ppermute | solution.py:14
  624.3 22.6 %collective-permute-done = bf16[128,4096]{1,0:T(8,128)(2,1)} collective-permute-done((bf16[128,4096]{1,0:T(8,128)(2,1)S(1)}, bf16[128,4096]{1,0:T(8,128)(2,1)}, u32[]{:S(2)}, u32[]{:S(2)}) %collective-permute-start) | collective-permute-done | bytes 1048608 | tf_op jit(solution)/shard_map/while/body/eval_jaxpr/ppermute | solution.py:14
  (141 shorter events, 102.2 us)
Async XLA Ops:
  9.3 51.9 %reduce-scatter.2.cloned.1.call-start = ((), (), s32[]{:S(2)}) async-start(), calls=%async_computation.1 | async-start | bytes 1179648 | tf_op jit(solution)/shard_map/while/body/eval_jaxpr/reduce_scatter | solution.py:85
  13.7 4.3 copy-start.2
  24.2 63.0 %all-gather.2.cloned.1.call-start = ((), (), s32[]{:S(2)}) async-start(), calls=%async_computation.2 | async-start | bytes 1179648 | tf_op jit(solution)/shard_map/while/body/eval_jaxpr/all_gather | solution.py:118
  88.3 26.6 %collective-permute-start.1 = (bf16[128,4096]{1,0:T(8,128)(2,1)}, bf16[128,4096]{1,0:T(8,128)(2,1)S(1)}, u32[]{:S(2)}, u32[]{:S(2)}) collective-permute-start(bf16[128,4096]{1,0:T(8,128)(2,1)} %broadcast_select_fusion.4), channel_id=1, source_target_pairs={{0,8},{8,16},{16,24},{1,9},{9,17},{17,25},{2,10},{10,18},{18,26},{... | collective-permute-start | bytes 3145736 | tf_op jit(solution)/shard_map/while/body/eval_jaxpr/ppermute | solution.py:14
  89.6 47.9 %collective-permute-start = (bf16[128,4096]{1,0:T(8,128)(2,1)S(1)}, bf16[128,4096]{1,0:T(8,128)(2,1)}, u32[]{:S(2)}, u32[]{:S(2)}) collective-permute-start(bf16[128,4096]{1,0:T(8,128)(2,1)S(1)} %copy-done), channel_id=1, source_target_pairs={{0,8},{8,16},{16,24},{1,9},{9,17},{17,25},{2,10},{10,18},{18,26},{... | collective-permute-start | bytes 3145736 | tf_op jit(solution)/shard_map/while/body/eval_jaxpr/ppermute | solution.py:14
  137.5 51.2 %reduce-scatter.2.cloned.1.call-start = ((), (), s32[]{:S(2)}) async-start(), calls=%async_computation.1 | async-start | bytes 1179648 | tf_op jit(solution)/shard_map/while/body/eval_jaxpr/reduce_scatter | solution.py:85
  152.2 62.3 %all-gather.2.cloned.1.call-start = ((), (), s32[]{:S(2)}) async-start(), calls=%async_computation.2 | async-start | bytes 1179648 | tf_op jit(solution)/shard_map/while/body/eval_jaxpr/all_gather | solution.py:118
  215.6 26.6 %collective-permute-start.1 = (bf16[128,4096]{1,0:T(8,128)(2,1)}, bf16[128,4096]{1,0:T(8,128)(2,1)S(1)}, u32[]{:S(2)}, u32[]{:S(2)}) collective-permute-start(bf16[128,4096]{1,0:T(8,128)(2,1)} %broadcast_select_fusion.4), channel_id=1, source_target_pairs={{0,8},{8,16},{16,24},{1,9},{9,17},{17,25},{2,10},{10,18},{18,26},{... | collective-permute-start | bytes 3145736 | tf_op jit(solution)/shard_map/while/body/eval_jaxpr/ppermute | solution.py:14
  216.9 47.9 %collective-permute-start = (bf16[128,4096]{1,0:T(8,128)(2,1)S(1)}, bf16[128,4096]{1,0:T(8,128)(2,1)}, u32[]{:S(2)}, u32[]{:S(2)}) collective-permute-start(bf16[128,4096]{1,0:T(8,128)(2,1)S(1)} %copy-done), channel_id=1, source_target_pairs={{0,8},{8,16},{16,24},{1,9},{9,17},{17,25},{2,10},{10,18},{18,26},{... | collective-permute-start | bytes 3145736 | tf_op jit(solution)/shard_map/while/body/eval_jaxpr/ppermute | solution.py:14
  264.8 51.2 %reduce-scatter.2.cloned.1.call-start = ((), (), s32[]{:S(2)}) async-start(), calls=%async_computation.1 | async-start | bytes 1179648 | tf_op jit(solution)/shard_map/while/body/eval_jaxpr/reduce_scatter | solution.py:85
  269.0 4.3 copy-start.2
  279.5 62.3 %all-gather.2.cloned.1.call-start = ((), (), s32[]{:S(2)}) async-start(), calls=%async_computation.2 | async-start | bytes 1179648 | tf_op jit(solution)/shard_map/while/body/eval_jaxpr/all_gather | solution.py:118
  342.9 26.6 %collective-permute-start.1 = (bf16[128,4096]{1,0:T(8,128)(2,1)}, bf16[128,4096]{1,0:T(8,128)(2,1)S(1)}, u32[]{:S(2)}, u32[]{:S(2)}) collective-permute-start(bf16[128,4096]{1,0:T(8,128)(2,1)} %broadcast_select_fusion.4), channel_id=1, source_target_pairs={{0,8},{8,16},{16,24},{1,9},{9,17},{17,25},{2,10},{10,18},{18,26},{... | collective-permute-start | bytes 3145736 | tf_op jit(solution)/shard_map/while/body/eval_jaxpr/ppermute | solution.py:14
  344.2 47.9 %collective-permute-start = (bf16[128,4096]{1,0:T(8,128)(2,1)S(1)}, bf16[128,4096]{1,0:T(8,128)(2,1)}, u32[]{:S(2)}, u32[]{:S(2)}) collective-permute-start(bf16[128,4096]{1,0:T(8,128)(2,1)S(1)} %copy-done), channel_id=1, source_target_pairs={{0,8},{8,16},{16,24},{1,9},{9,17},{17,25},{2,10},{10,18},{18,26},{... | collective-permute-start | bytes 3145736 | tf_op jit(solution)/shard_map/while/body/eval_jaxpr/ppermute | solution.py:14
  392.1 51.2 %reduce-scatter.2.cloned.1.call-start = ((), (), s32[]{:S(2)}) async-start(), calls=%async_computation.1 | async-start | bytes 1179648 | tf_op jit(solution)/shard_map/while/body/eval_jaxpr/reduce_scatter | solution.py:85
  396.3 4.3 copy-start.2
  406.9 62.4 %all-gather.2.cloned.1.call-start = ((), (), s32[]{:S(2)}) async-start(), calls=%async_computation.2 | async-start | bytes 1179648 | tf_op jit(solution)/shard_map/while/body/eval_jaxpr/all_gather | solution.py:118
  470.3 26.6 %collective-permute-start.1 = (bf16[128,4096]{1,0:T(8,128)(2,1)}, bf16[128,4096]{1,0:T(8,128)(2,1)S(1)}, u32[]{:S(2)}, u32[]{:S(2)}) collective-permute-start(bf16[128,4096]{1,0:T(8,128)(2,1)} %broadcast_select_fusion.4), channel_id=1, source_target_pairs={{0,8},{8,16},{16,24},{1,9},{9,17},{17,25},{2,10},{10,18},{18,26},{... | collective-permute-start | bytes 3145736 | tf_op jit(solution)/shard_map/while/body/eval_jaxpr/ppermute | solution.py:14
  471.6 47.9 %collective-permute-start = (bf16[128,4096]{1,0:T(8,128)(2,1)S(1)}, bf16[128,4096]{1,0:T(8,128)(2,1)}, u32[]{:S(2)}, u32[]{:S(2)}) collective-permute-start(bf16[128,4096]{1,0:T(8,128)(2,1)S(1)} %copy-done), channel_id=1, source_target_pairs={{0,8},{8,16},{16,24},{1,9},{9,17},{17,25},{2,10},{10,18},{18,26},{... | collective-permute-start | bytes 3145736 | tf_op jit(solution)/shard_map/while/body/eval_jaxpr/ppermute | solution.py:14
  519.5 51.2 %reduce-scatter.2.cloned.1.call-start = ((), (), s32[]{:S(2)}) async-start(), calls=%async_computation.1 | async-start | bytes 1179648 | tf_op jit(solution)/shard_map/while/body/eval_jaxpr/reduce_scatter | solution.py:85
  523.8 4.3 copy-start.2
  534.3 62.2 %all-gather.2.cloned.1.call-start = ((), (), s32[]{:S(2)}) async-start(), calls=%async_computation.2 | async-start | bytes 1179648 | tf_op jit(solution)/shard_map/while/body/eval_jaxpr/all_gather | solution.py:118
  597.6 26.6 %collective-permute-start.1 = (bf16[128,4096]{1,0:T(8,128)(2,1)}, bf16[128,4096]{1,0:T(8,128)(2,1)S(1)}, u32[]{:S(2)}, u32[]{:S(2)}) collective-permute-start(bf16[128,4096]{1,0:T(8,128)(2,1)} %broadcast_select_fusion.4), channel_id=1, source_target_pairs={{0,8},{8,16},{16,24},{1,9},{9,17},{17,25},{2,10},{10,18},{18,26},{... | collective-permute-start | bytes 3145736 | tf_op jit(solution)/shard_map/while/body/eval_jaxpr/ppermute | solution.py:14
  598.9 47.9 %collective-permute-start = (bf16[128,4096]{1,0:T(8,128)(2,1)S(1)}, bf16[128,4096]{1,0:T(8,128)(2,1)}, u32[]{:S(2)}, u32[]{:S(2)}) collective-permute-start(bf16[128,4096]{1,0:T(8,128)(2,1)S(1)} %copy-done), channel_id=1, source_target_pairs={{0,8},{8,16},{16,24},{1,9},{9,17},{17,25},{2,10},{10,18},{18,26},{... | collective-permute-start | bytes 3145736 | tf_op jit(solution)/shard_map/while/body/eval_jaxpr/ppermute | solution.py:14
  (14 other events, 40.5 us)
Sparse Core Ops, SparseCore 0:
  24.3 36.8 reduce-scatter.1
  63.1 24.0 all-gather.1
  152.3 36.2 reduce-scatter.1
  190.4 24.0 all-gather.1
  279.7 36.2 reduce-scatter.1
  317.7 24.0 all-gather.1
  407.0 36.2 reduce-scatter.1
  445.2 24.0 all-gather.1
  534.4 36.2 reduce-scatter.1
  572.5 24.0 all-gather.1
where the time goes:
time: 656 us; the launch traced here: 654 us
  waiting for transfers between devices  525 us (80%)
  matrix products  56.7 us (9%)
  other arithmetic  41.5 us (6%)
  between operations  13.4 us (2%)
  starting transfers between devices  13.1 us (2%)
    ppermute x10, waiting for transfers between devices, from_behind(): return lax.ppermute(x, axis, pairs)  221 us
    reduce_scatter x5, waiting for transfers between devices, layer(): lax.psum_scatter(jnp.dot(blended_payloads, w_output, preferred_element_ty...  183 us
    all_gather x5, waiting for transfers between devices, advance(): outgoing = lax.all_gather(share, 'seq', axis=0, tiled=True)  121 us
    dot_general x5, matrix products, layer(): keys_proj = jnp.dot(source_kv, w_key, preferred_element_type=jnp.float32)  21.2 us
    dot_general x5, matrix products, layer(): jnp.dot(blended_payloads, w_output, preferred_element_type=jnp.float32)  19.6 us
    reduce_sum x5, other arithmetic, normalize(): jnp.mean(values * values, axis=-1, keepdims=True) + epsilon  15.8 us
  transfers between devices with their start and end apart: 20, of which 20 were waited for; matrix products, arithmetic and copies ran while one was open for 2% of the time, Pallas kernels for 0%

commit v1 on v0

v1 whole, which is shorter than its diff:
```python
import functools

import jax
import jax.numpy as jnp
from jax import lax
from jax.experimental import pallas as pl
from jax.experimental.pallas import tpu as pltpu
from jax.sharding import PartitionSpec as P

EPSILON = 1e-06
LANES = 128
BF16 = jnp.bfloat16
F32 = jnp.float32
VMEM_LIMIT = 56 * 1024 * 1024
ANY = pl.BlockSpec(memory_space=pl.ANY)
IN_VMEM = pl.BlockSpec(memory_space=pltpu.VMEM)
IN_SMEM = pl.BlockSpec(memory_space=pltpu.SMEM)


def params():
    return pltpu.CompilerParams(vmem_limit_bytes=VMEM_LIMIT)


class Copies:
    def __init__(self, sems):
        self.sems, self.used = sems, 0

    def start(self, src, dst):
        copy = pltpu.make_async_copy(src, dst, self.sems.at[self.used])
        self.used += 1
        copy.start()
        return copy


def normalize_rows(raw, out, gain, rows, step=16):
    def body(i, _):
        at = pl.ds(pl.multiple_of(i * step, step), step)
        values = raw[at, :].astype(F32)
        factor = lax.rsqrt(jnp.mean(values * values, axis=-1, keepdims=True) + EPSILON)
        out[at, :] = (values * factor * gain[...]).astype(BF16)
        return 0

    lax.fori_loop(0, rows // step, body, 0)


def lane_masks(rows, head):
    lane = lax.broadcasted_iota(jnp.int32, (rows, LANES), 1)
    return [(lane // head) == i for i in range(LANES // head)]


def unit(block, head):
    masks = lane_masks(block.shape[0], head)
    squares = block * block
    factor = None
    for mask in masks:
        total = jnp.sum(jnp.where(mask, squares, 0.0), axis=-1, keepdims=True)
        own = lax.rsqrt(total / head + EPSILON)
        factor = own if factor is None else jnp.where(mask, own, factor)
    return (block * factor).astype(BF16)


def attend(queries, keys, values, scales, head):
    rows = queries.shape[0]
    masks = lane_masks(rows, head)
    stacked = jnp.concatenate(
        [jnp.where(mask, queries, jnp.zeros_like(queries)) for mask in masks], axis=0
    )
    scores = lax.dot_general(
        stacked, keys, (((1,), (1,)), ((), ())), preferred_element_type=F32
    )
    weights = []
    for i, scale in enumerate(scales):
        raised = jnp.exp(scores[i * rows : (i + 1) * rows] * scale)
        weights.append((raised / jnp.sum(raised, axis=-1, keepdims=True)).astype(BF16))
    mixed = jnp.dot(jnp.concatenate(weights, axis=0), values, preferred_element_type=F32)
    out = mixed[:rows]
    for i in range(1, len(scales)):
        out = jnp.where(masks[i], mixed[i * rows : (i + 1) * rows], out)
    return out.astype(BF16)


class Weight:
    def __init__(self, copies, sources, scratch, wide):
        self.scratch, self.chunks = scratch, []
        for source in sources:
            for at in range(0, source.shape[1], wide):
                self.chunks.append(
                    copies.start(source.at[:, pl.ds(at, wide)], scratch.at[len(self.chunks)])
                )

    def times(self, rows, chunk):
        self.chunks[chunk].wait()
        return jnp.dot(rows, self.scratch[chunk], preferred_element_type=F32)


class OutWeight:
    def __init__(self, copies, sources, scratch, wide):
        self.scratch, self.wide, self.chunks = scratch, wide, []
        for at in range(0, scratch.shape[1], wide):
            parts, low = [], 0
            for source in sources:
                height = source.shape[0]
                parts.append(
                    copies.start(
                        source.at[:, pl.ds(at, wide)],
                        scratch.at[pl.ds(low, height), pl.ds(at, wide)],
                    )
                )
                low += height
            self.chunks.append(parts)

    def into(self, mixture, outs):
        height = mixture.shape[0] // len(outs)
        for i, parts in enumerate(self.chunks):
            for part in parts:
                part.wait()
            at = pl.ds(i * self.wide, self.wide)
            product = jnp.dot(mixture, self.scratch[:, at], preferred_element_type=F32).astype(BF16)
            for k, out in enumerate(outs):
                out[:, at] = product[k * height : (k + 1) * height]


def load_rows(copies, source, batch, scratch, low, chip, blocks):
    height = source.shape[1] // blocks
    waits = []
    for j in range(blocks):
        at = pl.multiple_of((chip ^ j) * height, height)
        waits.append(
            copies.start(
                source.at[batch, pl.ds(at, height), :],
                scratch.at[pl.ds(low + j * height, height), :],
            )
        )
    return waits


def load_pieces(copies, pieces, scratch):
    waits, low = [], 0
    for piece in pieces:
        height = piece.shape[0]
        waits.append(copies.start(piece, scratch.at[pl.ds(low, height), :]))
        low += height
    return waits


WIDE = 256
OUT_WIDE = 1024


def first_kernel(config, place, sharp, gain, source, wq, wk, wv, own_ref, other_ref,
                 raw, rows, wq_s, wk_s, wv_s, sems):
    head, blocks, length = config
    copies = Copies(sems)
    chip, core = place[0], place[1]
    waits = load_rows(copies, source, core, raw, 0, chip, blocks)
    waits += load_rows(copies, source, 1 - core, raw, length, chip, blocks)
    weights = [Weight(copies, [w], s, WIDE) for w, s in ((wq, wq_s), (wk, wk_s), (wv, wv_s))]
    for wait in waits:
        wait.wait()
    normalize_rows(raw, rows, gain, raw.shape[0])
    normed = rows[...]
    per = LANES // head
    for chunk in range(wq.shape[1] // WIDE):
        q, k, v = (w.times(normed, chunk) for w in weights)
        v = v.astype(BF16)
        for g in range(WIDE // LANES):
            lanes = slice(g * LANES, (g + 1) * LANES)
            group = chunk * (WIDE // LANES) + g
            scales = [sharp[group * per + i] for i in range(per)]
            uq, uk = unit(q[:, lanes], head), unit(k[:, lanes], head)
            for b, out in enumerate((own_ref, other_ref)):
                at = slice(b * length, (b + 1) * length)
                out[:, group * LANES : (group + 1) * LANES] = attend(
                    uq[at], uk[at], v[at, lanes], scales, head
                )


def out_kernel(config, own, other, wo_own, wo_other, *refs):
    outs, (mixture, wo_s, sems) = refs[:-3], refs[-3:]
    copies = Copies(sems)
    waits = [
        copies.start(part, mixture.at[:, pl.ds(i * part.shape[1], part.shape[1])])
        for i, part in enumerate((own, other))
    ]
    weight = OutWeight(copies, (wo_own, wo_other), wo_s, OUT_WIDE)
    for wait in waits:
        wait.wait()
    weight.into(mixture[...], outs)


def query_kernel(config, place, gain, source, wq_own, wq_other, uq_ref, raw, rows, wq_s, sems):
    head, blocks, length = config
    copies = Copies(sems)
    waits = load_rows(copies, source, place[1], raw, 0, place[0], blocks)
    weight = Weight(copies, (wq_own, wq_other), wq_s, WIDE)
    for wait in waits:
        wait.wait()
    normalize_rows(raw, rows, gain, length)
    project_units(rows[...], weight, uq_ref, head)


def project_units(normed, weight, out, head):
    for chunk in range(len(weight.chunks)):
        product = weight.times(normed, chunk)
        for g in range(WIDE // LANES):
            at = chunk * WIDE + g * LANES
            out[:, at : at + LANES] = unit(product[:, g * LANES : (g + 1) * LANES], head)


def memory_kernel(config, count, gain, *refs):
    head, blocks, length = config
    pieces, refs = refs[:count], refs[count:]
    wk_own, wk_other, wv_own, wv_other, uk_ref, v_ref, raw, rows, wk_s, wv_s, sems = refs
    copies = Copies(sems)
    waits = load_pieces(copies, pieces, raw)
    wk = Weight(copies, (wk_own, wk_other), wk_s, WIDE)
    wv = Weight(copies, (wv_own, wv_other), wv_s, WIDE)
    for wait in waits:
        wait.wait()
    normalize_rows(raw, rows, gain, length)
    normed = rows[...]
    project_units(normed, wk, uk_ref, head)
    for chunk in range(len(wv.chunks)):
        v_ref[:, chunk * WIDE : (chunk + 1) * WIDE] = wv.times(normed, chunk).astype(BF16)


def attend_all(uq, uk, v, sharps, mixture, head):
    per = LANES // head
    each = sharps[0].shape[0]
    for group in range(uq.shape[1] // LANES):
        lanes = slice(group * LANES, (group + 1) * LANES)
        scales = []
        for i in range(per):
            index = group * per + i
            scales.append(sharps[index // each][index % each])
        mixture[:, lanes] = attend(uq[:, lanes], uk[:, lanes], v[:, lanes], scales, head)


def mix_kernel(config, sharp_own, sharp_other, uq, uk, v, wo_own, wo_other, *refs):
    head = config[0]
    outs, (mixture, wo_s, sems) = refs[:-3], refs[-3:]
    copies = Copies(sems)
    weight = OutWeight(copies, (wo_own, wo_other), wo_s, OUT_WIDE)
    attend_all(uq, uk, v, (sharp_own, sharp_other), mixture, head)
    weight.into(mixture[...], outs)


def section_kernel(config, count, sharp_own, sharp_other, gain, *refs):
    head, blocks, length = config
    pieces, refs = refs[:count], refs[count:]
    uk, v, wq_own, wq_other, wo_own, wo_other = refs[:6]
    outs, (raw, rows, uq, mixture, wq_s, wo_s, sems) = refs[6:-7], refs[-7:]
    copies = Copies(sems)
    waits = load_pieces(copies, pieces, raw)
    wq = Weight(copies, (wq_own, wq_other), wq_s, WIDE)
    wo = OutWeight(copies, (wo_own, wo_other), wo_s, OUT_WIDE)
    for wait in waits:
        wait.wait()
    normalize_rows(raw, rows, gain, length)
    project_units(rows[...], wq, uq, head)
    attend_all(uq, uk, v, (sharp_own, sharp_other), mixture, head)
    wo.into(mixture[...], outs)


def place_kernel(count, place, *refs):
    pieces, out, sems = refs[:-2], refs[-2], refs[-1]
    copies = Copies(sems)
    chip, core = place[0], place[1]
    waits = []
    for i, piece in enumerate(pieces):
        height = piece.shape[0]
        batch = core if i < count else 1 - core
        at = pl.multiple_of((chip ^ (i % count)) * height, height)
        waits.append(copies.start(piece, out.at[batch, pl.ds(at, height), :]))
    for wait in waits:
        wait.wait()


def shards(
    inbound_embedding_batches,
    decoder_embedding_batches,
    asking_projections,
    probe_projections,
    payload_projections,
    exit_projections,
    layer_rescale_weights,
    logit_sharpness,
    last_rescale_weights,
):
    sections = lax.axis_size("section")
    seq = lax.axis_size("seq")
    section = lax.axis_index("section")
    position = lax.axis_index("seq")
    encoders = 3 * sections // 8
    batches, length, width = inbound_embedding_batches.shape
    cores = 2
    blocks = seq // cores
    assert batches == cores and blocks & (blocks - 1) == 0
    core, chip = position % cores, position // cores
    height = length // blocks
    heads = logit_sharpness.shape[1]
    inner = asking_projections.shape[2]
    head = inner // heads
    both = cores * inner
    config = (head, blocks, length)

    def flip(bits, only_later=False):
        pairs = [(i, i ^ bits) for i in range(seq)]
        if not only_later:
            return lambda x: lax.ppermute(x, "seq", pairs)
        pairs = [(s * seq + a, s * seq + b) for s in range(1, sections) for a, b in pairs]
        return lambda x: lax.ppermute(x, ("section", "seq"), pairs)

    def up(x, source, target):
        return lax.ppermute(x, "section", [(source, target)])

    to_core = flip(1)
    to_chip = [None] + [flip(j * cores) for j in range(1, blocks)]
    later_core = flip(1, only_later=True)

    wq, wk, wv, wo = (
        w[0] for w in (asking_projections, probe_projections, payload_projections, exit_projections)
    )
    gain = layer_rescale_weights
    last_gain = last_rescale_weights.reshape(1, width)
    sharp = logit_sharpness[0] * (head ** -0.5)
    sharp_other = to_core(sharp)
    wo_other = to_core(wo)
    wk_other, wv_other, wq_other = later_core(wk), later_core(wv), later_core(wq)
    place = jnp.stack([chip, core]).astype(jnp.int32)

    def sds(shape, dtype=BF16):
        return jax.ShapeDtypeStruct(shape, dtype)

    def in_chunks(columns):
        return pltpu.VMEM((columns // WIDE, width, WIDE), BF16)

    row_scratch = pltpu.VMEM((length, width), BF16)
    out_scratch = [pltpu.VMEM((length, both), BF16), pltpu.VMEM((both, width), BF16)]
    partials = [sds((height, width))] * blocks
    chunks = both // WIDE
    out_copies = cores * (width // OUT_WIDE)

    def sems(n):
        return pltpu.SemaphoreType.DMA((n,))

    def gather(share):
        return [share] + [to_chip[j](share) for j in range(1, blocks)]

    def finish(parts, residual):
        total = residual.astype(F32) + parts[0].astype(F32)
        for j in range(1, blocks):
            total = total + to_chip[j](parts[j]).astype(F32)
        return total.astype(BF16)

    def own_rows(source):
        return lax.dynamic_slice(source, (core, chip * height, 0), (1, height, width))[0]

    mixed_own, mixed_other = pl.pallas_call(
        functools.partial(first_kernel, config),
        out_shape=[sds((length, inner))] * 2,
        in_specs=[IN_SMEM, IN_SMEM, IN_VMEM, ANY, ANY, ANY, ANY],
        out_specs=[IN_VMEM] * 2,
        scratch_shapes=[
            pltpu.VMEM((batches * length, width), BF16),
            pltpu.VMEM((batches * length, width), BF16),
            in_chunks(inner), in_chunks(inner), in_chunks(inner),
            sems(batches * blocks + 3 * inner // WIDE),
        ],
        compiler_params=params(),
    )(place, sharp, gain, inbound_embedding_batches, wq, wk, wv)
    mixed_other = to_core(mixed_other)
    parts = pl.pallas_call(
        functools.partial(out_kernel, config),
        out_shape=partials,
        in_specs=[ANY] * 4,
        out_specs=[IN_VMEM] * blocks,
        scratch_shapes=out_scratch + [sems(2 + out_copies)],
        compiler_params=params(),
    )(mixed_own, mixed_other, wo, wo_other)
    share = finish(parts, own_rows(inbound_embedding_batches))
    kept = share

    unit_queries = pl.pallas_call(
        functools.partial(query_kernel, config),
        out_shape=sds((length, both)),
        in_specs=[IN_SMEM, IN_VMEM, ANY, ANY, ANY],
        out_specs=IN_VMEM,
        scratch_shapes=[row_scratch, row_scratch, in_chunks(both), sems(blocks + chunks)],
        compiler_params=params(),
    )(place, gain, decoder_embedding_batches, wq, wq_other)

    def project_memory(pieces, scale):
        return pl.pallas_call(
            functools.partial(memory_kernel, config, blocks),
            out_shape=[sds((length, both))] * 2,
            in_specs=[IN_VMEM] + [ANY] * (blocks + 4),
            out_specs=[IN_VMEM] * 2,
            scratch_shapes=[row_scratch, row_scratch, in_chunks(both), in_chunks(both),
                            sems(blocks + 2 * chunks)],
            compiler_params=params(),
        )(scale, *pieces, wk, wk_other, wv, wv_other)

    for step in range(1, sections):
        if step == encoders:
            memory = None
            for target in range(step, sections):
                arrived = up(share, step - 1, target)
                memory = arrived if memory is None else jnp.where(section == target, arrived, memory)
            unit_keys, values = project_memory(gather(memory), last_gain)
            residual = own_rows(decoder_embedding_batches)
            parts = pl.pallas_call(
                functools.partial(mix_kernel, config),
                out_shape=partials,
                in_specs=[IN_SMEM] * 2 + [IN_VMEM] * 3 + [ANY] * 2,
                out_specs=[IN_VMEM] * blocks,
                scratch_shapes=out_scratch + [sems(out_copies)],
                compiler_params=params(),
            )(sharp, sharp_other, unit_queries, unit_keys, values, wo, wo_other)
        else:
            residual = up(share, step - 1, step)
            pieces = gather(residual)
            if step < encoders:
                unit_keys, values = project_memory(pieces, gain)
            parts = pl.pallas_call(
                functools.partial(section_kernel, config, blocks),
                out_shape=partials,
                in_specs=[IN_SMEM] * 2 + [IN_VMEM] + [ANY] * blocks + [IN_VMEM] * 2 + [ANY] * 4,
                out_specs=[IN_VMEM] * blocks,
                scratch_shapes=[
                    row_scratch, row_scratch, pltpu.VMEM((length, both), BF16), out_scratch[0],
                    in_chunks(both), out_scratch[1], sems(blocks + chunks + out_copies),
                ],
                compiler_params=params(),
            )(sharp, sharp_other, gain, *pieces, unit_keys, values, wq, wq_other, wo, wo_other)
        share = finish(parts, residual)
        kept = jnp.where(section == step, share, kept)

    pieces = gather(kept)
    pieces = pieces + [to_core(piece) for piece in pieces]
    finished = pl.pallas_call(
        functools.partial(place_kernel, blocks),
        out_shape=sds((batches, length, width)),
        in_specs=[IN_SMEM] + [ANY] * len(pieces),
        out_specs=ANY,
        scratch_shapes=[sems(len(pieces))],
        compiler_params=params(),
    )(place, *pieces)
    return finished[None]


def solution(mesh):
    return jax.shard_map(
        shards,
        mesh=mesh,
        in_specs=(
            P(),
            P(),
            P("section", None, "seq"),
            P("section", None, "seq"),
            P("section", None, "seq"),
            P("section", "seq", None),
            P("section", None),
            P("section", "seq"),
            P(),
        ),
        out_specs=P("section", None, None, None),
        check_vma=False,
    )
```

time: 656 us -> 283 us (0.43)
  waiting for transfers between devices: 525 us -> 78.5 us
  Pallas kernels: 0 us -> 128 us
  matrix products: 56.7 us -> 0 us
  starting transfers between devices: 13.1 us -> 62.8 us
  other arithmetic: 41.5 us -> 6.83 us
  between operations: 13.4 us -> 0.61 us
    reduce_scatter x5 -> x0, waiting for transfers between devices: 183 us -> none  [layer(): lax.psum_scatter(jnp.dot(blended_payloads, w_output, preferred_element_ty...]
    ppermute x10 -> x39, waiting for transfers between devices: 221 us -> 78.5 us  [the longest x31 57.2 us: flip(): return lambda x: lax.ppermute(x, 'seq', pairs)]
    pallas_call x0 -> x8, Pallas kernels: none -> 128 us  [the longest x1 65.4 us: shards(): pl.pallas_call(functools.partial(place_kernel, blocks), out_shape=sds((ba...]
    all_gather x5 -> x0, waiting for transfers between devices: 121 us -> none  [advance(): outgoing = lax.all_gather(share, 'seq', axis=0, tiled=True)]
    dot_general x30 -> x0, matrix products: 56.7 us -> none  [the longest x5 21.2 us: layer(): keys_proj = jnp.dot(source_kv, w_key, preferred_element_type=jnp.float32)]
    ppermute x10 -> x39, starting transfers between devices: 12.9 us -> 62.8 us  [the longest x31 51.5 us: flip(): return lambda x: lax.ppermute(x, 'seq', pairs)]
    select_n x10 -> x2, other arithmetic: 17.7 us -> 1.34 us  [the longest x1 1.3 us: shards(): kept = jnp.where(section == step, share, kept)]
    reduce_sum x5 -> x0, other arithmetic: 15.8 us -> none  [normalize(): jnp.mean(values * values, axis=-1, keepdims=True) + epsilon]
  transfers between devices with their start and end apart: 20 -> 39, of which waited for: 20 -> 19; matrix products, arithmetic and copies ran while one was open for 2% -> 1% of each run, Pallas kernels for 0% -> 13%
where the time goes in v1:
time: 283 us; the launch traced here: 282 us
  Pallas kernels  128 us (45%)
  waiting for transfers between devices  78.5 us (28%)
  starting transfers between devices  62.8 us (22%)
  other arithmetic  6.83 us (2%)
  local copies, waits for them, and re-layouts  4.93 us (2%)
    pallas_call x1, Pallas kernels, shards(): pl.pallas_call(functools.partial(place_kernel, blocks), out_shape=sds((ba...  65.4 us
    ppermute x31, waiting for transfers between devices, flip(): return lambda x: lax.ppermute(x, 'seq', pairs)  57.2 us
    ppermute x31, starting transfers between devices, flip(): return lambda x: lax.ppermute(x, 'seq', pairs)  51.5 us
    ppermute x5, waiting for transfers between devices, up(): return lax.ppermute(x, 'section', [(source, target)])  21.3 us
    pallas_call x2, Pallas kernels, shards(): pl.pallas_call(functools.partial(section_kernel, config, blocks), out_sha...  20.1 us
    pallas_call x1, Pallas kernels, shards(): pl.pallas_call(functools.partial(first_kernel, config), out_shape=[sds((l...  14.6 us
    pallas_call x1, Pallas kernels, project_memory(): pl.pallas_call(functools.partial(memory_kernel, config, blocks), out_shap...  9.98 us
    pallas_call x1, Pallas kernels, shards(): pl.pallas_call(functools.partial(query_kernel, config), out_shape=sds((le...  7.18 us
  transfers between devices with their start and end apart: 39, of which 19 were waited for; matrix products, arithmetic and copies ran while one was open for 1% of the time, Pallas kernels for 13%

profile of v1, /device:TPU:25, one launch (start us, length us, event | category | flops | bytes accessed | tf_op | source)
XLA Modules:
  0.0 282.1 jit_solution(15931658322785457939)
XLA Ops:
  8.9 14.6 %shard_map.92 = (bf16[128,512]{1,0:T(8,128)(2,1)}, bf16[128,512]{1,0:T(8,128)(2,1)}) custom-call(s32[2]{0:T(128)} %pad_add_fusion.place, f32[8]{0:T(128)} %multiply_bitcast_fusion.sharp.sharp_own, f32[1,4096]{1,0:T(1,128)} %gain.7, bf16[2,128,4096]{2,1,0:T(8,128)(2,1)} %source.3, bf16[4096,512]{1,0:T(8,128)(2,1)} %bitcast.17, bf16[4096,512]{1,0:T(8,128)(2,1)} %bitcast.27, ...), custom_call_target="tpu_custom_call" | custom-call | tf_op jit(solution)/shard_map/pallas_call | solution.py:359
  26.5 5.1 %shard_map.93 = (bf16[32,4096]{1,0:T(8,128)(2,1)}, bf16[32,4096]{1,0:T(8,128)(2,1)}, bf16[32,4096]{1,0:T(8,128)(2,1)}, bf16[32,4096]{1,0:T(8,128)(2,1)}) custom-call(bf16[128,512]{1,0:T(8,128)(2,1)} %get-tuple-element.25.own, bf16[128,512]{1,0:T(8,128)(2,1)} %copy-done.20, bf16[512,4096]{1,0:T(8,128)(2,1)} %bitcast.22, ...), custom_call_target="tpu_custom_call" | custom-call | tf_op jit(solution)/shard_map/pallas_call | solution.py:373
  34.1 5.3 %collective-permute-done.4 = bf16[32,4096]{1,0:T(8,128)(2,1)S(1)} collective-permute-done((bf16[32,4096]{1,0:T(8,128)(2,1)}, bf16[32,4096]{1,0:T(8,128)(2,1)S(1)}, u32[]{:S(2)}, u32[]{:S(2)}) %collective-permute-start.4) | collective-permute-done | bytes 262176 | tf_op jit(solution)/shard_map/ppermute | solution.py:310
  41.5 5.5 %collective-permute-done.6 = bf16[32,4096]{1,0:T(8,128)(2,1)S(1)} collective-permute-done((bf16[32,4096]{1,0:T(8,128)(2,1)}, bf16[32,4096]{1,0:T(8,128)(2,1)S(1)}, u32[]{:S(2)}, u32[]{:S(2)}) %collective-permute-start.6) | collective-permute-done | bytes 262176 | tf_op jit(solution)/shard_map/ppermute | solution.py:310
  50.3 7.4 %collective-permute-done.7 = bf16[32,4096]{1,0:T(8,128)(2,1)S(1)} collective-permute-done((bf16[32,4096]{1,0:T(8,128)(2,1)S(1)}, bf16[32,4096]{1,0:T(8,128)(2,1)S(1)}, u32[]{:S(2)}, u32[]{:S(2)}) %collective-permute-start.7) | collective-permute-done | bytes 262176 | tf_op jit(solution)/shard_map/ppermute | solution.py:315
  61.3 7.2 %shard_map.91.uq = bf16[128,1024]{1,0:T(8,128)(2,1)} custom-call(s32[2]{0:T(128)} %pad_add_fusion.place, f32[1,4096]{1,0:T(1,128)} %gain.7, bf16[2,128,4096]{2,1,0:T(8,128)(2,1)} %source.2, bf16[4096,512]{1,0:T(8,128)(2,1)} %bitcast.18, bf16[4096,512]{1,0:T(8,128)(2,1)} %collective-permute-done.1.wq_other.refs_7_), custom_call_target="tpu_custom_call" | custom-call | tf_op jit(solution)/shard_map/pallas_call | solution.py:384
  68.5 6.6 %collective-permute-start = (f32[8]{0:T(128)S(1)}, f32[8]{0:T(128)S(1)}, u32[]{:S(2)}, u32[]{:S(2)}) collective-permute-start(f32[8]{0:T(128)S(1)} %copy-done.21), channel_id=1, source_target_pairs={{0,1},{1,0},{2,3},{3,2},{4,5},{5,4},{6,7},{7,6},{8,9},{9,8},{10,11... | collective-permute-start | bytes 104 | tf_op jit(solution)/shard_map/ppermute | solution.py:310
  76.0 10.0 %shard_map.94 = (bf16[128,1024]{1,0:T(8,128)(2,1)}, bf16[128,1024]{1,0:T(8,128)(2,1)}) custom-call(f32[1,4096]{1,0:T(1,128)} %bitcast.32, bf16[32,4096]{1,0:T(8,128)(2,1)} %copy-done.1, bf16[32,4096]{1,0:T(8,128)(2,1)} %copy-done.4, bf16[32,4096]{1,0:T(8,128)(2,1)} %copy-done.5, bf16[32,4096]{1,0:T(8,128)(2,1)} %copy-done.6, bf16[4096,512]{1,0:T(8,128)(2,1)} %bitcast.28, ...), custom_call_target="tpu_custom_call" | custom-call | tf_op jit(solution)/shard_map/pallas_call | solution.py:394
  86.6 6.1 %shard_map.95 = (bf16[32,4096]{1,0:T(8,128)(2,1)}, bf16[32,4096]{1,0:T(8,128)(2,1)}, bf16[32,4096]{1,0:T(8,128)(2,1)}, bf16[32,4096]{1,0:T(8,128)(2,1)}) custom-call(f32[8]{0:T(128)} %multiply_bitcast_fusion.sharp.sharp_own, f32[8]{0:T(128)} %copy-done.22, bf16[128,1024]{1,0:T(8,128)(2,1)} %shard_map.91.uq, bf16[128,1024]{1,0:T(8,128)(2,1)} %get-tuple-element.31.uk.refs_4_, ...), custom_call_target="tpu_custom_call" | custom-call | tf_op jit(solution)/shard_map/pallas_call | solution.py:412
  95.5 5.5 %collective-permute-done.15 = bf16[32,4096]{1,0:T(8,128)(2,1)S(1)} collective-permute-done((bf16[32,4096]{1,0:T(8,128)(2,1)}, bf16[32,4096]{1,0:T(8,128)(2,1)S(1)}, u32[]{:S(2)}, u32[]{:S(2)}) %collective-permute-start.15) | collective-permute-done | bytes 262176 | tf_op jit(solution)/shard_map/ppermute | solution.py:310
  100.9 5.5 %collective-permute-done.16 = bf16[32,4096]{1,0:T(8,128)(2,1)S(1)} collective-permute-done((bf16[32,4096]{1,0:T(8,128)(2,1)}, bf16[32,4096]{1,0:T(8,128)(2,1)S(1)}, u32[]{:S(2)}, u32[]{:S(2)}) %collective-permute-start.16) | collective-permute-done | bytes 262176 | tf_op jit(solution)/shard_map/ppermute | solution.py:310
  112.4 4.1 %collective-permute-done.19.refs_1_ = bf16[32,4096]{1,0:T(8,128)(2,1)S(1)} collective-permute-done((bf16[32,4096]{1,0:T(8,128)(2,1)S(1)}, bf16[32,4096]{1,0:T(8,128)(2,1)S(1)}, u32[]{:S(2)}, u32[]{:S(2)}) %collective-permute-start.19) | collective-permute-done | bytes 262176 | tf_op jit(solution)/shard_map/ppermute | solution.py:310
  118.0 4.9 %collective-permute-done.21.refs_3_ = bf16[32,4096]{1,0:T(8,128)(2,1)S(1)} collective-permute-done((bf16[32,4096]{1,0:T(8,128)(2,1)S(1)}, bf16[32,4096]{1,0:T(8,128)(2,1)S(1)}, u32[]{:S(2)}, u32[]{:S(2)}) %collective-permute-start.21) | collective-permute-done | bytes 262176 | tf_op jit(solution)/shard_map/ppermute | solution.py:310
  123.6 10.0 %shard_map.96 = (bf16[32,4096]{1,0:T(8,128)(2,1)}, bf16[32,4096]{1,0:T(8,128)(2,1)}, bf16[32,4096]{1,0:T(8,128)(2,1)}, bf16[32,4096]{1,0:T(8,128)(2,1)}) custom-call(f32[8]{0:T(128)} %multiply_bitcast_fusion.sharp.sharp_own, f32[8]{0:T(128)} %copy-done.22, f32[1,4096]{1,0:T(1,128)} %gain.7, bf16[32,4096]{1,0:T(8,128)(2,1)} %copy-done.2, ...), custom_call_target="tpu_custom_call" | custom-call | tf_op jit(solution)/shard_map/pallas_call | solution.py:425
  136.4 2.8 collective-permute-done.22
  140.9 3.5 %collective-permute-done.24 = bf16[32,4096]{1,0:T(8,128)(2,1)S(1)} collective-permute-done((bf16[32,4096]{1,0:T(8,128)(2,1)}, bf16[32,4096]{1,0:T(8,128)(2,1)S(1)}, u32[]{:S(2)}, u32[]{:S(2)}) %collective-permute-start.24) | collective-permute-done | bytes 262176 | tf_op jit(solution)/shard_map/ppermute | solution.py:310
  146.9 13.9 %collective-permute-done.25.refs_0_ = bf16[32,4096]{1,0:T(8,128)(2,1)S(1)} collective-permute-done((bf16[32,4096]{1,0:T(8,128)(2,1)S(1)}, bf16[32,4096]{1,0:T(8,128)(2,1)S(1)}, u32[]{:S(2)}, u32[]{:S(2)}) %collective-permute-start.25) | collective-permute-done | bytes 262176 | tf_op jit(solution)/shard_map/ppermute | solution.py:315
  166.8 4.5 %collective-permute-done.27.refs_2_ = bf16[32,4096]{1,0:T(8,128)(2,1)S(1)} collective-permute-done((bf16[32,4096]{1,0:T(8,128)(2,1)S(1)}, bf16[32,4096]{1,0:T(8,128)(2,1)S(1)}, u32[]{:S(2)}, u32[]{:S(2)}) %collective-permute-start.27) | collective-permute-done | bytes 262176 | tf_op jit(solution)/shard_map/ppermute | solution.py:310
  172.7 10.0 %shard_map.97 = (bf16[32,4096]{1,0:T(8,128)(2,1)}, bf16[32,4096]{1,0:T(8,128)(2,1)}, bf16[32,4096]{1,0:T(8,128)(2,1)}, bf16[32,4096]{1,0:T(8,128)(2,1)}) custom-call(f32[8]{0:T(128)} %multiply_bitcast_fusion.sharp.sharp_own, f32[8]{0:T(128)} %copy-done.22, f32[1,4096]{1,0:T(1,128)} %gain.7, bf16[32,4096]{1,0:T(8,128)(2,1)} %copy-done, ...), custom_call_target="tpu_custom_call" | custom-call | tf_op jit(solution)/shard_map/pallas_call | solution.py:425
  185.5 2.8 collective-permute-done.29
  188.3 2.9 %collective-permute-done.30 = bf16[32,4096]{1,0:T(8,128)(2,1)S(1)} collective-permute-done((bf16[32,4096]{1,0:T(8,128)(2,1)}, bf16[32,4096]{1,0:T(8,128)(2,1)S(1)}, u32[]{:S(2)}, u32[]{:S(2)}) %collective-permute-start.30) | collective-permute-done | bytes 262176 | tf_op jit(solution)/shard_map/ppermute | solution.py:310
  195.2 12.2 %collective-permute-start.35 = (bf16[32,4096]{1,0:T(8,128)(2,1)S(1)}, bf16[32,4096]{1,0:T(8,128)(2,1)S(1)}, u32[]{:S(2)}, u32[]{:S(2)}) collective-permute-start(bf16[32,4096]{1,0:T(8,128)(2,1)S(1)} %fusion.8.refs_0_), channel_id=1, source_target_pairs={{0,1},{1,0},{2,3},{3,2},{4,5},{5,4},{6,7},{7,6},{8,9},{9,8},{10,11... | collective-permute-start | bytes 786440 | tf_op jit(solution)/shard_map/ppermute | solution.py:310
  209.5 3.2 %collective-permute-start.37 = (bf16[32,4096]{1,0:T(8,128)(2,1)S(1)}, bf16[32,4096]{1,0:T(8,128)(2,1)S(1)}, u32[]{:S(2)}, u32[]{:S(2)}) collective-permute-start(bf16[32,4096]{1,0:T(8,128)(2,1)S(1)} %collective-permute-done.33.refs_2_), channel_id=1, source_target_pairs={{0,1},{1,0},{2,3},{3,2},{4,5},{5,4},{6,7},{7,6},{8,9},{9,8},{10,11... | collective-permute-start | bytes 786440 | tf_op jit(solution)/shard_map/ppermute | solution.py:310
  216.5 65.4 %shard_map.98 = bf16[2,128,4096]{2,1,0:T(8,128)(2,1)} custom-call(s32[2]{0:T(128)} %pad_add_fusion.place, bf16[32,4096]{1,0:T(8,128)(2,1)} %copy-done.3, bf16[32,4096]{1,0:T(8,128)(2,1)} %copy-done.13, bf16[32,4096]{1,0:T(8,128)(2,1)} %copy-done.14, bf16[32,4096]{1,0:T(8,128)(2,1)} %copy-done.15, bf16[32,4096]{1,0:T(8,128)(2,1)} %copy-done.16, ...), custom_call_target="tpu_custom_call" | custom-call | tf_op jit(solution)/shard_map/pallas_call | solution.py:441
  (115 shorter events, 62.4 us)
Async XLA Ops:
  0.0 25.9 %collective-permute-start.3 = (bf16[512,4096]{1,0:T(8,128)(2,1)}, bf16[512,4096]{1,0:T(8,128)(2,1)}, u32[]{:S(2)}, u32[]{:S(2)}) collective-permute-start(bf16[512,4096]{1,0:T(8,128)(2,1)} %bitcast.21), channel_id=1, source_target_pairs={{0,1},{1,0},{2,3},{3,2},{4,5},{5,4},{6,7},{7,6},{8,9},{9,8},{10,11... | collective-permute-start | bytes 12582920 | tf_op jit(solution)/shard_map/ppermute | solution.py:310
  0.7 60.4 %collective-permute-start.1 = (bf16[4096,512]{1,0:T(8,128)(2,1)}, bf16[4096,512]{1,0:T(8,128)(2,1)}, u32[]{:S(2)}, u32[]{:S(2)}) collective-permute-start(bf16[4096,512]{1,0:T(8,128)(2,1)} %bitcast.16), channel_id=1, source_target_pairs={{8,9},{9,8},{10,11},{11,10},{12,13},{13,12},{14,15},{15,14},{16,17... | collective-permute-start | bytes 12582920 | tf_op jit(solution)/shard_map/ppermute | solution.py:312
  2.6 65.9 %collective-permute-start.13 = (bf16[4096,512]{1,0:T(8,128)(2,1)}, bf16[4096,512]{1,0:T(8,128)(2,1)}, u32[]{:S(2)}, u32[]{:S(2)}) collective-permute-start(bf16[4096,512]{1,0:T(8,128)(2,1)} %bitcast.26), channel_id=1, source_target_pairs={{8,9},{9,8},{10,11},{11,10},{12,13},{13,12},{14,15},{15,14},{16,17... | collective-permute-start | bytes 12582920 | tf_op jit(solution)/shard_map/ppermute | solution.py:312
  5.0 70.1 %collective-permute-start.14 = (bf16[4096,512]{1,0:T(8,128)(2,1)}, bf16[4096,512]{1,0:T(8,128)(2,1)}, u32[]{:S(2)}, u32[]{:S(2)}) collective-permute-start(bf16[4096,512]{1,0:T(8,128)(2,1)} %bitcast.29), channel_id=1, source_target_pairs={{8,9},{9,8},{10,11},{11,10},{12,13},{13,12},{14,15},{15,14},{16,17... | collective-permute-start | bytes 12582920 | tf_op jit(solution)/shard_map/ppermute | solution.py:312
  32.9 8.7 %collective-permute-start.5 = (bf16[32,4096]{1,0:T(8,128)(2,1)}, bf16[32,4096]{1,0:T(8,128)(2,1)S(1)}, u32[]{:S(2)}, u32[]{:S(2)}) collective-permute-start(bf16[32,4096]{1,0:T(8,128)(2,1)} %get-tuple-element.29), channel_id=1, source_target_pairs={{0,4},{1,5},{2,6},{3,7},{4,0},{5,1},{6,2},{7,3},{8,12},{9,13},{10,... | collective-permute-start | bytes 786440 | tf_op jit(solution)/shard_map/ppermute | solution.py:310
  48.3 9.4 %collective-permute-start.7 = (bf16[32,4096]{1,0:T(8,128)(2,1)S(1)}, bf16[32,4096]{1,0:T(8,128)(2,1)S(1)}, u32[]{:S(2)}, u32[]{:S(2)}) collective-permute-start(bf16[32,4096]{1,0:T(8,128)(2,1)S(1)} %fusion.3), channel_id=1, source_target_pairs={{0,24},{1,25},{2,26},{3,27},{4,28},{5,29},{6,30},{7,31}} | collective-permute-start | bytes 786440 | tf_op jit(solution)/shard_map/ppermute | solution.py:315
  49.6 8.9 %collective-permute-start.8 = (bf16[32,4096]{1,0:T(8,128)(2,1)S(1)}, bf16[32,4096]{1,0:T(8,128)(2,1)S(1)}, u32[]{:S(2)}, u32[]{:S(2)}) collective-permute-start(bf16[32,4096]{1,0:T(8,128)(2,1)S(1)} %fusion.3), channel_id=1, source_target_pairs={{0,16},{1,17},{2,18},{3,19},{4,20},{5,21},{6,22},{7,23}} | collective-permute-start | bytes 786440 | tf_op jit(solution)/shard_map/ppermute | solution.py:315
  58.6 16.5 %collective-permute-start.10 = (bf16[32,4096]{1,0:T(8,128)(2,1)S(1)}, bf16[32,4096]{1,0:T(8,128)(2,1)S(1)}, u32[]{:S(2)}, u32[]{:S(2)}) collective-permute-start(bf16[32,4096]{1,0:T(8,128)(2,1)S(1)} %select_select_fusion.refs_0_), channel_id=1, source_target_pairs={{0,2},{1,3},{2,0},{3,1},{4,6},{5,7},{6,4},{7,5},{8,10},{9,11},{10,... | collective-permute-start | bytes 786440 | tf_op jit(solution)/shard_map/ppermute | solution.py:310
  59.9 15.3 %collective-permute-start.11 = (bf16[32,4096]{1,0:T(8,128)(2,1)S(1)}, bf16[32,4096]{1,0:T(8,128)(2,1)S(1)}, u32[]{:S(2)}, u32[]{:S(2)}) collective-permute-start(bf16[32,4096]{1,0:T(8,128)(2,1)S(1)} %select_select_fusion.refs_0_), channel_id=1, source_target_pairs={{0,4},{1,5},{2,6},{3,7},{4,0},{5,1},{6,2},{7,3},{8,12},{9,13},{10,... | collective-permute-start | bytes 786440 | tf_op jit(solution)/shard_map/ppermute | solution.py:310
  61.1 14.1 %collective-permute-start.12 = (bf16[32,4096]{1,0:T(8,128)(2,1)S(1)}, bf16[32,4096]{1,0:T(8,128)(2,1)S(1)}, u32[]{:S(2)}, u32[]{:S(2)}) collective-permute-start(bf16[32,4096]{1,0:T(8,128)(2,1)S(1)} %select_select_fusion.refs_0_), channel_id=1, source_target_pairs={{0,6},{1,7},{2,4},{3,5},{4,2},{5,3},{6,0},{7,1},{8,14},{9,15},{10,... | collective-permute-start | bytes 786440 | tf_op jit(solution)/shard_map/ppermute | solution.py:310
  68.5 17.5 %collective-permute-start = (f32[8]{0:T(128)S(1)}, f32[8]{0:T(128)S(1)}, u32[]{:S(2)}, u32[]{:S(2)}) collective-permute-start(f32[8]{0:T(128)S(1)} %copy-done.21), channel_id=1, source_target_pairs={{0,1},{1,0},{2,3},{3,2},{4,5},{5,4},{6,7},{7,6},{8,9},{9,8},{10,11... | collective-permute-start | bytes 104 | tf_op jit(solution)/shard_map/ppermute | solution.py:310
  92.8 8.2 %collective-permute-start.15 = (bf16[32,4096]{1,0:T(8,128)(2,1)}, bf16[32,4096]{1,0:T(8,128)(2,1)S(1)}, u32[]{:S(2)}, u32[]{:S(2)}) collective-permute-start(bf16[32,4096]{1,0:T(8,128)(2,1)} %get-tuple-element.34), channel_id=1, source_target_pairs={{0,2},{1,3},{2,0},{3,1},{4,6},{5,7},{6,4},{7,5},{8,10},{9,11},{10,... | collective-permute-start | bytes 786440 | tf_op jit(solution)/shard_map/ppermute | solution.py:310
  94.0 12.4 %collective-permute-start.16 = (bf16[32,4096]{1,0:T(8,128)(2,1)}, bf16[32,4096]{1,0:T(8,128)(2,1)S(1)}, u32[]{:S(2)}, u32[]{:S(2)}) collective-permute-start(bf16[32,4096]{1,0:T(8,128)(2,1)} %get-tuple-element.35), channel_id=1, source_target_pairs={{0,4},{1,5},{2,6},{3,7},{4,0},{5,1},{6,2},{7,3},{8,12},{9,13},{10,... | collective-permute-start | bytes 786440 | tf_op jit(solution)/shard_map/ppermute | solution.py:310
  95.3 12.3 %collective-permute-start.17 = (bf16[32,4096]{1,0:T(8,128)(2,1)}, bf16[32,4096]{1,0:T(8,128)(2,1)S(1)}, u32[]{:S(2)}, u32[]{:S(2)}) collective-permute-start(bf16[32,4096]{1,0:T(8,128)(2,1)} %get-tuple-element.36), channel_id=1, source_target_pairs={{0,6},{1,7},{2,4},{3,5},{4,2},{5,3},{6,0},{7,1},{8,14},{9,15},{10,... | collective-permute-start | bytes 786440 | tf_op jit(solution)/shard_map/ppermute | solution.py:310
  111.2 11.7 %collective-permute-start.21 = (bf16[32,4096]{1,0:T(8,128)(2,1)S(1)}, bf16[32,4096]{1,0:T(8,128)(2,1)S(1)}, u32[]{:S(2)}, u32[]{:S(2)}) collective-permute-start(bf16[32,4096]{1,0:T(8,128)(2,1)S(1)} %collective-permute-done.18.refs_0_), channel_id=1, source_target_pairs={{0,6},{1,7},{2,4},{3,5},{4,2},{5,3},{6,0},{7,1},{8,14},{9,15},{10,... | collective-permute-start | bytes 786440 | tf_op jit(solution)/shard_map/ppermute | solution.py:310
  135.6 8.8 %collective-permute-start.24 = (bf16[32,4096]{1,0:T(8,128)(2,1)}, bf16[32,4096]{1,0:T(8,128)(2,1)S(1)}, u32[]{:S(2)}, u32[]{:S(2)}) collective-permute-start(bf16[32,4096]{1,0:T(8,128)(2,1)} %get-tuple-element.40), channel_id=1, source_target_pairs={{0,6},{1,7},{2,4},{3,5},{4,2},{5,3},{6,0},{7,1},{8,14},{9,15},{10,... | collective-permute-start | bytes 786440 | tf_op jit(solution)/shard_map/ppermute | solution.py:310
  145.6 15.2 %collective-permute-start.25 = (bf16[32,4096]{1,0:T(8,128)(2,1)S(1)}, bf16[32,4096]{1,0:T(8,128)(2,1)S(1)}, u32[]{:S(2)}, u32[]{:S(2)}) collective-permute-start(bf16[32,4096]{1,0:T(8,128)(2,1)S(1)} %add_convert_fusion.1), channel_id=1, source_target_pairs={{16,24},{17,25},{18,26},{19,27},{20,28},{21,29},{22,30},{23,31}} | collective-permute-start | bytes 786440 | tf_op jit(solution)/shard_map/ppermute | solution.py:315
  163.0 8.3 %collective-permute-start.27 = (bf16[32,4096]{1,0:T(8,128)(2,1)S(1)}, bf16[32,4096]{1,0:T(8,128)(2,1)S(1)}, u32[]{:S(2)}, u32[]{:S(2)}) collective-permute-start(bf16[32,4096]{1,0:T(8,128)(2,1)S(1)} %collective-permute-done.25.refs_0_), channel_id=1, source_target_pairs={{0,4},{1,5},{2,6},{3,7},{4,0},{5,1},{6,2},{7,3},{8,12},{9,13},{10,... | collective-permute-start | bytes 786440 | tf_op jit(solution)/shard_map/ppermute | solution.py:310
  163.0 8.3 %collective-permute-start.28 = (bf16[32,4096]{1,0:T(8,128)(2,1)S(1)}, bf16[32,4096]{1,0:T(8,128)(2,1)S(1)}, u32[]{:S(2)}, u32[]{:S(2)}) collective-permute-start(bf16[32,4096]{1,0:T(8,128)(2,1)S(1)} %collective-permute-done.25.refs_0_), channel_id=1, source_target_pairs={{0,6},{1,7},{2,4},{3,5},{4,2},{5,3},{6,0},{7,1},{8,14},{9,15},{10,... | collective-permute-start | bytes 786440 | tf_op jit(solution)/shard_map/ppermute | solution.py:310
  182.8 8.3 %collective-permute-start.30 = (bf16[32,4096]{1,0:T(8,128)(2,1)}, bf16[32,4096]{1,0:T(8,128)(2,1)S(1)}, u32[]{:S(2)}, u32[]{:S(2)}) collective-permute-start(bf16[32,4096]{1,0:T(8,128)(2,1)} %get-tuple-element.43), channel_id=1, source_target_pairs={{0,4},{1,5},{2,6},{3,7},{4,0},{5,1},{6,2},{7,3},{8,12},{9,13},{10,... | collective-permute-start | bytes 786440 | tf_op jit(solution)/shard_map/ppermute | solution.py:310
  192.5 15.0 %collective-permute-start.32 = (bf16[32,4096]{1,0:T(8,128)(2,1)S(1)}, bf16[32,4096]{1,0:T(8,128)(2,1)S(1)}, u32[]{:S(2)}, u32[]{:S(2)}) collective-permute-start(bf16[32,4096]{1,0:T(8,128)(2,1)S(1)} %fusion.8.refs_0_), channel_id=1, source_target_pairs={{0,2},{1,3},{2,0},{3,1},{4,6},{5,7},{6,4},{7,5},{8,10},{9,11},{10,... | collective-permute-start | bytes 786440 | tf_op jit(solution)/shard_map/ppermute | solution.py:310
  193.9 15.6 %collective-permute-start.33 = (bf16[32,4096]{1,0:T(8,128)(2,1)S(1)}, bf16[32,4096]{1,0:T(8,128)(2,1)S(1)}, u32[]{:S(2)}, u32[]{:S(2)}) collective-permute-start(bf16[32,4096]{1,0:T(8,128)(2,1)S(1)} %fusion.8.refs_0_), channel_id=1, source_target_pairs={{0,4},{1,5},{2,6},{3,7},{4,0},{5,1},{6,2},{7,3},{8,12},{9,13},{10,... | collective-permute-start | bytes 786440 | tf_op jit(solution)/shard_map/ppermute | solution.py:310
  193.9 18.8 %collective-permute-start.34 = (bf16[32,4096]{1,0:T(8,128)(2,1)S(1)}, bf16[32,4096]{1,0:T(8,128)(2,1)S(1)}, u32[]{:S(2)}, u32[]{:S(2)}) collective-permute-start(bf16[32,4096]{1,0:T(8,128)(2,1)S(1)} %fusion.8.refs_0_), channel_id=1, source_target_pairs={{0,6},{1,7},{2,4},{3,5},{4,2},{5,3},{6,0},{7,1},{8,14},{9,15},{10,... | collective-permute-start | bytes 786440 | tf_op jit(solution)/shard_map/ppermute | solution.py:310
  195.2 19.4 %collective-permute-start.35 = (bf16[32,4096]{1,0:T(8,128)(2,1)S(1)}, bf16[32,4096]{1,0:T(8,128)(2,1)S(1)}, u32[]{:S(2)}, u32[]{:S(2)}) collective-permute-start(bf16[32,4096]{1,0:T(8,128)(2,1)S(1)} %fusion.8.refs_0_), channel_id=1, source_target_pairs={{0,1},{1,0},{2,3},{3,2},{4,5},{5,4},{6,7},{7,6},{8,9},{9,8},{10,11... | collective-permute-start | bytes 786440 | tf_op jit(solution)/shard_map/ppermute | solution.py:310
  (38 other events, 190.8 us)

commit v2 on v0

v2 whole, which is shorter than its diff:
```python
import functools

import jax
import jax.numpy as jnp
from jax import lax
from jax.experimental import pallas as pl
from jax.experimental.pallas import tpu as pltpu
from jax.sharding import PartitionSpec as P

EPSILON = 1e-06
LANES = 128
WIDE = 256
OUT_WIDE = 1024
STEP = 16
BF16 = jnp.bfloat16
F32 = jnp.float32
MIB = 1024 * 1024
ANY = pl.BlockSpec(memory_space=pl.ANY)
IN_HBM = pl.BlockSpec(memory_space=pltpu.HBM)
IN_VMEM = pl.BlockSpec(memory_space=pltpu.VMEM)
IN_SMEM = pl.BlockSpec(memory_space=pltpu.SMEM)


def kernel_call(body, outs, ins, scratch, vmem, flops=0, moved=0):
    return pl.pallas_call(
        body,
        out_shape=outs,
        in_specs=ins,
        out_specs=jax.tree.map(lambda _: IN_VMEM, outs),
        scratch_shapes=scratch,
        compiler_params=pltpu.CompilerParams(vmem_limit_bytes=vmem * MIB),
        cost_estimate=pl.CostEstimate(flops=flops, bytes_accessed=moved, transcendentals=0),
    )


class Copies:
    def __init__(self, sems):
        self.sems, self.used = sems, 0

    def start(self, src, dst):
        copy = pltpu.make_async_copy(src, dst, self.sems.at[self.used])
        self.used += 1
        copy.start()
        return copy


def normalize(values, gain):
    values = values.astype(F32)
    factor = lax.rsqrt(jnp.mean(values * values, axis=-1, keepdims=True) + EPSILON)
    return (values * factor * gain).astype(BF16)


def normalize_rows(raw, out, gain):
    def body(i, _):
        at = pl.ds(pl.multiple_of(i * STEP, STEP), STEP)
        out[at, :] = normalize(raw[at, :], gain[...])
        return 0

    lax.fori_loop(0, raw.shape[0] // STEP, body, 0)


def normalize_pieces(pieces, out, gain):
    low = 0
    for piece in pieces:
        height = piece.shape[0]
        out[low : low + height, :] = normalize(piece[...], gain[...])
        low += height


def lane_masks(rows, head):
    lane = lax.broadcasted_iota(jnp.int32, (rows, LANES), 1)
    return [(lane // head) == i for i in range(LANES // head)]


def unit(block, head):
    masks = lane_masks(block.shape[0], head)
    squares = block * block
    factor = None
    for mask in masks:
        total = jnp.sum(jnp.where(mask, squares, 0.0), axis=-1, keepdims=True)
        own = lax.rsqrt(total / head + EPSILON)
        factor = own if factor is None else jnp.where(mask, own, factor)
    return (block * factor).astype(BF16)


def attend(queries, keys, values, scales, head):
    rows = queries.shape[0]
    masks = lane_masks(rows, head)
    stacked = jnp.concatenate(
        [jnp.where(mask, queries, jnp.zeros_like(queries)) for mask in masks], axis=0
    )
    scores = lax.dot_general(
        stacked, keys, (((1,), (1,)), ((), ())), preferred_element_type=F32
    )
    weights = []
    for i, scale in enumerate(scales):
        raised = jnp.exp(scores[i * rows : (i + 1) * rows] * scale)
        weights.append((raised / jnp.sum(raised, axis=-1, keepdims=True)).astype(BF16))
    mixed = jnp.dot(jnp.concatenate(weights, axis=0), values, preferred_element_type=F32)
    out = mixed[:rows]
    for i in range(1, len(scales)):
        out = jnp.where(masks[i], mixed[i * rows : (i + 1) * rows], out)
    return out.astype(BF16)


def attend_all(uq, uk, v, sharps, mixture, head):
    per = LANES // head
    each = sharps[0].shape[0]
    for group in range(uq.shape[1] // LANES):
        lanes = slice(group * LANES, (group + 1) * LANES)
        scales = []
        for i in range(per):
            index = group * per + i
            scales.append(sharps[index // each][index % each])
        mixture[:, lanes] = attend(uq[:, lanes], uk[:, lanes], v[:, lanes], scales, head)


def project(normed, weights, out, finish, wide=WIDE):
    low = 0
    for weight in weights:
        for at in range(0, weight.shape[1], wide):
            product = jnp.dot(normed, weight[:, at : at + wide], preferred_element_type=F32)
            for g in range(0, wide, LANES):
                out[:, low + g : low + g + LANES] = finish(product[:, g : g + LANES])
            low += wide


def project_out(mixture, weights, outs, arrivals=None):
    for at in range(0, weights[0].shape[1], OUT_WIDE):
        for arrival in arrivals[at // OUT_WIDE] if arrivals else ():
            arrival.wait()
        total, low = None, 0
        for weight in weights:
            high = low + weight.shape[0]
            term = jnp.dot(
                mixture[:, low:high], weight[:, at : at + OUT_WIDE], preferred_element_type=F32
            )
            total, low = term if total is None else total + term, high
        total = total.astype(BF16)
        low = 0
        for out in outs:
            out[:, at : at + OUT_WIDE] = total[low : low + out.shape[0]]
            low += out.shape[0]


def load_rows(copies, source, batch, scratch, low, chip, blocks):
    height = source.shape[1] // blocks
    waits = []
    for j in range(blocks):
        at = pl.multiple_of((chip ^ j) * height, height)
        waits.append(
            copies.start(
                source.at[batch, pl.ds(at, height), :],
                scratch.at[pl.ds(low + j * height, height), :],
            )
        )
    return waits


def only_in(sections):
    def wrap(body):
        def wrapped(config, place, *refs):
            here = place[2]
            active = here == sections[0]
            for other in sections[1:]:
                active = active | (here == other)
            pl.when(active)(lambda: body(config, place, *refs))

        return wrapped

    return wrap


def first_kernel(config, place, sharp, gain, source, wq, wk, wv, wo, own_ref, other_ref,
                 raw, rows, wq_s, wk_s, wv_s, wo_s, uq, uk, v, mixture, sems):
    head, blocks, length, _ = config
    copies = Copies(sems)
    chip, core = place[0], place[1]
    waits = load_rows(copies, source, core, raw, 0, chip, blocks)
    waits += load_rows(copies, source, 1 - core, raw, length, chip, blocks)
    weights = [copies.start(w, s) for w, s in ((wq, wq_s), (wk, wk_s), (wv, wv_s))]
    arrivals = stream_out(copies, ((wo, wo_s),))
    for wait in waits:
        wait.wait()
    normalize_rows(raw, rows, gain)
    normed = rows[...]
    wide = wq.shape[1]
    weights[0].wait()
    project(normed, (wq_s,), uq, lambda x: unit(x, head), wide)
    weights[1].wait()
    project(normed, (wk_s,), uk, lambda x: unit(x, head), wide)
    weights[2].wait()
    project(normed, (wv_s,), v, lambda x: x.astype(BF16), wide)
    for low in (0, length):
        at = pl.ds(low, length)
        attend_all(uq[at, :], uk[at, :], v[at, :], (sharp,), mixture.at[at], head)
    project_out(mixture[...], (wo_s,), (own_ref, other_ref), arrivals)


def join_kernel(config, place, own, other, *outs):
    low = 0
    for out in outs:
        at = pl.ds(low, out.shape[0])
        out[...] = (own[at, :].astype(F32) + other[at, :].astype(F32)).astype(BF16)
        low += out.shape[0]


def finish_kernel(config, place, *refs):
    terms, out = refs[:-1], refs[-1]
    total = terms[0][...].astype(F32)
    for term in terms[1:]:
        total = total + term[...].astype(F32)
    out[...] = total.astype(BF16)


def stream_out(copies, pairs):
    arrivals = []
    for at in range(0, pairs[0][0].shape[1], OUT_WIDE):
        columns = pl.ds(at, OUT_WIDE)
        arrivals.append(
            [copies.start(source.at[:, columns], scratch.at[:, columns]) for source, scratch in pairs]
        )
    return arrivals


def query_kernel(config, place, gain, source, wq_own, wq_other, uq_ref, raw, rows, wq_s, sems):
    head, blocks, _, _ = config
    copies = Copies(sems)
    waits = load_rows(copies, source, place[1], raw, 0, place[0], blocks)
    arrivals = [
        copies.start(weight, wq_s.at[i]) for i, weight in enumerate((wq_own, wq_other))
    ]
    for wait in waits:
        wait.wait()
    normalize_rows(raw, rows, gain)
    for wait in arrivals:
        wait.wait()
    project(rows[...], (wq_s.at[0], wq_s.at[1]), uq_ref, lambda x: unit(x, head))


def memory_kernel(config, place, gain, *refs):
    head, _, _, count = config
    pieces, refs = refs[:count], refs[count:]
    wk_own, wk_other, wv_own, wv_other, uk_ref, v_ref, rows = refs
    normalize_pieces(pieces, rows, gain)
    normed = rows[...]
    project(normed, (wk_own, wk_other), uk_ref, lambda x: unit(x, head))
    project(normed, (wv_own, wv_other), v_ref, lambda x: x.astype(BF16))


def keep_kernel(config, place, *refs):
    count = len(refs) // 2 - 1
    copies = Copies(refs[-1])
    for wait in [copies.start(refs[i], refs[count + i]) for i in range(count)]:
        wait.wait()
    refs[2 * count][...] = jnp.zeros_like(refs[2 * count])


def mix_kernel(config, place, sharp_own, sharp_other, uq, uk, v, wo_own, wo_other, *refs):
    outs, (mixture, own_s, other_s, sems) = refs[:-4], refs[-4:]
    arrivals = stream_out(Copies(sems), ((wo_own, own_s), (wo_other, other_s)))
    attend_all(uq, uk, v, (sharp_own, sharp_other), mixture, config[0])
    project_out(mixture[...], (own_s, other_s), outs, arrivals)


def section_kernel(config, place, sharp_own, sharp_other, gain, *refs):
    head, _, _, count = config
    pieces, refs = refs[:count], refs[count:]
    uk, v, wq_own, wq_other, wo_own, wo_other = refs[:6]
    outs, (rows, uq, mixture) = refs[6:-3], refs[-3:]
    normalize_pieces(pieces, rows, gain)
    project(rows[...], (wq_own, wq_other), uq, lambda x: unit(x, head))
    attend_all(uq, uk, v, (sharp_own, sharp_other), mixture, head)
    project_out(mixture[...], (wo_own, wo_other), outs)


def place_kernel(config, place, *refs):
    _, blocks, _, count = config
    pieces, out = refs[:-1], refs[-1]
    chip, core = place[0], place[1]
    groups = count // blocks
    for i, piece in enumerate(pieces):
        height = piece.shape[0]
        batch = core if i < count else 1 - core
        j, g = (i % count) // groups, i % groups
        at = pl.multiple_of(((chip ^ j) * groups + g) * height, height)
        out[batch, pl.ds(at, height), :] = piece[...]


def shards(
    inbound_embedding_batches,
    decoder_embedding_batches,
    asking_projections,
    probe_projections,
    payload_projections,
    exit_projections,
    layer_rescale_weights,
    logit_sharpness,
    last_rescale_weights,
):
    sections = lax.axis_size("section")
    seq = lax.axis_size("seq")
    section = lax.axis_index("section")
    position = lax.axis_index("seq")
    encoders = 3 * sections // 8
    batches, length, width = inbound_embedding_batches.shape
    cores = 2
    blocks = seq // cores
    assert batches == cores and blocks & (blocks - 1) == 0
    core, chip = position % cores, position // cores
    height = length // blocks
    groups = 2 if height % 32 == 0 else 1
    piece = height // groups
    heads = logit_sharpness.shape[1]
    inner = asking_projections.shape[2]
    head = inner // heads
    both = cores * inner
    count = blocks * groups
    config = (head, blocks, length, count)

    def flip(bits):
        pairs = [(i, i ^ bits) for i in range(seq)]
        return lambda x: lax.ppermute(x, "seq", pairs)

    def up(x, source, target):
        return lax.ppermute(x, "section", [(source, target)])

    to_core = flip(1)
    to_chip = [None] + [flip(j * cores) for j in range(1, blocks)]

    wq, wk, wv, wo = (
        w[0] for w in (asking_projections, probe_projections, payload_projections, exit_projections)
    )
    gain = layer_rescale_weights
    last_gain = last_rescale_weights.reshape(1, width)
    sharp = logit_sharpness[0] * (head ** -0.5)
    sharp_other = to_core(sharp)
    wq_other = to_core(wq)
    stay = pltpu.with_memory_space_constraint

    place = jnp.stack([chip, core, section]).astype(jnp.int32)

    def sds(shape, dtype=BF16):
        return jax.ShapeDtypeStruct(shape, dtype)

    row_scratch = pltpu.VMEM((length, width), BF16)
    out_weight = pltpu.VMEM((inner, width), BF16)
    both_scratch = pltpu.VMEM((length, both), BF16)
    chunks = pltpu.VMEM((inner // WIDE, width, WIDE), BF16)
    partials = [sds((piece, width))] * count

    def sems(n):
        return pltpu.SemaphoreType.DMA((n,))

    def gather(shares):
        by_group = [[share] + [to_chip[j](share) for j in range(1, blocks)] for share in shares]
        return [by_group[g][j] for j in range(blocks) for g in range(groups)]

    def finish(parts, residuals, step):
        shares = []
        for g, residual in enumerate(residuals):
            arrived = [to_chip[j](parts[j * groups + g]) for j in range(1, blocks)]
            shares.append(
                kernel_call(
                    functools.partial(only_in([step])(finish_kernel), config),
                    sds((piece, width)),
                    [IN_SMEM] + [IN_VMEM] * (blocks + 1),
                    [],
                    4,
                )(place, residual, parts[g], *arrived)
            )
        return shares

    def own_rows(source):
        rows = lax.dynamic_slice(source, (core, chip * height, 0), (1, height, width))[0]
        return [rows[g * piece : (g + 1) * piece] for g in range(groups)]

    own, other = kernel_call(
        functools.partial(only_in([0])(first_kernel), config),
        [sds((length, width))] * 2,
        [IN_SMEM, IN_SMEM, IN_VMEM] + [IN_HBM] * 5,
        [pltpu.VMEM((batches * length, width), BF16)] * 2
        + [pltpu.VMEM((width, inner), BF16)] * 3
        + [out_weight]
        + [pltpu.VMEM((batches * length, inner), BF16)] * 4
        + [sems(batches * blocks + 3 + width // OUT_WIDE)],
        32,
    )(place, sharp, gain, *(stay(x, pltpu.HBM) for x in (inbound_embedding_batches, wq, wk, wv, wo)))
    parts = kernel_call(
        functools.partial(only_in([0])(join_kernel), config),
        partials,
        [IN_SMEM] + [IN_VMEM] * 2,
        [],
        8,
    )(place, own, to_core(other))

    unit_queries = kernel_call(
        functools.partial(only_in([encoders])(query_kernel), config),
        sds((length, both)),
        [IN_SMEM, IN_VMEM] + [IN_HBM] * 3,
        [row_scratch, row_scratch, pltpu.VMEM((cores, width, inner), BF16), sems(blocks + cores)],
        18,
        flops=2 * length * width * both,
        moved=2 * width * both,
    )(place, gain, *(stay(x, pltpu.HBM) for x in (decoder_embedding_batches, wq, wq_other)))

    parts, unit_queries, wk, wv = lax.optimization_barrier((parts, unit_queries, wk, wv))
    wk_other, wv_other = to_core(wk), to_core(wv)
    shares = finish(parts, own_rows(inbound_embedding_batches), 0)
    kept = shares
    _, late_wo = lax.optimization_barrier((shares[0], wo))
    wo_other = to_core(late_wo)

    def keep(arrays, users, after):
        after, at_place = lax.optimization_barrier((after, place))
        return kernel_call(
            functools.partial(only_in(users)(keep_kernel), config),
            [pltpu.VMEM(x.shape, x.dtype) for x in arrays] + [sds((8, LANES))],
            [IN_SMEM] + [IN_HBM] * len(arrays),
            [sems(len(arrays))],
            2,
            moved=2 * sum(x.size * x.dtype.itemsize for x in arrays),
        )(at_place, *(stay(x, pltpu.HBM) for x in arrays))

    def project_memory(pieces, scale, users, kv):
        return kernel_call(
            functools.partial(only_in(users)(memory_kernel), config),
            [sds((length, both))] * 2,
            [IN_SMEM] + [IN_VMEM] * (1 + count + 4),
            [row_scratch],
            10,
        )(place, scale, *pieces, *kv)

    queries_and_out = (wq, wq_other, wo, wo_other)
    for step in range(1, sections):
        if step == encoders:
            memory = None
            memory = [up(share, step - 1, step) for share in shares]
            whole, _ = lax.optimization_barrier((jnp.concatenate(shares), memory))
            for target in range(step + 1, sections):
                arrived = up(whole, step - 1, target)
                whole, _ = lax.optimization_barrier((whole, arrived))
                memory = [
                    jnp.where(section == target, arrived[g * piece : (g + 1) * piece], m)
                    for g, m in enumerate(memory)
                ]
            memory, unit_queries = lax.optimization_barrier((memory, unit_queries))
            users = range(step, sections)
            *kv, _ = keep((wk, wk_other, wv, wv_other), users, memory)
            unit_keys, values = project_memory(gather(memory), last_gain, users, kv)
            residuals = own_rows(decoder_embedding_batches)
            parts = kernel_call(
                functools.partial(only_in([step])(mix_kernel), config),
                partials,
                [IN_SMEM] * 3 + [IN_VMEM] * 3 + [IN_HBM] * 2,
                [both_scratch, out_weight, out_weight, sems(2 * (width // OUT_WIDE))],
                16,
            )(
                place, sharp, sharp_other, unit_queries, unit_keys, values,
                stay(wo, pltpu.HBM), stay(wo_other, pltpu.HBM),
            )
            *queries_and_out, mark = keep(
                (wq, wq_other, wo, wo_other), range(step + 1, sections), parts
            )
        else:
            residuals = [up(share, step - 1, step) for share in shares]
            pieces = gather(residuals)
            if step < encoders:
                unit_keys, values = project_memory(pieces, gain, [step], (wk, wk_other, wv, wv_other))
            parts = kernel_call(
                functools.partial(only_in([step])(section_kernel), config),
                partials,
                [IN_SMEM] * 3 + [IN_VMEM] * (1 + count + 6),
                [row_scratch, both_scratch, both_scratch],
                10,
            )(
                place, sharp, sharp_other, gain, *pieces, unit_keys, values,
                *queries_and_out,
            )
        shares = finish(parts, residuals, step)
        if step == encoders:
            shares[-1], _ = lax.optimization_barrier((shares[-1], mark))
        kept = [jnp.where(section == step, share, old) for share, old in zip(shares, kept)]

    pieces = gather(kept)
    pieces = pieces + [to_core(x) for x in pieces]
    finished = kernel_call(
        functools.partial(place_kernel, config),
        sds((batches, length, width)),
        [IN_SMEM] + [IN_VMEM] * len(pieces),
        [],
        8,
    )(place, *pieces)
    return finished[None]


def solution(mesh):
    return jax.shard_map(
        shards,
        mesh=mesh,
        in_specs=(
            P(),
            P(),
            P("section", None, "seq"),
            P("section", None, "seq"),
            P("section", None, "seq"),
            P("section", "seq", None),
            P("section", None),
            P("section", "seq"),
            P(),
        ),
        out_specs=P("section", None, None, None),
        check_vma=False,
    )
```

time: 656 us -> 175 us (0.27)
  waiting for transfers between devices: 525 us -> 63.4 us
  starting transfers between devices: 13.1 us -> 75.6 us
  matrix products: 56.7 us -> 0 us
  other arithmetic: 41.5 us -> 0.86 us
  Pallas kernels: 0 us -> 31.3 us
  between operations: 13.4 us -> 0.45 us
    reduce_scatter x5 -> x0, waiting for transfers between devices: 183 us -> none  [layer(): lax.psum_scatter(jnp.dot(blended_payloads, w_output, preferred_element_ty...]
    ppermute x10 -> x70, waiting for transfers between devices: 221 us -> 63.4 us  [the longest x62 41.3 us: flip(): return lambda x: lax.ppermute(x, 'seq', pairs)]
    all_gather x5 -> x0, waiting for transfers between devices: 121 us -> none  [advance(): outgoing = lax.all_gather(share, 'seq', axis=0, tiled=True)]
    ppermute x10 -> x70, starting transfers between devices: 12.9 us -> 75.6 us  [the longest x62 68.4 us: flip(): return lambda x: lax.ppermute(x, 'seq', pairs)]
    dot_general x30 -> x0, matrix products: 56.7 us -> none  [the longest x5 21.2 us: layer(): keys_proj = jnp.dot(source_kv, w_key, preferred_element_type=jnp.float32)]
    pallas_call x0 -> x18, Pallas kernels: none -> 31.3 us  [the longest x2 14 us: keep(): kernel_call(functools.partial(only_in(users)(keep_kernel), config), [pltp...]
    select_n x10 -> x3, other arithmetic: 17.7 us -> 0.11 us  [the longest x2 0.07 us: shards(): jnp.where(section == step, share, old)]
    reduce_sum x5 -> x0, other arithmetic: 15.8 us -> none  [normalize(): jnp.mean(values * values, axis=-1, keepdims=True) + epsilon]
  transfers between devices with their start and end apart: 20 -> 70, of which waited for: 20 -> 28; matrix products, arithmetic and copies ran while one was open for 2% -> 2% of each run, Pallas kernels for 0% -> 13%
where the time goes in v2:
time: 175 us; the launch traced here: 174 us
  starting transfers between devices  75.6 us (43%)
  waiting for transfers between devices  63.4 us (36%)
  Pallas kernels  31.3 us (18%)
  local copies, waits for them, and re-layouts  2.7 us (2%)
    ppermute x62, starting transfers between devices, flip(): return lambda x: lax.ppermute(x, 'seq', pairs)  68.4 us
    ppermute x62, waiting for transfers between devices, flip(): return lambda x: lax.ppermute(x, 'seq', pairs)  41.3 us
    ppermute x8, waiting for transfers between devices, up(): return lax.ppermute(x, 'section', [(source, target)])  22.2 us
    pallas_call x2, Pallas kernels, keep(): kernel_call(functools.partial(only_in(users)(keep_kernel), config), [pltp...  14 us
    ppermute x8, starting transfers between devices, up(): return lax.ppermute(x, 'section', [(source, target)])  7.22 us
    pallas_call x2, Pallas kernels, shards(): kernel_call(functools.partial(only_in([step])(section_kernel), config), p...  4.63 us
    pallas_call x8, Pallas kernels, finish(): kernel_call(functools.partial(only_in([step])(finish_kernel), config), sd...  4.54 us
  transfers between devices with their start and end apart: 70, of which 28 were waited for; matrix products, arithmetic and copies ran while one was open for 2% of the time, Pallas kernels for 13%

profile of v2, /device:TPU:25, one launch (start us, length us, event | category | flops | bytes accessed | tf_op | source)
XLA Modules:
  0.0 174.3 jit_solution(2135934902880483600)
XLA Ops:
  2.9 6.0 %collective-permute-done.1.refs_1_ = bf16[128,4096]{1,0:T(8,128)(2,1)S(1)} collective-permute-done((bf16[128,4096]{1,0:T(8,128)(2,1)S(1)}, bf16[128,4096]{1,0:T(8,128)(2,1)S(1)}, u32[]{:S(2)}, u32[]{:S(2)}) %collective-permute-start.1) | collective-permute-done | bytes 1048608 | tf_op jit(solution)/shard_map/ppermute | solution.py:323
  16.3 2.7 %collective-permute-done.5.refs_4_ = bf16[16,4096]{1,0:T(8,128)(2,1)S(1)} collective-permute-done((bf16[16,4096]{1,0:T(8,128)(2,1)S(1)}, bf16[16,4096]{1,0:T(8,128)(2,1)S(1)}, u32[]{:S(2)}, u32[]{:S(2)}) %collective-permute-start.5) | collective-permute-done | bytes 131104 | tf_op jit(solution)/shard_map/ppermute | solution.py:323
  19.6 1.7 collective-permute-start.21
  22.8 3.6 %collective-permute-done.6.refs_2_ = bf16[16,4096]{1,0:T(8,128)(2,1)S(1)} collective-permute-done((bf16[16,4096]{1,0:T(8,128)(2,1)S(1)}, bf16[16,4096]{1,0:T(8,128)(2,1)S(1)}, u32[]{:S(2)}, u32[]{:S(2)}) %collective-permute-start.6) | collective-permute-done | bytes 131104 | tf_op jit(solution)/shard_map/ppermute | solution.py:323
  28.2 3.2 %collective-permute-done.8.refs_4_ = bf16[16,4096]{1,0:T(8,128)(2,1)S(1)} collective-permute-done((bf16[16,4096]{1,0:T(8,128)(2,1)S(1)}, bf16[16,4096]{1,0:T(8,128)(2,1)S(1)}, u32[]{:S(2)}, u32[]{:S(2)}) %collective-permute-start.8) | collective-permute-done | bytes 131104 | tf_op jit(solution)/shard_map/ppermute | solution.py:323
  34.7 18.8 %collective-permute-done.12 = bf16[32,4096]{1,0:T(8,128)(2,1)S(1)} collective-permute-done((bf16[32,4096]{1,0:T(8,128)(2,1)S(1)}, bf16[32,4096]{1,0:T(8,128)(2,1)S(1)}, u32[]{:S(2)}, u32[]{:S(2)}) %collective-permute-start.12) | collective-permute-done | bytes 262176 | tf_op jit(solution)/shard_map/ppermute | solution.py:326
  55.1 2.4 %collective-permute-done.13.refs_3_ = bf16[16,4096]{1,0:T(8,128)(2,1)S(1)} collective-permute-done((bf16[16,4096]{1,0:T(8,128)(2,1)S(1)}, bf16[16,4096]{1,0:T(8,128)(2,1)S(1)}, u32[]{:S(2)}, u32[]{:S(2)}) %collective-permute-start.13) | collective-permute-done | bytes 131104 | tf_op jit(solution)/shard_map/ppermute | solution.py:323
  62.5 7.0 %shard_map.96 = (bf16[4096,512]{1,0:T(8,128)(2,1)S(1)}, bf16[4096,512]{1,0:T(8,128)(2,1)S(1)}, bf16[4096,512]{1,0:T(8,128)(2,1)S(1)}, bf16[4096,512]{1,0:T(8,128)(2,1)S(1)}, bf16[8,128]{1,0:T(8,128)(2,1)}) custom-call(s32[3]{0:T(128)S(1)} %pad_add_fusion.place, bf16[4096,512]{1,0:T(8,128)(2,1)} %bitcast.7.refs_4_.refs_0_, ...), custom_call_target="tpu_custom_call" | custom-call | bytes 33554432 | tf_op jit(solution)/shard_map/pallas_call | solution.py:416
  69.5 6.3 %collective-permute-start = (f32[8]{0:T(128)S(1)}, f32[8]{0:T(128)S(1)}, u32[]{:S(2)}, u32[]{:S(2)}) collective-permute-start(f32[8]{0:T(128)S(1)} %multiply_bitcast_fusion.refs_0_), channel_id=1, source_target_pairs={{0,1},{1,0},{2,3},{3,2},{4,5},{5,4},{6,7},{7,6},{8,9},{9,8},{10,11... | collective-permute-start | bytes 104 | tf_op jit(solution)/shard_map/ppermute | solution.py:323
  75.8 3.4 %shard_map.97 = (bf16[128,1024]{1,0:T(8,128)(2,1)S(1)}, bf16[128,1024]{1,0:T(8,128)(2,1)S(1)}) custom-call(s32[3]{0:T(128)S(1)} %pad_add_fusion.place, f32[1,4096]{1,0:T(1,128)S(1)} %bitcast.19, bf16[16,4096]{1,0:T(8,128)(2,1)S(1)} %get-tuple-element.90.refs_1_, bf16[16,4096]{1,0:T(8,128)(2,1)S(1)} %get-tuple-element.91.refs_2_, ...), custom_call_target="tpu_custom_call" | custom-call | tf_op jit(solution)/shard_map/pallas_call | solution.py:426
  89.2 1.6 collective-permute-done.22.refs_2_
  90.8 3.3 %collective-permute-done.23.refs_3_ = bf16[16,4096]{1,0:T(8,128)(2,1)S(1)} collective-permute-done((bf16[16,4096]{1,0:T(8,128)(2,1)S(1)}, bf16[16,4096]{1,0:T(8,128)(2,1)S(1)}, u32[]{:S(2)}, u32[]{:S(2)}) %collective-permute-start.23) | collective-permute-done | bytes 131104 | tf_op jit(solution)/shard_map/ppermute | solution.py:323
  100.8 7.0 %shard_map.101 = (bf16[4096,512]{1,0:T(8,128)(2,1)S(1)}, bf16[4096,512]{1,0:T(8,128)(2,1)S(1)}, bf16[512,4096]{1,0:T(8,128)(2,1)S(1)}, bf16[512,4096]{1,0:T(8,128)(2,1)S(1)}, bf16[8,128]{1,0:T(8,128)(2,1)}) custom-call(s32[3]{0:T(128)S(1)} %pad_add_fusion.place, bf16[4096,512]{1,0:T(8,128)(2,1)} %bitcast.23, ...), custom_call_target="tpu_custom_call" | custom-call | bytes 33554432 | tf_op jit(solution)/shard_map/pallas_call | solution.py:416
  114.6 1.8 %collective-permute-done.42.refs_4_ = bf16[16,4096]{1,0:T(8,128)(2,1)S(1)} collective-permute-done((bf16[16,4096]{1,0:T(8,128)(2,1)S(1)}, bf16[16,4096]{1,0:T(8,128)(2,1)S(1)}, u32[]{:S(2)}, u32[]{:S(2)}) %collective-permute-start.42) | collective-permute-done | bytes 131104 | tf_op jit(solution)/shard_map/ppermute | solution.py:323
  119.7 2.4 %collective-permute-done.38.refs_4_ = bf16[16,4096]{1,0:T(8,128)(2,1)S(1)} collective-permute-done((bf16[16,4096]{1,0:T(8,128)(2,1)S(1)}, bf16[16,4096]{1,0:T(8,128)(2,1)S(1)}, u32[]{:S(2)}, u32[]{:S(2)}) %collective-permute-start.38) | collective-permute-done | bytes 131104 | tf_op jit(solution)/shard_map/ppermute | solution.py:323
  126.7 3.3 %collective-permute-done.39.refs_3_.refs_0_ = bf16[16,4096]{1,0:T(8,128)(2,1)S(1)} collective-permute-done((bf16[16,4096]{1,0:T(8,128)(2,1)S(1)}, bf16[16,4096]{1,0:T(8,128)(2,1)S(1)}, u32[]{:S(2)}, u32[]{:S(2)}) %collective-permute-start.39) | collective-permute-done | bytes 131104 | tf_op jit(solution)/shard_map/ppermute | solution.py:326
  132.7 2.0 %collective-permute-done.44.refs_5_ = bf16[16,4096]{1,0:T(8,128)(2,1)S(1)} collective-permute-done((bf16[16,4096]{1,0:T(8,128)(2,1)S(1)}, bf16[16,4096]{1,0:T(8,128)(2,1)S(1)}, u32[]{:S(2)}, u32[]{:S(2)}) %collective-permute-start.44) | collective-permute-done | bytes 131104 | tf_op jit(solution)/shard_map/ppermute | solution.py:323
  134.7 1.9 %collective-permute-done.48.refs_9_ = bf16[16,4096]{1,0:T(8,128)(2,1)S(1)} collective-permute-done((bf16[16,4096]{1,0:T(8,128)(2,1)S(1)}, bf16[16,4096]{1,0:T(8,128)(2,1)S(1)}, u32[]{:S(2)}, u32[]{:S(2)}) %collective-permute-start.48) | collective-permute-done | bytes 131104 | tf_op jit(solution)/shard_map/ppermute | solution.py:323
  136.6 4.1 %shard_map.105 = (bf16[16,4096]{1,0:T(8,128)(2,1)S(1)}, bf16[16,4096]{1,0:T(8,128)(2,1)S(1)}, bf16[16,4096]{1,0:T(8,128)(2,1)S(1)}, bf16[16,4096]{1,0:T(8,128)(2...) custom-call(s32[3]{0:T(128)S(1)} %pad_add_fusion.place, ...), custom_call_target="tpu_custom_call" | custom-call | tf_op jit(solution)/shard_map/pallas_call | solution.py:470
  140.6 1.9 %collective-permute-start.53 = (bf16[16,4096]{1,0:T(8,128)(2,1)S(1)}, bf16[16,4096]{1,0:T(8,128)(2,1)S(1)}, u32[]{:S(2)}, u32[]{:S(2)}) collective-permute-start(bf16[16,4096]{1,0:T(8,128)(2,1)S(1)} %get-tuple-element.128), channel_id=1, source_target_pairs={{0,2},{1,3},{2,0},{3,1},{4,6},{5,7},{6,4},{7,5},{8,10},{9,11},{10,... | collective-permute-start | bytes 393224 | tf_op jit(solution)/shard_map/ppermute | solution.py:323
  151.2 8.9 %collective-permute-start.63 = (bf16[16,4096]{1,0:T(8,128)(2,1)S(1)}, bf16[16,4096]{1,0:T(8,128)(2,1)S(1)}, u32[]{:S(2)}, u32[]{:S(2)}) collective-permute-start(bf16[16,4096]{1,0:T(8,128)(2,1)S(1)} %select_select_fusion.refs_1_), channel_id=1, source_target_pairs={{0,1},{1,0},{2,3},{3,2},{4,5},{5,4},{6,7},{7,6},{8,9},{9,8},{10,11... | collective-permute-start | bytes 393224 | tf_op jit(solution)/shard_map/ppermute | solution.py:323
  163.5 2.6 %collective-permute-start.62 = (bf16[16,4096]{1,0:T(8,128)(2,1)S(1)}, bf16[16,4096]{1,0:T(8,128)(2,1)S(1)}, u32[]{:S(2)}, u32[]{:S(2)}) collective-permute-start(bf16[16,4096]{1,0:T(8,128)(2,1)S(1)} %select_select_fusion.1.refs_0_), channel_id=1, source_target_pairs={{0,1},{1,0},{2,3},{3,2},{4,5},{5,4},{6,7},{7,6},{8,9},{9,8},{10,11... | collective-permute-start | bytes 393224 | tf_op jit(solution)/shard_map/ppermute | solution.py:323
  168.4 1.6 collective-permute-done.60.refs_6_
  172.3 2.0 %shard_map.108 = bf16[2,128,4096]{2,1,0:T(8,128)(2,1)} custom-call(s32[3]{0:T(128)S(1)} %pad_add_fusion.place, bf16[16,4096]{1,0:T(8,128)(2,1)S(1)} %select_select_fusion.1.refs_0_, bf16[16,4096]{1,0:T(8,128)(2,1)S(1)} %select_select_fusion.refs_1_, bf16[16,4096]{1,0:T(8,128)(2,1)S(1)} %collective-permute-done.56.refs_2_, ...), custom_call_target="tpu_custom_call" | custom-call | tf_op jit(solution)/shard_map/pallas_call | solution.py:487
  (148 shorter events, 74.4 us)
Async XLA Ops:
  0.0 9.5 %collective-permute-start.2 = (bf16[4096,512]{1,0:T(8,128)(2,1)}, bf16[4096,512]{1,0:T(8,128)(2,1)}, u32[]{:S(2)}, u32[]{:S(2)}) collective-permute-start(bf16[4096,512]{1,0:T(8,128)(2,1)} %bitcast.20), channel_id=1, source_target_pairs={{0,1},{1,0},{2,3},{3,2},{4,5},{5,4},{6,7},{7,6},{8,9},{9,8},{10,11... | collective-permute-start | bytes 12582920 | tf_op jit(solution)/shard_map/ppermute | solution.py:323
  10.2 49.9 %collective-permute-start.19 = (bf16[4096,512]{1,0:T(8,128)(2,1)}, bf16[4096,512]{1,0:T(8,128)(2,1)}, u32[]{:S(2)}, u32[]{:S(2)}) collective-permute-start(bf16[4096,512]{1,0:T(8,128)(2,1)} %bitcast.7.refs_4_.refs_0_), channel_id=1, source_target_pairs={{0,1},{1,0},{2,3},{3,2},{4,5},{5,4},{6,7},{7,6},{8,9},{9,8},{10,11... | collective-permute-start | bytes 12582920 | tf_op jit(solution)/shard_map/ppermute | solution.py:323
  10.6 50.4 %collective-permute-start.20 = (bf16[4096,512]{1,0:T(8,128)(2,1)}, bf16[4096,512]{1,0:T(8,128)(2,1)}, u32[]{:S(2)}, u32[]{:S(2)}) collective-permute-start(bf16[4096,512]{1,0:T(8,128)(2,1)} %bitcast.8.refs_5_.refs_2_), channel_id=1, source_target_pairs={{0,1},{1,0},{2,3},{3,2},{4,5},{5,4},{6,7},{7,6},{8,9},{9,8},{10,11... | collective-permute-start | bytes 12582920 | tf_op jit(solution)/shard_map/ppermute | solution.py:323
  19.6 59.6 %collective-permute-start.21 = (bf16[512,4096]{1,0:T(8,128)(2,1)}, bf16[512,4096]{1,0:T(8,128)(2,1)}, u32[]{:S(2)}, u32[]{:S(2)}) collective-permute-start(bf16[512,4096]{1,0:T(8,128)(2,1)} %bitcast.9.refs_6_.refs_5_.refs_2_), channel_id=1, source_target_pairs={{0,1},{1,0},{2,3},{3,2},{4,5},{5,4},{6,7},{7,6},{8,9},{9,8},{10,11... | collective-permute-start | bytes 12582920 | tf_op jit(solution)/shard_map/ppermute | solution.py:323
  33.4 20.1 %collective-permute-start.12 = (bf16[32,4096]{1,0:T(8,128)(2,1)S(1)}, bf16[32,4096]{1,0:T(8,128)(2,1)S(1)}, u32[]{:S(2)}, u32[]{:S(2)}) collective-permute-start(bf16[32,4096]{1,0:T(8,128)(2,1)S(1)} %pad_maximum_fusion), channel_id=1, source_target_pairs={{0,24},{1,25},{2,26},{3,27},{4,28},{5,29},{6,30},{7,31}} | collective-permute-start | bytes 786440 | tf_op jit(solution)/shard_map/ppermute | solution.py:326
  57.4 12.0 %collective-permute-start.15 = (bf16[16,4096]{1,0:T(8,128)(2,1)S(1)}, bf16[16,4096]{1,0:T(8,128)(2,1)S(1)}, u32[]{:S(2)}, u32[]{:S(2)}) collective-permute-start(bf16[16,4096]{1,0:T(8,128)(2,1)S(1)} %get-tuple-element.90.refs_1_), channel_id=1, source_target_pairs={{0,4},{1,5},{2,6},{3,7},{4,0},{5,1},{6,2},{7,3},{8,12},{9,13},{10,... | collective-permute-start | bytes 393224 | tf_op jit(solution)/shard_map/ppermute | solution.py:323
  58.8 16.9 %collective-permute-start.16 = (bf16[16,4096]{1,0:T(8,128)(2,1)S(1)}, bf16[16,4096]{1,0:T(8,128)(2,1)S(1)}, u32[]{:S(2)}, u32[]{:S(2)}) collective-permute-start(bf16[16,4096]{1,0:T(8,128)(2,1)S(1)} %get-tuple-element.91.refs_2_), channel_id=1, source_target_pairs={{0,4},{1,5},{2,6},{3,7},{4,0},{5,1},{6,2},{7,3},{8,12},{9,13},{10,... | collective-permute-start | bytes 393224 | tf_op jit(solution)/shard_map/ppermute | solution.py:323
  60.1 15.7 %collective-permute-start.17 = (bf16[16,4096]{1,0:T(8,128)(2,1)S(1)}, bf16[16,4096]{1,0:T(8,128)(2,1)S(1)}, u32[]{:S(2)}, u32[]{:S(2)}) collective-permute-start(bf16[16,4096]{1,0:T(8,128)(2,1)S(1)} %get-tuple-element.90.refs_1_), channel_id=1, source_target_pairs={{0,6},{1,7},{2,4},{3,5},{4,2},{5,3},{6,0},{7,1},{8,14},{9,15},{10,... | collective-permute-start | bytes 393224 | tf_op jit(solution)/shard_map/ppermute | solution.py:323
  61.0 14.8 %collective-permute-start.18 = (bf16[16,4096]{1,0:T(8,128)(2,1)S(1)}, bf16[16,4096]{1,0:T(8,128)(2,1)S(1)}, u32[]{:S(2)}, u32[]{:S(2)}) collective-permute-start(bf16[16,4096]{1,0:T(8,128)(2,1)S(1)} %get-tuple-element.91.refs_2_), channel_id=1, source_target_pairs={{0,6},{1,7},{2,4},{3,5},{4,2},{5,3},{6,0},{7,1},{8,14},{9,15},{10,... | collective-permute-start | bytes 393224 | tf_op jit(solution)/shard_map/ppermute | solution.py:323
  69.5 9.7 %collective-permute-start = (f32[8]{0:T(128)S(1)}, f32[8]{0:T(128)S(1)}, u32[]{:S(2)}, u32[]{:S(2)}) collective-permute-start(f32[8]{0:T(128)S(1)} %multiply_bitcast_fusion.refs_0_), channel_id=1, source_target_pairs={{0,1},{1,0},{2,3},{3,2},{4,5},{5,4},{6,7},{7,6},{8,9},{9,8},{10,11... | collective-permute-start | bytes 104 | tf_op jit(solution)/shard_map/ppermute | solution.py:323
  84.4 9.8 %collective-permute-start.23 = (bf16[16,4096]{1,0:T(8,128)(2,1)S(1)}, bf16[16,4096]{1,0:T(8,128)(2,1)S(1)}, u32[]{:S(2)}, u32[]{:S(2)}) collective-permute-start(bf16[16,4096]{1,0:T(8,128)(2,1)S(1)} %get-tuple-element.104), channel_id=1, source_target_pairs={{0,4},{1,5},{2,6},{3,7},{4,0},{5,1},{6,2},{7,3},{8,12},{9,13},{10,... | collective-permute-start | bytes 393224 | tf_op jit(solution)/shard_map/ppermute | solution.py:323
  85.2 9.0 %collective-permute-start.24 = (bf16[16,4096]{1,0:T(8,128)(2,1)S(1)}, bf16[16,4096]{1,0:T(8,128)(2,1)S(1)}, u32[]{:S(2)}, u32[]{:S(2)}) collective-permute-start(bf16[16,4096]{1,0:T(8,128)(2,1)S(1)} %get-tuple-element.105), channel_id=1, source_target_pairs={{0,6},{1,7},{2,4},{3,5},{4,2},{5,3},{6,0},{7,1},{8,14},{9,15},{10,... | collective-permute-start | bytes 393224 | tf_op jit(solution)/shard_map/ppermute | solution.py:323
  96.4 11.4 %collective-permute-start.33 = (bf16[16,4096]{1,0:T(8,128)(2,1)S(1)}, bf16[16,4096]{1,0:T(8,128)(2,1)S(1)}, u32[]{:S(2)}, u32[]{:S(2)}) collective-permute-start(bf16[16,4096]{1,0:T(8,128)(2,1)S(1)} %collective-permute-done.29.refs_4_.refs_0_), channel_id=1, source_target_pairs={{0,4},{1,5},{2,6},{3,7},{4,0},{5,1},{6,2},{7,3},{8,12},{9,13},{10,... | collective-permute-start | bytes 393224 | tf_op jit(solution)/shard_map/ppermute | solution.py:323
  96.7 11.1 %collective-permute-start.35 = (bf16[16,4096]{1,0:T(8,128)(2,1)S(1)}, bf16[16,4096]{1,0:T(8,128)(2,1)S(1)}, u32[]{:S(2)}, u32[]{:S(2)}) collective-permute-start(bf16[16,4096]{1,0:T(8,128)(2,1)S(1)} %collective-permute-done.29.refs_4_.refs_0_), channel_id=1, source_target_pairs={{0,6},{1,7},{2,4},{3,5},{4,2},{5,3},{6,0},{7,1},{8,14},{9,15},{10,... | collective-permute-start | bytes 393224 | tf_op jit(solution)/shard_map/ppermute | solution.py:323
  98.1 9.7 %collective-permute-start.30 = (bf16[16,4096]{1,0:T(8,128)(2,1)S(1)}, bf16[16,4096]{1,0:T(8,128)(2,1)S(1)}, u32[]{:S(2)}, u32[]{:S(2)}) collective-permute-start(bf16[16,4096]{1,0:T(8,128)(2,1)S(1)} %collective-permute-done.25.refs_3_.refs_0_), channel_id=1, source_target_pairs={{0,2},{1,3},{2,0},{3,1},{4,6},{5,7},{6,4},{7,5},{8,10},{9,11},{10,... | collective-permute-start | bytes 393224 | tf_op jit(solution)/shard_map/ppermute | solution.py:323
  99.1 8.8 %collective-permute-start.32 = (bf16[16,4096]{1,0:T(8,128)(2,1)S(1)}, bf16[16,4096]{1,0:T(8,128)(2,1)S(1)}, u32[]{:S(2)}, u32[]{:S(2)}) collective-permute-start(bf16[16,4096]{1,0:T(8,128)(2,1)S(1)} %collective-permute-done.25.refs_3_.refs_0_), channel_id=1, source_target_pairs={{0,4},{1,5},{2,6},{3,7},{4,0},{5,1},{6,2},{7,3},{8,12},{9,13},{10,... | collective-permute-start | bytes 393224 | tf_op jit(solution)/shard_map/ppermute | solution.py:323
  99.7 9.0 %collective-permute-start.34 = (bf16[16,4096]{1,0:T(8,128)(2,1)S(1)}, bf16[16,4096]{1,0:T(8,128)(2,1)S(1)}, u32[]{:S(2)}, u32[]{:S(2)}) collective-permute-start(bf16[16,4096]{1,0:T(8,128)(2,1)S(1)} %collective-permute-done.25.refs_3_.refs_0_), channel_id=1, source_target_pairs={{0,6},{1,7},{2,4},{3,5},{4,2},{5,3},{6,0},{7,1},{8,14},{9,15},{10,... | collective-permute-start | bytes 393224 | tf_op jit(solution)/shard_map/ppermute | solution.py:323
  113.7 8.3 %collective-permute-start.38 = (bf16[16,4096]{1,0:T(8,128)(2,1)S(1)}, bf16[16,4096]{1,0:T(8,128)(2,1)S(1)}, u32[]{:S(2)}, u32[]{:S(2)}) collective-permute-start(bf16[16,4096]{1,0:T(8,128)(2,1)S(1)} %get-tuple-element.118), channel_id=1, source_target_pairs={{0,6},{1,7},{2,4},{3,5},{4,2},{5,3},{6,0},{7,1},{8,14},{9,15},{10,... | collective-permute-start | bytes 393224 | tf_op jit(solution)/shard_map/ppermute | solution.py:323
  124.3 8.3 %collective-permute-start.47 = (bf16[16,4096]{1,0:T(8,128)(2,1)S(1)}, bf16[16,4096]{1,0:T(8,128)(2,1)S(1)}, u32[]{:S(2)}, u32[]{:S(2)}) collective-permute-start(bf16[16,4096]{1,0:T(8,128)(2,1)S(1)} %collective-permute-done.43.refs_4_.refs_0_), channel_id=1, source_target_pairs={{0,4},{1,5},{2,6},{3,7},{4,0},{5,1},{6,2},{7,3},{8,12},{9,13},{10,... | collective-permute-start | bytes 393224 | tf_op jit(solution)/shard_map/ppermute | solution.py:323
  145.6 14.6 %collective-permute-start.52 = (bf16[16,4096]{1,0:T(8,128)(2,1)S(1)}, bf16[16,4096]{1,0:T(8,128)(2,1)S(1)}, u32[]{:S(2)}, u32[]{:S(2)}) collective-permute-start(bf16[16,4096]{1,0:T(8,128)(2,1)S(1)} %get-tuple-element.126), channel_id=1, source_target_pairs={{0,6},{1,7},{2,4},{3,5},{4,2},{5,3},{6,0},{7,1},{8,14},{9,15},{10,... | collective-permute-start | bytes 393224 | tf_op jit(solution)/shard_map/ppermute | solution.py:323
  148.5 13.6 %collective-permute-start.57 = (bf16[16,4096]{1,0:T(8,128)(2,1)S(1)}, bf16[16,4096]{1,0:T(8,128)(2,1)S(1)}, u32[]{:S(2)}, u32[]{:S(2)}) collective-permute-start(bf16[16,4096]{1,0:T(8,128)(2,1)S(1)} %select_select_fusion.refs_1_), channel_id=1, source_target_pairs={{0,2},{1,3},{2,0},{3,1},{4,6},{5,7},{6,4},{7,5},{8,10},{9,11},{10,... | collective-permute-start | bytes 393224 | tf_op jit(solution)/shard_map/ppermute | solution.py:323
  149.9 12.6 %collective-permute-start.59 = (bf16[16,4096]{1,0:T(8,128)(2,1)S(1)}, bf16[16,4096]{1,0:T(8,128)(2,1)S(1)}, u32[]{:S(2)}, u32[]{:S(2)}) collective-permute-start(bf16[16,4096]{1,0:T(8,128)(2,1)S(1)} %select_select_fusion.refs_1_), channel_id=1, source_target_pairs={{0,4},{1,5},{2,6},{3,7},{4,0},{5,1},{6,2},{7,3},{8,12},{9,13},{10,... | collective-permute-start | bytes 393224 | tf_op jit(solution)/shard_map/ppermute | solution.py:323
  150.3 13.3 %collective-permute-start.61 = (bf16[16,4096]{1,0:T(8,128)(2,1)S(1)}, bf16[16,4096]{1,0:T(8,128)(2,1)S(1)}, u32[]{:S(2)}, u32[]{:S(2)}) collective-permute-start(bf16[16,4096]{1,0:T(8,128)(2,1)S(1)} %select_select_fusion.refs_1_), channel_id=1, source_target_pairs={{0,6},{1,7},{2,4},{3,5},{4,2},{5,3},{6,0},{7,1},{8,14},{9,15},{10,... | collective-permute-start | bytes 393224 | tf_op jit(solution)/shard_map/ppermute | solution.py:323
  151.2 14.9 %collective-permute-start.63 = (bf16[16,4096]{1,0:T(8,128)(2,1)S(1)}, bf16[16,4096]{1,0:T(8,128)(2,1)S(1)}, u32[]{:S(2)}, u32[]{:S(2)}) collective-permute-start(bf16[16,4096]{1,0:T(8,128)(2,1)S(1)} %select_select_fusion.refs_1_), channel_id=1, source_target_pairs={{0,1},{1,0},{2,3},{3,2},{4,5},{5,4},{6,7},{7,6},{8,9},{9,8},{10,11... | collective-permute-start | bytes 393224 | tf_op jit(solution)/shard_map/ppermute | solution.py:323
  (49 other events, 262.8 us)

commit v3 on v2

--- a/solution.py
+++ b/solution.py
@@ -21,12 +21,12 @@
 IN_SMEM = pl.BlockSpec(memory_space=pltpu.SMEM)
 
 
-def kernel_call(body, outs, ins, scratch, vmem, flops=0, moved=0):
+def kernel_call(body, outs, ins, scratch, vmem, flops=0, moved=0, out_spec=IN_VMEM):
     return pl.pallas_call(
         body,
         out_shape=outs,
         in_specs=ins,
-        out_specs=jax.tree.map(lambda _: IN_VMEM, outs),
+        out_specs=jax.tree.map(lambda _: out_spec, outs),
         scratch_shapes=scratch,
         compiler_params=pltpu.CompilerParams(vmem_limit_bytes=vmem * MIB),
         cost_estimate=pl.CostEstimate(flops=flops, bytes_accessed=moved, transcendentals=0),
@@ -171,8 +171,16 @@
     return wrap
 
 
-def first_kernel(config, place, sharp, gain, source, wq, wk, wv, wo, own_ref, other_ref,
-                 raw, rows, wq_s, wk_s, wv_s, wo_s, uq, uk, v, mixture, sems):
+def give_rows(raw, outs):
+    low = 0
+    for out in outs:
+        out[...] = raw[low : low + out.shape[0], :]
+        low += out.shape[0]
+
+
+def first_kernel(config, place, sharp, gain, source, wq, wk, wv, wo, own_ref, other_ref, *refs):
+    residuals, refs = refs[:-11], refs[-11:]
+    raw, rows, wq_s, wk_s, wv_s, wo_s, uq, uk, v, mixture, sems = refs
     head, blocks, length, _ = config
     copies = Copies(sems)
     chip, core = place[0], place[1]
@@ -182,6 +190,7 @@
     arrivals = stream_out(copies, ((wo, wo_s),))
     for wait in waits:
         wait.wait()
+    give_rows(raw, residuals)
     normalize_rows(raw, rows, gain)
     normed = rows[...]
     wide = wq.shape[1]
@@ -213,6 +222,20 @@
     out[...] = total.astype(BF16)
 
 
+def finish_whole_kernel(config, place, *refs):
+    _, blocks, _, count = config
+    groups = count // blocks
+    residuals, terms, outs = refs[:groups], refs[groups:-groups], refs[-groups:]
+    low = 0
+    for residual, out in zip(residuals, outs):
+        at = pl.ds(low, out.shape[0])
+        total = residual[...].astype(F32)
+        for term in terms:
+            total = total + term[at, :].astype(F32)
+        out[...] = total.astype(BF16)
+        low += out.shape[0]
+
+
 def stream_out(copies, pairs):
     arrivals = []
     for at in range(0, pairs[0][0].shape[1], OUT_WIDE):
@@ -223,7 +246,8 @@
     return arrivals
 
 
-def query_kernel(config, place, gain, source, wq_own, wq_other, uq_ref, raw, rows, wq_s, sems):
+def query_kernel(config, place, gain, source, wq_own, wq_other, uq_ref, *refs):
+    residuals, (raw, rows, wq_s, sems) = refs[:-4], refs[-4:]
     head, blocks, _, _ = config
     copies = Copies(sems)
     waits = load_rows(copies, source, place[1], raw, 0, place[0], blocks)
@@ -232,6 +256,7 @@
     ]
     for wait in waits:
         wait.wait()
+    give_rows(raw, residuals)
     normalize_rows(raw, rows, gain)
     for wait in arrivals:
         wait.wait()
@@ -239,9 +264,8 @@
 
 
 def memory_kernel(config, place, gain, *refs):
-    head, _, _, count = config
-    pieces, refs = refs[:count], refs[count:]
-    wk_own, wk_other, wv_own, wv_other, uk_ref, v_ref, rows = refs
+    head = config[0]
+    pieces, (wk_own, wk_other, wv_own, wv_other, uk_ref, v_ref, rows) = refs[:-7], refs[-7:]
     normalize_pieces(pieces, rows, gain)
     normed = rows[...]
     project(normed, (wk_own, wk_other), uk_ref, lambda x: unit(x, head))
@@ -249,11 +273,27 @@
 
 
 def keep_kernel(config, place, *refs):
-    count = len(refs) // 2 - 1
-    copies = Copies(refs[-1])
+    sems, refs = refs[-1], refs[:-1]
+    count = len(refs) // 2
+    copies = Copies(sems)
     for wait in [copies.start(refs[i], refs[count + i]) for i in range(count)]:
         wait.wait()
-    refs[2 * count][...] = jnp.zeros_like(refs[2 * count])
+
+
+def keep_keys_kernel(config, place, wk, wv, stack, *refs):
+    keep_kernel(config, place, wk, stack.at[0], wv, stack.at[1], *refs)
+
+
+def stack_kernel(config, place, *refs):
+    sources, (out, held, sems) = refs[:-3], refs[-3:]
+    copies = Copies(sems)
+    arrivals = [copies.start(source, held.at[i]) for i, source in enumerate(sources)]
+    leaving = []
+    for i, arrival in enumerate(arrivals):
+        arrival.wait()
+        leaving.append(copies.start(held.at[i], out.at[i]))
+    for wait in leaving:
+        wait.wait()
 
 
 def mix_kernel(config, place, sharp_own, sharp_other, uq, uk, v, wo_own, wo_other, *refs):
@@ -354,7 +394,7 @@
 
     def gather(shares):
         by_group = [[share] + [to_chip[j](share) for j in range(1, blocks)] for share in shares]
-        return [by_group[g][j] for j in range(blocks) for g in range(groups)]
+        return [group[j] for j in range(blocks) for group in by_group]
 
     def finish(parts, residuals, step):
         shares = []
@@ -371,13 +411,20 @@
             )
         return shares
 
-    def own_rows(source):
-        rows = lax.dynamic_slice(source, (core, chip * height, 0), (1, height, width))[0]
-        return [rows[g * piece : (g + 1) * piece] for g in range(groups)]
-
-    own, other = kernel_call(
+    def finish_whole(parts, residuals, step):
+        arrived = [to_chip[j](parts[j]) for j in range(1, blocks)]
+        return kernel_call(
+            functools.partial(only_in([step])(finish_whole_kernel), config),
+            [sds((piece, width))] * groups,
+            [IN_SMEM] + [IN_VMEM] * (groups + blocks),
+            [],
+            6,
+        )(place, *residuals, parts[0], *arrived)
+
+    residual_shapes = [sds((piece, width))] * groups
+    own, other, *first_residuals = kernel_call(
         functools.partial(only_in([0])(first_kernel), config),
-        [sds((length, width))] * 2,
+        [sds((length, width))] * 2 + residual_shapes,
         [IN_SMEM, IN_SMEM, IN_VMEM] + [IN_HBM] * 5,
         [pltpu.VMEM((batches * length, width), BF16)] * 2
         + [pltpu.VMEM((width, inner), BF16)] * 3
@@ -386,17 +433,26 @@
         + [sems(batches * blocks + 3 + width // OUT_WIDE)],
         32,
     )(place, sharp, gain, *(stay(x, pltpu.HBM) for x in (inbound_embedding_batches, wq, wk, wv, wo)))
+    stack = kernel_call(
+        functools.partial(only_in(range(1, sections))(stack_kernel), config),
+        pltpu.HBM((2, width, inner), BF16),
+        [IN_SMEM] + [IN_HBM] * 2,
+        [pltpu.VMEM((2, width, inner), BF16), sems(4)],
+        10,
+        out_spec=IN_HBM,
+    )(place, stay(wk, pltpu.HBM), stay(wv, pltpu.HBM))
+    received, stack = lax.optimization_barrier((to_core(other), stack))
     parts = kernel_call(
         functools.partial(only_in([0])(join_kernel), config),
-        partials,
+        [sds((height, width))] * blocks,
         [IN_SMEM] + [IN_VMEM] * 2,
         [],
         8,
-    )(place, own, to_core(other))
-
-    unit_queries = kernel_call(
+    )(place, own, received)
+
+    unit_queries, *target_residuals = kernel_call(
         functools.partial(only_in([encoders])(query_kernel), config),
-        sds((length, both)),
+        [sds((length, both))] + residual_shapes,
         [IN_SMEM, IN_VMEM] + [IN_HBM] * 3,
         [row_scratch, row_scratch, pltpu.VMEM((cores, width, inner), BF16), sems(blocks + cores)],
         18,
@@ -404,51 +460,54 @@
         moved=2 * width * both,
     )(place, gain, *(stay(x, pltpu.HBM) for x in (decoder_embedding_batches, wq, wq_other)))
 
-    parts, unit_queries, wk, wv = lax.optimization_barrier((parts, unit_queries, wk, wv))
-    wk_other, wv_other = to_core(wk), to_core(wv)
-    shares = finish(parts, own_rows(inbound_embedding_batches), 0)
+    parts, unit_queries, stack = lax.optimization_barrier((parts, unit_queries, stack))
+    stack = to_core(stack)
+    shares = finish_whole(parts, first_residuals, 0)
     kept = shares
     _, late_wo = lax.optimization_barrier((shares[0], wo))
     wo_other = to_core(late_wo)
 
-    def keep(arrays, users, after):
-        after, at_place = lax.optimization_barrier((after, place))
+    def keep(body, arrays, shapes, users, after):
+        _, at_place = lax.optimization_barrier((after, place))
         return kernel_call(
-            functools.partial(only_in(users)(keep_kernel), config),
-            [pltpu.VMEM(x.shape, x.dtype) for x in arrays] + [sds((8, LANES))],
+            functools.partial(only_in(users)(body), config),
+            [pltpu.VMEM(shape, BF16) for shape in shapes],
             [IN_SMEM] + [IN_HBM] * len(arrays),
-            [sems(len(arrays))],
+            [sems(4)],
             2,
-            moved=2 * sum(x.size * x.dtype.itemsize for x in arrays),
+            moved=8 * width * both,
         )(at_place, *(stay(x, pltpu.HBM) for x in arrays))
+
+    def keep_keys(users, after):
+        return keep(keep_keys_kernel, (wk, wv, stack), [(width, inner)] * 4, users, after)
+
+    def keep_queries(users, after):
+        arrays = (wq, wq_other, wo, wo_other)
+        return keep(keep_kernel, arrays, [x.shape for x in arrays], users, after)
 
     def project_memory(pieces, scale, users, kv):
         return kernel_call(
             functools.partial(only_in(users)(memory_kernel), config),
             [sds((length, both))] * 2,
-            [IN_SMEM] + [IN_VMEM] * (1 + count + 4),
+            [IN_SMEM] + [IN_VMEM] * (1 + len(pieces) + 4),
             [row_scratch],
             10,
         )(place, scale, *pieces, *kv)
 
-    queries_and_out = (wq, wq_other, wo, wo_other)
     for step in range(1, sections):
         if step == encoders:
-            memory = None
             memory = [up(share, step - 1, step) for share in shares]
             whole, _ = lax.optimization_barrier((jnp.concatenate(shares), memory))
+            memory = jnp.concatenate(memory)
             for target in range(step + 1, sections):
                 arrived = up(whole, step - 1, target)
                 whole, _ = lax.optimization_barrier((whole, arrived))
-                memory = [
-                    jnp.where(section == target, arrived[g * piece : (g + 1) * piece], m)
-                    for g, m in enumerate(memory)
-                ]
+                memory = jnp.where(section == target, arrived, memory)
             memory, unit_queries = lax.optimization_barrier((memory, unit_queries))
             users = range(step, sections)
-            *kv, _ = keep((wk, wk_other, wv, wv_other), users, memory)
-            unit_keys, values = project_memory(gather(memory), last_gain, users, kv)
-            residuals = own_rows(decoder_embedding_batches)
+            kv = keep_keys(users, memory)
+            unit_keys, values = project_memory(gather([memory]), last_gain, users, kv)
+            residuals = target_residuals
             parts = kernel_call(
                 functools.partial(only_in([step])(mix_kernel), config),
                 partials,
@@ -459,14 +518,14 @@
                 place, sharp, sharp_other, unit_queries, unit_keys, values,
                 stay(wo, pltpu.HBM), stay(wo_other, pltpu.HBM),
             )
-            *queries_and_out, mark = keep(
-                (wq, wq_other, wo, wo_other), range(step + 1, sections), parts
-            )
         else:
             residuals = [up(share, step - 1, step) for share in shares]
             pieces = gather(residuals)
+            if step in (1, encoders + 1):
+                queries_and_out = keep_queries(range(step, sections), residuals)
             if step < encoders:
-                unit_keys, values = project_memory(pieces, gain, [step], (wk, wk_other, wv, wv_other))
+                kv = keep_keys([step], residuals)
+                unit_keys, values = project_memory(pieces, gain, [step], kv)
             parts = kernel_call(
                 functools.partial(only_in([step])(section_kernel), config),
                 partials,
@@ -478,8 +537,6 @@
                 *queries_and_out,
             )
         shares = finish(parts, residuals, step)
-        if step == encoders:
-            shares[-1], _ = lax.optimization_barrier((shares[-1], mark))
         kept = [jnp.where(section == step, share, old) for share, old in zip(shares, kept)]
 
     pieces = gather(kept)

time: 175 us -> 164 us (0.937)
  starting transfers between devices: 75.6 us -> 68.5 us
  waiting for transfers between devices: 63.4 us -> 56.5 us
  Pallas kernels: 31.3 us -> 36.3 us
  local copies, waits for them, and re-layouts: 2.7 us -> 0.73 us
    ppermute x62 -> x55, waiting for transfers between devices: 41.3 us -> 28.7 us  [flip(): return lambda x: lax.ppermute(x, 'seq', pairs)]
    ppermute x62 -> x55, starting transfers between devices: 68.4 us -> 61.3 us  [flip(): return lambda x: lax.ppermute(x, 'seq', pairs)]
    pallas_call x3 -> x5, Pallas kernels: 14.6 us -> 20.6 us  [the longest x2 12.9 us: keep(): kernel_call(functools.partial(only_in(users)(body), config), [pltpu.VMEM(...]
    ppermute x8, waiting for transfers between devices: 22.2 us -> 27.8 us  [up(): return lax.ppermute(x, 'section', [(source, target)])]
    slice x2 -> x0, local copies, waits for them, and re-layouts: 1.97 us -> none  [own_rows(): return [rows[g * piece:(g + 1) * piece] for g in range(groups)]]
    pallas_call x8 -> x6, Pallas kernels: 4.54 us -> 3.46 us  [finish(): kernel_call(functools.partial(only_in([step])(finish_kernel), config), sd...]
  transfers between devices with their start and end apart: 70 -> 63, of which waited for: 28 -> 22; matrix products, arithmetic and copies ran while one was open for 2% -> 1% of each run, Pallas kernels for 13% -> 17%
where the time goes in v3:
time: 164 us; the launch traced here: 163 us
  starting transfers between devices  68.5 us (42%)
  waiting for transfers between devices  56.5 us (34%)
  Pallas kernels  36.3 us (22%)
    ppermute x55, starting transfers between devices, flip(): return lambda x: lax.ppermute(x, 'seq', pairs)  61.3 us
    ppermute x55, waiting for transfers between devices, flip(): return lambda x: lax.ppermute(x, 'seq', pairs)  28.7 us
    ppermute x8, waiting for transfers between devices, up(): return lax.ppermute(x, 'section', [(source, target)])  27.8 us
    pallas_call x2, Pallas kernels, keep(): kernel_call(functools.partial(only_in(users)(body), config), [pltpu.VMEM(...  12.9 us
    ppermute x8, starting transfers between devices, up(): return lax.ppermute(x, 'section', [(source, target)])  7.22 us
    pallas_call x1, Pallas kernels, shards(): kernel_call(functools.partial(only_in(range(1, sections))(stack_kernel),...  6.69 us
    pallas_call x2, Pallas kernels, shards(): kernel_call(functools.partial(only_in([step])(section_kernel), config), p...  4.63 us
    pallas_call x6, Pallas kernels, finish(): kernel_call(functools.partial(only_in([step])(finish_kernel), config), sd...  3.46 us
  transfers between devices with their start and end apart: 63, of which 22 were waited for; matrix products, arithmetic and copies ran while one was open for 1% of the time, Pallas kernels for 17%

profile of v3, /device:TPU:25, one launch (start us, length us, event | category | flops | bytes accessed | tf_op | source)
XLA Modules:
  0.0 163.3 jit_solution(7943623061180454225)
XLA Ops:
  2.9 6.7 %shard_map.93 = bf16[2,4096,512]{2,1,0:T(8,128)(2,1)} custom-call(s32[3]{0:T(128)S(1)} %pad_add_fusion.place, bf16[4096,512]{1,0:T(8,128)(2,1)} %bitcast.13, bf16[4096,512]{1,0:T(8,128)(2,1)} %bitcast.16), custom_call_target="tpu_custom_call" | custom-call | tf_op jit(solution)/shard_map/pallas_call | solution.py:436
  14.0 5.2 %collective-permute-done.3.refs_3_ = bf16[32,4096]{1,0:T(8,128)(2,1)S(1)} collective-permute-done((bf16[32,4096]{1,0:T(8,128)(2,1)S(1)}, bf16[32,4096]{1,0:T(8,128)(2,1)S(1)}, u32[]{:S(2)}, u32[]{:S(2)}) %collective-permute-start.3) | collective-permute-done | bytes 262176 | tf_op jit(solution)/shard_map/ppermute | solution.py:363
  19.2 5.4 %collective-permute-done.4.refs_4_ = bf16[32,4096]{1,0:T(8,128)(2,1)S(1)} collective-permute-done((bf16[32,4096]{1,0:T(8,128)(2,1)S(1)}, bf16[32,4096]{1,0:T(8,128)(2,1)S(1)}, u32[]{:S(2)}, u32[]{:S(2)}) %collective-permute-start.4) | collective-permute-done | bytes 262176 | tf_op jit(solution)/shard_map/ppermute | solution.py:363
  30.9 23.5 %collective-permute-done.9 = bf16[32,4096]{1,0:T(8,128)(2,1)S(1)} collective-permute-done((bf16[32,4096]{1,0:T(8,128)(2,1)S(1)}, bf16[32,4096]{1,0:T(8,128)(2,1)S(1)}, u32[]{:S(2)}, u32[]{:S(2)}) %collective-permute-start.9) | collective-permute-done | bytes 262176 | tf_op jit(solution)/shard_map/ppermute | solution.py:366
  57.3 2.9 %collective-permute-start.1 = (f32[8]{0:T(128)S(1)}, f32[8]{0:T(128)S(1)}, u32[]{:S(2)}, u32[]{:S(2)}) collective-permute-start(f32[8]{0:T(128)S(1)} %multiply_bitcast_fusion.refs_0_), channel_id=1, source_target_pairs={{0,1},{1,0},{2,3},{3,2},{4,5},{5,4},{6,7},{7,6},{8,9},{9,8},{10,11... | collective-permute-start | bytes 104 | tf_op jit(solution)/shard_map/ppermute | solution.py:363
  60.2 6.4 %shard_map.96 = (bf16[4096,512]{1,0:T(8,128)(2,1)S(1)}, bf16[4096,512]{1,0:T(8,128)(2,1)S(1)}, bf16[4096,512]{1,0:T(8,128)(2,1)S(1)}, bf16[4096,512]{1,0:T(8,128)(2,1)S(1)}) custom-call(s32[3]{0:T(128)S(1)} %pad_add_fusion.place, bf16[4096,512]{1,0:T(8,128)(2,1)} %bitcast.14, bf16[4096,512]{1,0:T(8,128)(2,1)} %bitcast.17, ...), custom_call_target="tpu_custom_call" | custom-call | bytes 33554432 | tf_op jit(solution)/shard_map/pallas_call | solution.py:472
  67.0 3.4 %shard_map.97 = (bf16[128,1024]{1,0:T(8,128)(2,1)S(1)}, bf16[128,1024]{1,0:T(8,128)(2,1)S(1)}) custom-call(s32[3]{0:T(128)S(1)} %pad_add_fusion.place, f32[1,4096]{1,0:T(1,128)S(1)} %bitcast.11, bf16[32,4096]{1,0:T(8,128)(2,1)S(1)} %fusion.refs_1_, bf16[32,4096]{1,0:T(8,128)(2,1)S(1)} %collective-permute-done.10.refs_2_, ...), custom_call_target="tpu_custom_call" | custom-call | tf_op jit(solution)/shard_map/pallas_call | solution.py:489
  72.5 1.5 collective-permute-start.21
  75.2 1.5 collective-permute-start.17
  79.8 3.0 %collective-permute-done.17.refs_4_ = bf16[16,4096]{1,0:T(8,128)(2,1)S(1)} collective-permute-done((bf16[16,4096]{1,0:T(8,128)(2,1)S(1)}, bf16[16,4096]{1,0:T(8,128)(2,1)S(1)}, u32[]{:S(2)}, u32[]{:S(2)}) %collective-permute-start.17) | collective-permute-done | bytes 131104 | tf_op jit(solution)/shard_map/ppermute | solution.py:363
  84.0 1.4 collective-permute-start.24
  89.7 6.4 %shard_map.101 = (bf16[4096,512]{1,0:T(8,128)(2,1)S(1)}, bf16[4096,512]{1,0:T(8,128)(2,1)S(1)}, bf16[512,4096]{1,0:T(8,128)(2,1)S(1)}, bf16[512,4096]{1,0:T(8,128)(2,1)S(1)}) custom-call(s32[3]{0:T(128)S(1)} %pad_add_fusion.place, bf16[4096,512]{1,0:T(8,128)(2,1)} %bitcast.21, bf16[4096,512]{1,0:T(8,128)(2,1)} %collective-permute-done.refs_3_.refs_1_, ...), custom_call_target="tpu_custom_call" | custom-call | bytes 33554432 | tf_op jit(solution)/shard_map/pallas_call | solution.py:472
  108.0 3.3 %collective-permute-done.36.refs_4_.refs_0_ = bf16[16,4096]{1,0:T(8,128)(2,1)S(1)} collective-permute-done((bf16[16,4096]{1,0:T(8,128)(2,1)S(1)}, bf16[16,4096]{1,0:T(8,128)(2,1)S(1)}, u32[]{:S(2)}, u32[]{:S(2)}) %collective-permute-start.36) | collective-permute-done | bytes 131104 | tf_op jit(solution)/shard_map/ppermute | solution.py:366
  112.1 1.9 %collective-permute-start.42 = (bf16[16,4096]{1,0:T(8,128)(2,1)S(1)}, bf16[16,4096]{1,0:T(8,128)(2,1)S(1)}, u32[]{:S(2)}, u32[]{:S(2)}) collective-permute-start(bf16[16,4096]{1,0:T(8,128)(2,1)S(1)} %collective-permute-done.36.refs_4_.refs_0_), channel_id=1, source_target_pairs={{0,6},{1,7},{2,4},{3,5},{4,2},{5,3},{6,0},{7,1},{8,14},{9,15},{10,... | collective-permute-start | bytes 393224 | tf_op jit(solution)/shard_map/ppermute | solution.py:363
  115.8 1.7 %collective-permute-start.41 = (bf16[16,4096]{1,0:T(8,128)(2,1)S(1)}, bf16[16,4096]{1,0:T(8,128)(2,1)S(1)}, u32[]{:S(2)}, u32[]{:S(2)}) collective-permute-start(bf16[16,4096]{1,0:T(8,128)(2,1)S(1)} %collective-permute-done.32.refs_3_.refs_0_), channel_id=1, source_target_pairs={{0,6},{1,7},{2,4},{3,5},{4,2},{5,3},{6,0},{7,1},{8,14},{9,15},{10,... | collective-permute-start | bytes 393224 | tf_op jit(solution)/shard_map/ppermute | solution.py:363
  118.7 1.8 %collective-permute-done.41.refs_9_ = bf16[16,4096]{1,0:T(8,128)(2,1)S(1)} collective-permute-done((bf16[16,4096]{1,0:T(8,128)(2,1)S(1)}, bf16[16,4096]{1,0:T(8,128)(2,1)S(1)}, u32[]{:S(2)}, u32[]{:S(2)}) %collective-permute-start.41) | collective-permute-done | bytes 131104 | tf_op jit(solution)/shard_map/ppermute | solution.py:363
  120.5 4.1 %shard_map.105 = (bf16[16,4096]{1,0:T(8,128)(2,1)S(1)}, bf16[16,4096]{1,0:T(8,128)(2,1)S(1)}, bf16[16,4096]{1,0:T(8,128)(2,1)S(1)}, bf16[16,4096]{1,0:T(8,128)(2...) custom-call(s32[3]{0:T(128)S(1)} %pad_add_fusion.place, ...), custom_call_target="tpu_custom_call" | custom-call | tf_op jit(solution)/shard_map/pallas_call | solution.py:529
  124.6 1.4 collective-permute-start.46
  127.3 1.4 collective-permute-start.43
  130.1 1.7 %collective-permute-start.45 = (bf16[16,4096]{1,0:T(8,128)(2,1)S(1)}, bf16[16,4096]{1,0:T(8,128)(2,1)S(1)}, u32[]{:S(2)}, u32[]{:S(2)}) collective-permute-start(bf16[16,4096]{1,0:T(8,128)(2,1)S(1)} %get-tuple-element.124), channel_id=1, source_target_pairs={{0,6},{1,7},{2,4},{3,5},{4,2},{5,3},{6,0},{7,1},{8,14},{9,15},{10,... | collective-permute-start | bytes 393224 | tf_op jit(solution)/shard_map/ppermute | solution.py:363
  136.1 13.3 %collective-permute-start.56 = (bf16[16,4096]{1,0:T(8,128)(2,1)S(1)}, bf16[16,4096]{1,0:T(8,128)(2,1)S(1)}, u32[]{:S(2)}, u32[]{:S(2)}) collective-permute-start(bf16[16,4096]{1,0:T(8,128)(2,1)S(1)} %select_select_fusion.refs_1_), channel_id=1, source_target_pairs={{0,1},{1,0},{2,3},{3,2},{4,5},{5,4},{6,7},{7,6},{8,9},{9,8},{10,11... | collective-permute-start | bytes 393224 | tf_op jit(solution)/shard_map/ppermute | solution.py:363
  153.9 1.3 collective-permute-done.49.refs_2_
  156.5 2.4 %collective-permute-done.53.refs_6_ = bf16[16,4096]{1,0:T(8,128)(2,1)S(1)} collective-permute-done((bf16[16,4096]{1,0:T(8,128)(2,1)S(1)}, bf16[16,4096]{1,0:T(8,128)(2,1)S(1)}, u32[]{:S(2)}, u32[]{:S(2)}) %collective-permute-start.53) | collective-permute-done | bytes 131104 | tf_op jit(solution)/shard_map/ppermute | solution.py:363
  161.3 2.0 %shard_map.108 = bf16[2,128,4096]{2,1,0:T(8,128)(2,1)} custom-call(s32[3]{0:T(128)S(1)} %pad_add_fusion.place, bf16[16,4096]{1,0:T(8,128)(2,1)S(1)} %select_select_fusion.1.refs_0_, bf16[16,4096]{1,0:T(8,128)(2,1)S(1)} %select_select_fusion.refs_1_, bf16[16,4096]{1,0:T(8,128)(2,1)S(1)} %collective-permute-done.49.refs_2_, ...), custom_call_target="tpu_custom_call" | custom-call | tf_op jit(solution)/shard_map/pallas_call | solution.py:544
  (132 shorter events, 59.2 us)
Async XLA Ops:
  0.0 10.2 %collective-permute-start = (bf16[4096,512]{1,0:T(8,128)(2,1)}, bf16[4096,512]{1,0:T(8,128)(2,1)}, u32[]{:S(2)}, u32[]{:S(2)}) collective-permute-start(bf16[4096,512]{1,0:T(8,128)(2,1)} %bitcast.18), channel_id=1, source_target_pairs={{0,1},{1,0},{2,3},{3,2},{4,5},{5,4},{6,7},{7,6},{8,9},{9,8},{10,11... | collective-permute-start | bytes 12582920 | tf_op jit(solution)/shard_map/ppermute | solution.py:363
  10.8 46.5 %collective-permute-start.13 = (bf16[2,4096,512]{2,1,0:T(8,128)(2,1)}, bf16[2,4096,512]{2,1,0:T(8,128)(2,1)}, u32[]{:S(2)}, u32[]{:S(2)}) collective-permute-start(bf16[2,4096,512]{2,1,0:T(8,128)(2,1)} %shard_map.93), channel_id=1, source_target_pairs={{0,1},{1,0},{2,3},{3,2},{4,5},{5,4},{6,7},{7,6},{8,9},{9,8},{10,11... | collective-permute-start | bytes 25165832 | tf_op jit(solution)/shard_map/ppermute | solution.py:363
  11.3 7.9 %collective-permute-start.3 = (bf16[32,4096]{1,0:T(8,128)(2,1)S(1)}, bf16[32,4096]{1,0:T(8,128)(2,1)S(1)}, u32[]{:S(2)}, u32[]{:S(2)}) collective-permute-start(bf16[32,4096]{1,0:T(8,128)(2,1)S(1)} %get-tuple-element.80), channel_id=1, source_target_pairs={{0,2},{1,3},{2,0},{3,1},{4,6},{5,7},{6,4},{7,5},{8,10},{9,11},{10,... | collective-permute-start | bytes 786440 | tf_op jit(solution)/shard_map/ppermute | solution.py:363
  12.6 12.1 %collective-permute-start.4 = (bf16[32,4096]{1,0:T(8,128)(2,1)S(1)}, bf16[32,4096]{1,0:T(8,128)(2,1)S(1)}, u32[]{:S(2)}, u32[]{:S(2)}) collective-permute-start(bf16[32,4096]{1,0:T(8,128)(2,1)S(1)} %get-tuple-element.81), channel_id=1, source_target_pairs={{0,4},{1,5},{2,6},{3,7},{4,0},{5,1},{6,2},{7,3},{8,12},{9,13},{10,... | collective-permute-start | bytes 786440 | tf_op jit(solution)/shard_map/ppermute | solution.py:363
  13.8 12.0 %collective-permute-start.5 = (bf16[32,4096]{1,0:T(8,128)(2,1)S(1)}, bf16[32,4096]{1,0:T(8,128)(2,1)S(1)}, u32[]{:S(2)}, u32[]{:S(2)}) collective-permute-start(bf16[32,4096]{1,0:T(8,128)(2,1)S(1)} %get-tuple-element.82), channel_id=1, source_target_pairs={{0,6},{1,7},{2,4},{3,5},{4,2},{5,3},{6,0},{7,1},{8,14},{9,15},{10,... | collective-permute-start | bytes 786440 | tf_op jit(solution)/shard_map/ppermute | solution.py:363
  26.4 44.0 %collective-permute-start.14 = (bf16[512,4096]{1,0:T(8,128)(2,1)}, bf16[512,4096]{1,0:T(8,128)(2,1)}, u32[]{:S(2)}, u32[]{:S(2)}) collective-permute-start(bf16[512,4096]{1,0:T(8,128)(2,1)} %bitcast.7.refs_6_.refs_5_.refs_2_), channel_id=1, source_target_pairs={{0,1},{1,0},{2,3},{3,2},{4,5},{5,4},{6,7},{7,6},{8,9},{9,8},{10,11... | collective-permute-start | bytes 12582920 | tf_op jit(solution)/shard_map/ppermute | solution.py:363
  29.6 24.9 %collective-permute-start.9 = (bf16[32,4096]{1,0:T(8,128)(2,1)S(1)}, bf16[32,4096]{1,0:T(8,128)(2,1)S(1)}, u32[]{:S(2)}, u32[]{:S(2)}) collective-permute-start(bf16[32,4096]{1,0:T(8,128)(2,1)S(1)} %pad_maximum_fusion), channel_id=1, source_target_pairs={{0,24},{1,25},{2,26},{3,27},{4,28},{5,29},{6,30},{7,31}} | collective-permute-start | bytes 786440 | tf_op jit(solution)/shard_map/ppermute | solution.py:366
  54.6 12.0 %collective-permute-start.10 = (bf16[32,4096]{1,0:T(8,128)(2,1)S(1)}, bf16[32,4096]{1,0:T(8,128)(2,1)S(1)}, u32[]{:S(2)}, u32[]{:S(2)}) collective-permute-start(bf16[32,4096]{1,0:T(8,128)(2,1)S(1)} %fusion.refs_1_), channel_id=1, source_target_pairs={{0,2},{1,3},{2,0},{3,1},{4,6},{5,7},{6,4},{7,5},{8,10},{9,11},{10,... | collective-permute-start | bytes 786440 | tf_op jit(solution)/shard_map/ppermute | solution.py:363
  55.6 11.0 %collective-permute-start.11 = (bf16[32,4096]{1,0:T(8,128)(2,1)S(1)}, bf16[32,4096]{1,0:T(8,128)(2,1)S(1)}, u32[]{:S(2)}, u32[]{:S(2)}) collective-permute-start(bf16[32,4096]{1,0:T(8,128)(2,1)S(1)} %fusion.refs_1_), channel_id=1, source_target_pairs={{0,4},{1,5},{2,6},{3,7},{4,0},{5,1},{6,2},{7,3},{8,12},{9,13},{10,... | collective-permute-start | bytes 786440 | tf_op jit(solution)/shard_map/ppermute | solution.py:363
  56.2 10.8 %collective-permute-start.12 = (bf16[32,4096]{1,0:T(8,128)(2,1)S(1)}, bf16[32,4096]{1,0:T(8,128)(2,1)S(1)}, u32[]{:S(2)}, u32[]{:S(2)}) collective-permute-start(bf16[32,4096]{1,0:T(8,128)(2,1)S(1)} %fusion.refs_1_), channel_id=1, source_target_pairs={{0,6},{1,7},{2,4},{3,5},{4,2},{5,3},{6,0},{7,1},{8,14},{9,15},{10,... | collective-permute-start | bytes 786440 | tf_op jit(solution)/shard_map/ppermute | solution.py:363
  57.3 13.1 %collective-permute-start.1 = (f32[8]{0:T(128)S(1)}, f32[8]{0:T(128)S(1)}, u32[]{:S(2)}, u32[]{:S(2)}) collective-permute-start(f32[8]{0:T(128)S(1)} %multiply_bitcast_fusion.refs_0_), channel_id=1, source_target_pairs={{0,1},{1,0},{2,3},{3,2},{4,5},{5,4},{6,7},{7,6},{8,9},{9,8},{10,11... | collective-permute-start | bytes 104 | tf_op jit(solution)/shard_map/ppermute | solution.py:363
  75.2 7.6 %collective-permute-start.17 = (bf16[16,4096]{1,0:T(8,128)(2,1)S(1)}, bf16[16,4096]{1,0:T(8,128)(2,1)S(1)}, u32[]{:S(2)}, u32[]{:S(2)}) collective-permute-start(bf16[16,4096]{1,0:T(8,128)(2,1)S(1)} %get-tuple-element.102), channel_id=1, source_target_pairs={{0,6},{1,7},{2,4},{3,5},{4,2},{5,3},{6,0},{7,1},{8,14},{9,15},{10,... | collective-permute-start | bytes 393224 | tf_op jit(solution)/shard_map/ppermute | solution.py:363
  85.4 10.7 %collective-permute-start.26 = (bf16[16,4096]{1,0:T(8,128)(2,1)S(1)}, bf16[16,4096]{1,0:T(8,128)(2,1)S(1)}, u32[]{:S(2)}, u32[]{:S(2)}) collective-permute-start(bf16[16,4096]{1,0:T(8,128)(2,1)S(1)} %collective-permute-done.22.refs_4_.refs_0_), channel_id=1, source_target_pairs={{0,4},{1,5},{2,6},{3,7},{4,0},{5,1},{6,2},{7,3},{8,12},{9,13},{10,... | collective-permute-start | bytes 393224 | tf_op jit(solution)/shard_map/ppermute | solution.py:363
  86.2 10.0 %collective-permute-start.28 = (bf16[16,4096]{1,0:T(8,128)(2,1)S(1)}, bf16[16,4096]{1,0:T(8,128)(2,1)S(1)}, u32[]{:S(2)}, u32[]{:S(2)}) collective-permute-start(bf16[16,4096]{1,0:T(8,128)(2,1)S(1)} %collective-permute-done.22.refs_4_.refs_0_), channel_id=1, source_target_pairs={{0,6},{1,7},{2,4},{3,5},{4,2},{5,3},{6,0},{7,1},{8,14},{9,15},{10,... | collective-permute-start | bytes 393224 | tf_op jit(solution)/shard_map/ppermute | solution.py:363
  86.7 9.4 %collective-permute-start.23 = (bf16[16,4096]{1,0:T(8,128)(2,1)S(1)}, bf16[16,4096]{1,0:T(8,128)(2,1)S(1)}, u32[]{:S(2)}, u32[]{:S(2)}) collective-permute-start(bf16[16,4096]{1,0:T(8,128)(2,1)S(1)} %collective-permute-done.18.refs_3_.refs_0_), channel_id=1, source_target_pairs={{0,2},{1,3},{2,0},{3,1},{4,6},{5,7},{6,4},{7,5},{8,10},{9,11},{10,... | collective-permute-start | bytes 393224 | tf_op jit(solution)/shard_map/ppermute | solution.py:363
  88.0 8.1 %collective-permute-start.25 = (bf16[16,4096]{1,0:T(8,128)(2,1)S(1)}, bf16[16,4096]{1,0:T(8,128)(2,1)S(1)}, u32[]{:S(2)}, u32[]{:S(2)}) collective-permute-start(bf16[16,4096]{1,0:T(8,128)(2,1)S(1)} %collective-permute-done.18.refs_3_.refs_0_), channel_id=1, source_target_pairs={{0,4},{1,5},{2,6},{3,7},{4,0},{5,1},{6,2},{7,3},{8,12},{9,13},{10,... | collective-permute-start | bytes 393224 | tf_op jit(solution)/shard_map/ppermute | solution.py:363
  88.8 7.6 %collective-permute-start.27 = (bf16[16,4096]{1,0:T(8,128)(2,1)S(1)}, bf16[16,4096]{1,0:T(8,128)(2,1)S(1)}, u32[]{:S(2)}, u32[]{:S(2)}) collective-permute-start(bf16[16,4096]{1,0:T(8,128)(2,1)S(1)} %collective-permute-done.18.refs_3_.refs_0_), channel_id=1, source_target_pairs={{0,6},{1,7},{2,4},{3,5},{4,2},{5,3},{6,0},{7,1},{8,14},{9,15},{10,... | collective-permute-start | bytes 393224 | tf_op jit(solution)/shard_map/ppermute | solution.py:363
  106.7 8.2 %collective-permute-start.32 = (bf16[16,4096]{1,0:T(8,128)(2,1)S(1)}, bf16[16,4096]{1,0:T(8,128)(2,1)S(1)}, u32[]{:S(2)}, u32[]{:S(2)}) collective-permute-start(bf16[16,4096]{1,0:T(8,128)(2,1)S(1)} %shard_map.103), channel_id=1, source_target_pairs={{16,24},{17,25},{18,26},{19,27},{20,28},{21,29},{22,30},{23,31}} | collective-permute-start | bytes 393224 | tf_op jit(solution)/shard_map/ppermute | solution.py:366
  130.1 19.2 %collective-permute-start.45 = (bf16[16,4096]{1,0:T(8,128)(2,1)S(1)}, bf16[16,4096]{1,0:T(8,128)(2,1)S(1)}, u32[]{:S(2)}, u32[]{:S(2)}) collective-permute-start(bf16[16,4096]{1,0:T(8,128)(2,1)S(1)} %get-tuple-element.124), channel_id=1, source_target_pairs={{0,6},{1,7},{2,4},{3,5},{4,2},{5,3},{6,0},{7,1},{8,14},{9,15},{10,... | collective-permute-start | bytes 393224 | tf_op jit(solution)/shard_map/ppermute | solution.py:363
  133.3 17.3 %collective-permute-start.50 = (bf16[16,4096]{1,0:T(8,128)(2,1)S(1)}, bf16[16,4096]{1,0:T(8,128)(2,1)S(1)}, u32[]{:S(2)}, u32[]{:S(2)}) collective-permute-start(bf16[16,4096]{1,0:T(8,128)(2,1)S(1)} %select_select_fusion.refs_1_), channel_id=1, source_target_pairs={{0,2},{1,3},{2,0},{3,1},{4,6},{5,7},{6,4},{7,5},{8,10},{9,11},{10,... | collective-permute-start | bytes 393224 | tf_op jit(solution)/shard_map/ppermute | solution.py:363
  134.6 16.8 %collective-permute-start.52 = (bf16[16,4096]{1,0:T(8,128)(2,1)S(1)}, bf16[16,4096]{1,0:T(8,128)(2,1)S(1)}, u32[]{:S(2)}, u32[]{:S(2)}) collective-permute-start(bf16[16,4096]{1,0:T(8,128)(2,1)S(1)} %select_select_fusion.refs_1_), channel_id=1, source_target_pairs={{0,4},{1,5},{2,6},{3,7},{4,0},{5,1},{6,2},{7,3},{8,12},{9,13},{10,... | collective-permute-start | bytes 393224 | tf_op jit(solution)/shard_map/ppermute | solution.py:363
  134.8 17.9 %collective-permute-start.54 = (bf16[16,4096]{1,0:T(8,128)(2,1)S(1)}, bf16[16,4096]{1,0:T(8,128)(2,1)S(1)}, u32[]{:S(2)}, u32[]{:S(2)}) collective-permute-start(bf16[16,4096]{1,0:T(8,128)(2,1)S(1)} %select_select_fusion.refs_1_), channel_id=1, source_target_pairs={{0,6},{1,7},{2,4},{3,5},{4,2},{5,3},{6,0},{7,1},{8,14},{9,15},{10,... | collective-permute-start | bytes 393224 | tf_op jit(solution)/shard_map/ppermute | solution.py:363
  136.1 17.7 %collective-permute-start.56 = (bf16[16,4096]{1,0:T(8,128)(2,1)S(1)}, bf16[16,4096]{1,0:T(8,128)(2,1)S(1)}, u32[]{:S(2)}, u32[]{:S(2)}) collective-permute-start(bf16[16,4096]{1,0:T(8,128)(2,1)S(1)} %select_select_fusion.refs_1_), channel_id=1, source_target_pairs={{0,1},{1,0},{2,3},{3,2},{4,5},{5,4},{6,7},{7,6},{8,9},{9,8},{10,11... | collective-permute-start | bytes 393224 | tf_op jit(solution)/shard_map/ppermute | solution.py:363
  151.4 7.6 %collective-permute-start.53 = (bf16[16,4096]{1,0:T(8,128)(2,1)S(1)}, bf16[16,4096]{1,0:T(8,128)(2,1)S(1)}, u32[]{:S(2)}, u32[]{:S(2)}) collective-permute-start(bf16[16,4096]{1,0:T(8,128)(2,1)S(1)} %select_select_fusion.1.refs_0_), channel_id=1, source_target_pairs={{0,6},{1,7},{2,4},{3,5},{4,2},{5,3},{6,0},{7,1},{8,14},{9,15},{10,... | collective-permute-start | bytes 393224 | tf_op jit(solution)/shard_map/ppermute | solution.py:363
  (42 other events, 209.5 us)

commit v4 on v2

--- a/solution.py
+++ b/solution.py
@@ -171,8 +171,16 @@
     return wrap
 
 
-def first_kernel(config, place, sharp, gain, source, wq, wk, wv, wo, own_ref, other_ref,
-                 raw, rows, wq_s, wk_s, wv_s, wo_s, uq, uk, v, mixture, sems):
+def give_rows(raw, outs):
+    low = 0
+    for out in outs:
+        out[...] = raw[low : low + out.shape[0], :]
+        low += out.shape[0]
+
+
+def first_kernel(config, place, sharp, gain, source, wq, wk, wv, wo, own_ref, other_ref, *refs):
+    residuals, refs = refs[:-11], refs[-11:]
+    raw, rows, wq_s, wk_s, wv_s, wo_s, uq, uk, v, mixture, sems = refs
     head, blocks, length, _ = config
     copies = Copies(sems)
     chip, core = place[0], place[1]
@@ -182,6 +190,7 @@
     arrivals = stream_out(copies, ((wo, wo_s),))
     for wait in waits:
         wait.wait()
+    give_rows(raw, residuals)
     normalize_rows(raw, rows, gain)
     normed = rows[...]
     wide = wq.shape[1]
@@ -223,25 +232,27 @@
     return arrivals
 
 
-def query_kernel(config, place, gain, source, wq_own, wq_other, uq_ref, raw, rows, wq_s, sems):
-    head, blocks, _, _ = config
+def query_kernel(config, place, gain, source, wq, own_ref, other_ref, *refs):
+    residuals, (raw, rows, wq_s, uq, sems) = refs[:-5], refs[-5:]
+    head, blocks, length, _ = config
     copies = Copies(sems)
-    waits = load_rows(copies, source, place[1], raw, 0, place[0], blocks)
-    arrivals = [
-        copies.start(weight, wq_s.at[i]) for i, weight in enumerate((wq_own, wq_other))
-    ]
+    chip, core = place[0], place[1]
+    waits = load_rows(copies, source, core, raw, 0, chip, blocks)
+    waits += load_rows(copies, source, 1 - core, raw, length, chip, blocks)
+    arrival = copies.start(wq, wq_s)
     for wait in waits:
         wait.wait()
+    give_rows(raw, residuals)
     normalize_rows(raw, rows, gain)
-    for wait in arrivals:
-        wait.wait()
-    project(rows[...], (wq_s.at[0], wq_s.at[1]), uq_ref, lambda x: unit(x, head))
+    arrival.wait()
+    project(rows[...], (wq_s,), uq, lambda x: unit(x, head), wq.shape[1])
+    own_ref[...] = uq[:length, :]
+    other_ref[...] = uq[length:, :]
 
 
 def memory_kernel(config, place, gain, *refs):
-    head, _, _, count = config
-    pieces, refs = refs[:count], refs[count:]
-    wk_own, wk_other, wv_own, wv_other, uk_ref, v_ref, rows = refs
+    head = config[0]
+    pieces, (wk_own, wk_other, wv_own, wv_other, uk_ref, v_ref, rows) = refs[:-7], refs[-7:]
     normalize_pieces(pieces, rows, gain)
     normed = rows[...]
     project(normed, (wk_own, wk_other), uk_ref, lambda x: unit(x, head))
@@ -249,18 +260,25 @@
 
 
 def keep_kernel(config, place, *refs):
-    count = len(refs) // 2 - 1
-    copies = Copies(refs[-1])
+    sems, refs = refs[-1], refs[:-1]
+    count = len(refs) // 2
+    copies = Copies(sems)
     for wait in [copies.start(refs[i], refs[count + i]) for i in range(count)]:
         wait.wait()
-    refs[2 * count][...] = jnp.zeros_like(refs[2 * count])
-
-
-def mix_kernel(config, place, sharp_own, sharp_other, uq, uk, v, wo_own, wo_other, *refs):
-    outs, (mixture, own_s, other_s, sems) = refs[:-4], refs[-4:]
-    arrivals = stream_out(Copies(sems), ((wo_own, own_s), (wo_other, other_s)))
+    refs[-1][...] = jnp.zeros_like(refs[-1])
+
+
+def mix_kernel(config, place, sharp_own, sharp_other, uq_own, uq_other, uk, v, *refs):
+    wo_own, wo_other, outs, (uq, mixture) = refs[0], refs[1], refs[2:-2], refs[-2:]
+    inner = uq_own.shape[1]
+    uq[:, :inner] = uq_own[...]
+    uq[:, inner:] = uq_other[...]
     attend_all(uq, uk, v, (sharp_own, sharp_other), mixture, config[0])
-    project_out(mixture[...], (own_s, other_s), outs, arrivals)
+    project_out(mixture[...], (wo_own, wo_other), outs)
+
+
+def pass_kernel(share, mark, out):
+    out[...] = share[...]
 
 
 def section_kernel(config, place, sharp_own, sharp_other, gain, *refs):
@@ -335,7 +353,6 @@
     last_gain = last_rescale_weights.reshape(1, width)
     sharp = logit_sharpness[0] * (head ** -0.5)
     sharp_other = to_core(sharp)
-    wq_other = to_core(wq)
     stay = pltpu.with_memory_space_constraint
 
     place = jnp.stack([chip, core, section]).astype(jnp.int32)
@@ -353,16 +370,19 @@
         return pltpu.SemaphoreType.DMA((n,))
 
     def gather(shares):
-        by_group = [[share] + [to_chip[j](share) for j in range(1, blocks)] for share in shares]
-        return [by_group[g][j] for j in range(blocks) for g in range(groups)]
-
-    def finish(parts, residuals, step):
+        by_group = []
+        for share in shares:
+            others = {j: to_chip[j](share) for j in reversed(range(1, blocks))}
+            by_group.append([share] + [others[j] for j in range(1, blocks)])
+        return [group[j] for j in range(blocks) for group in by_group]
+
+    def finish(parts, residuals):
         shares = []
         for g, residual in enumerate(residuals):
-            arrived = [to_chip[j](parts[j * groups + g]) for j in range(1, blocks)]
+            arrived = [to_chip[j](parts[j * groups + g]) for j in reversed(range(1, blocks))]
             shares.append(
                 kernel_call(
-                    functools.partial(only_in([step])(finish_kernel), config),
+                    functools.partial(finish_kernel, config),
                     sds((piece, width)),
                     [IN_SMEM] + [IN_VMEM] * (blocks + 1),
                     [],
@@ -371,115 +391,162 @@
             )
         return shares
 
-    def own_rows(source):
-        rows = lax.dynamic_slice(source, (core, chip * height, 0), (1, height, width))[0]
-        return [rows[g * piece : (g + 1) * piece] for g in range(groups)]
-
-    own, other = kernel_call(
-        functools.partial(only_in([0])(first_kernel), config),
-        [sds((length, width))] * 2,
-        [IN_SMEM, IN_SMEM, IN_VMEM] + [IN_HBM] * 5,
-        [pltpu.VMEM((batches * length, width), BF16)] * 2
-        + [pltpu.VMEM((width, inner), BF16)] * 3
-        + [out_weight]
-        + [pltpu.VMEM((batches * length, inner), BF16)] * 4
-        + [sems(batches * blocks + 3 + width // OUT_WIDE)],
-        32,
-    )(place, sharp, gain, *(stay(x, pltpu.HBM) for x in (inbound_embedding_batches, wq, wk, wv, wo)))
-    parts = kernel_call(
-        functools.partial(only_in([0])(join_kernel), config),
-        partials,
-        [IN_SMEM] + [IN_VMEM] * 2,
-        [],
-        8,
-    )(place, own, to_core(other))
-
-    unit_queries = kernel_call(
-        functools.partial(only_in([encoders])(query_kernel), config),
-        sds((length, both)),
-        [IN_SMEM, IN_VMEM] + [IN_HBM] * 3,
-        [row_scratch, row_scratch, pltpu.VMEM((cores, width, inner), BF16), sems(blocks + cores)],
-        18,
-        flops=2 * length * width * both,
-        moved=2 * width * both,
-    )(place, gain, *(stay(x, pltpu.HBM) for x in (decoder_embedding_batches, wq, wq_other)))
-
-    parts, unit_queries, wk, wv = lax.optimization_barrier((parts, unit_queries, wk, wv))
-    wk_other, wv_other = to_core(wk), to_core(wv)
-    shares = finish(parts, own_rows(inbound_embedding_batches), 0)
-    kept = shares
-    _, late_wo = lax.optimization_barrier((shares[0], wo))
-    wo_other = to_core(late_wo)
-
-    def keep(arrays, users, after):
-        after, at_place = lax.optimization_barrier((after, place))
+    def finish_whole(parts, residual):
+        arrived = [to_chip[j](parts[j]) for j in reversed(range(1, blocks))]
         return kernel_call(
-            functools.partial(only_in(users)(keep_kernel), config),
-            [pltpu.VMEM(x.shape, x.dtype) for x in arrays] + [sds((8, LANES))],
+            functools.partial(finish_kernel, config),
+            sds((height, width)),
+            [IN_SMEM] + [IN_VMEM] * (1 + blocks),
+            [],
+            6,
+        )(place, residual, parts[0], *arrived)
+
+    residual_shapes = [sds((piece, width))] * groups
+
+    def zeros(shapes):
+        return [jnp.zeros(x.shape, x.dtype) for x in shapes]
+
+    def choose(chosen, body, shapes):
+        return lax.cond(chosen, lambda: list(body()), lambda: zeros(shapes))
+
+    def first_section():
+        own, other, residual = kernel_call(
+            functools.partial(first_kernel, config),
+            [sds((length, width))] * 2 + [sds((height, width))],
+            [IN_SMEM, IN_SMEM, IN_VMEM] + [IN_HBM] * 5,
+            [pltpu.VMEM((batches * length, width), BF16)] * 2
+            + [pltpu.VMEM((width, inner), BF16)] * 3
+            + [out_weight]
+            + [pltpu.VMEM((batches * length, inner), BF16)] * 4
+            + [sems(batches * blocks + 3 + width // OUT_WIDE)],
+            32,
+        )(
+            place, sharp, gain,
+            *(stay(x, pltpu.HBM) for x in (inbound_embedding_batches, wq, wk, wv, wo)),
+        )
+        parts = kernel_call(
+            functools.partial(join_kernel, config),
+            [sds((height, width))] * blocks,
+            [IN_SMEM] + [IN_VMEM] * 2,
+            [],
+            8,
+        )(place, own, to_core(other))
+        return [finish_whole(parts, residual)]
+
+    def decoder_queries():
+        own, other, *residuals = kernel_call(
+            functools.partial(query_kernel, config),
+            [sds((length, inner))] * 2 + residual_shapes,
+            [IN_SMEM, IN_VMEM] + [IN_HBM] * 2,
+            [pltpu.VMEM((batches * length, width), BF16)] * 2
+            + [pltpu.VMEM((width, inner), BF16), pltpu.VMEM((batches * length, inner), BF16)]
+            + [sems(batches * blocks + 1)],
+            20,
+        )(place, gain, *(stay(x, pltpu.HBM) for x in (decoder_embedding_batches, wq)))
+        return [own, to_core(other), *residuals]
+
+    def exchange():
+        return [to_core(w) for w in (wk, wv, wo, wq)]
+
+    def no_exchange():
+        arrays = [wk, wv, wo, wq] + query_shapes
+        return list(
+            pl.pallas_call(
+                lambda *refs: None,
+                out_shape=[pltpu.HBM(x.shape, x.dtype) for x in arrays],
+                out_specs=[IN_HBM] * len(arrays),
+            )()
+        )
+
+    share_shape = [sds((height, width))]
+    query_shapes = [sds((length, inner))] * 2 + residual_shapes
+    whole, wk_other, wv_other, wo_other, wq_other, queries_own, queries_other, *target_residuals = lax.switch(
+        jnp.where(section == 0, 0, jnp.where(section == encoders, 1, 2)),
+        [
+            lambda: first_section() + no_exchange(),
+            lambda: zeros(share_shape) + exchange() + decoder_queries(),
+            lambda: zeros(share_shape) + exchange() + zeros(query_shapes),
+        ],
+    )
+    kept = whole
+
+    def keep(arrays, after, users=None):
+        _, at_place = lax.optimization_barrier((after, place))
+        body = keep_kernel if users is None else only_in(users)(keep_kernel)
+        return kernel_call(
+            functools.partial(body, config),
+            [pltpu.VMEM(x.shape, BF16) for x in arrays] + [sds((8, LANES))],
             [IN_SMEM] + [IN_HBM] * len(arrays),
             [sems(len(arrays))],
             2,
-            moved=2 * sum(x.size * x.dtype.itemsize for x in arrays),
+            moved=4 * len(arrays) * width * inner,
         )(at_place, *(stay(x, pltpu.HBM) for x in arrays))
 
-    def project_memory(pieces, scale, users, kv):
+    def project_memory(pieces, scale, kv):
         return kernel_call(
-            functools.partial(only_in(users)(memory_kernel), config),
+            functools.partial(memory_kernel, config),
             [sds((length, both))] * 2,
-            [IN_SMEM] + [IN_VMEM] * (1 + count + 4),
+            [IN_SMEM] + [IN_VMEM] * (1 + len(pieces) + 4),
             [row_scratch],
             10,
         )(place, scale, *pieces, *kv)
 
-    queries_and_out = (wq, wq_other, wo, wo_other)
+    def first_decoder(memory):
+        *near, _ = keep((wk, wk_other, wv, wv_other, wo, wo_other), memory)
+        keys_values = list(project_memory(gather([memory]), last_gain, near[:4]))
+        parts = kernel_call(
+            functools.partial(mix_kernel, config),
+            partials,
+            [IN_SMEM] * 3 + [IN_VMEM] * 6,
+            [both_scratch, both_scratch],
+            12,
+        )(place, sharp, sharp_other, queries_own, queries_other, *keys_values, *near[4:])
+        return keys_values + finish(parts, target_residuals)
+
+    def other_sections(share):
+        arrived = {target: up(share, encoders - 1, target) for target in range(encoders + 1, sections)}
+        memory = arrived[sections - 1]
+        for target in reversed(range(encoders + 1, sections - 1)):
+            memory = jnp.where(section == target, arrived[target], memory)
+        *near, _ = keep((wk, wk_other, wv, wv_other), memory)
+        keys_values = list(project_memory(gather([memory]), last_gain, near))
+        return keys_values + zeros(residual_shapes)
+
+    def halves(share):
+        return [share[g * piece : (g + 1) * piece] for g in range(groups)]
+
+    kept = halves(kept)
+    shares = kept
+    unit_keys = whole
     for step in range(1, sections):
         if step == encoders:
-            memory = None
-            memory = [up(share, step - 1, step) for share in shares]
-            whole, _ = lax.optimization_barrier((jnp.concatenate(shares), memory))
-            for target in range(step + 1, sections):
-                arrived = up(whole, step - 1, target)
-                whole, _ = lax.optimization_barrier((whole, arrived))
-                memory = [
-                    jnp.where(section == target, arrived[g * piece : (g + 1) * piece], m)
-                    for g, m in enumerate(memory)
-                ]
-            memory, unit_queries = lax.optimization_barrier((memory, unit_queries))
-            users = range(step, sections)
-            *kv, _ = keep((wk, wk_other, wv, wv_other), users, memory)
-            unit_keys, values = project_memory(gather(memory), last_gain, users, kv)
-            residuals = own_rows(decoder_embedding_batches)
-            parts = kernel_call(
-                functools.partial(only_in([step])(mix_kernel), config),
-                partials,
-                [IN_SMEM] * 3 + [IN_VMEM] * 3 + [IN_HBM] * 2,
-                [both_scratch, out_weight, out_weight, sems(2 * (width // OUT_WIDE))],
-                16,
-            )(
-                place, sharp, sharp_other, unit_queries, unit_keys, values,
-                stay(wo, pltpu.HBM), stay(wo_other, pltpu.HBM),
-            )
-            *queries_and_out, mark = keep(
-                (wq, wq_other, wo, wo_other), range(step + 1, sections), parts
+            if step > 1:
+                whole = jnp.concatenate(shares)
+            memory = up(whole, step - 1, step)
+            unit_keys, values, *shares = lax.cond(
+                section == step,
+                functools.partial(first_decoder, memory),
+                functools.partial(other_sections, whole),
             )
         else:
+            if step in (1, encoders + 1):
+                *near, mark = keep((wq, wq_other, wo, wo_other), unit_keys, range(step, sections))
+                shares[-1] = kernel_call(
+                    pass_kernel, sds((piece, width)), [IN_VMEM] * 2, [], 4
+                )(shares[-1], mark)
             residuals = [up(share, step - 1, step) for share in shares]
             pieces = gather(residuals)
             if step < encoders:
-                unit_keys, values = project_memory(pieces, gain, [step], (wk, wk_other, wv, wv_other))
+                *kv, _ = keep((wk, wk_other, wv, wv_other), residuals)
+                unit_keys, values = project_memory(pieces, gain, kv)
             parts = kernel_call(
                 functools.partial(only_in([step])(section_kernel), config),
                 partials,
                 [IN_SMEM] * 3 + [IN_VMEM] * (1 + count + 6),
                 [row_scratch, both_scratch, both_scratch],
                 10,
-            )(
-                place, sharp, sharp_other, gain, *pieces, unit_keys, values,
-                *queries_and_out,
-            )
-        shares = finish(parts, residuals, step)
-        if step == encoders:
-            shares[-1], _ = lax.optimization_barrier((shares[-1], mark))
+            )(place, sharp, sharp_other, gain, *pieces, unit_keys, values, *near)
+            shares = finish(parts, residuals)
         kept = [jnp.where(section == step, share, old) for share, old in zip(shares, kept)]
 
     pieces = gather(kept)

time: 175 us -> 160 us (0.914)
  starting transfers between devices: 75.6 us -> 58.7 us
  waiting for transfers between devices: 63.4 us -> 68.6 us
  Pallas kernels: 31.3 us -> 27.8 us
    ppermute x62 -> x46, starting transfers between devices: 68.4 us -> 52.1 us  [flip(): return lambda x: lax.ppermute(x, 'seq', pairs)]
    ppermute x62 -> x46, waiting for transfers between devices: 41.3 us -> 50.6 us  [flip(): return lambda x: lax.ppermute(x, 'seq', pairs)]
    pallas_call x15 -> x8, Pallas kernels: 24.7 us -> 20.1 us  [the longest x2 13.4 us: keep(): kernel_call(functools.partial(body, config), [pltpu.VMEM(x.shape, BF16) f...]
    ppermute x8 -> x7, waiting for transfers between devices: 22.2 us -> 18 us  [up(): return lax.ppermute(x, 'section', [(source, target)])]
    another operation x0 -> x7, local copies, waits for them, and re-layouts: none -> 3.26 us
    slice x2 -> x0, local copies, waits for them, and re-layouts: 1.97 us -> none  [own_rows(): return [rows[g * piece:(g + 1) * piece] for g in range(groups)]]
    ppermute x8 -> x7, starting transfers between devices: 7.22 us -> 6.56 us  [up(): return lax.ppermute(x, 'section', [(source, target)])]
  transfers between devices with their start and end apart: 70 -> 53, of which waited for: 28 -> 29; matrix products, arithmetic and copies ran while one was open for 2% -> 0% of each run, Pallas kernels for 13% -> 6%
where the time goes in v4:
time: 160 us
  waiting for transfers between devices  68.6 us (43%)
  starting transfers between devices  58.7 us (37%)
  Pallas kernels  27.8 us (17%)
  local copies, waits for them, and re-layouts  3.28 us (2%)
    ppermute x46, starting transfers between devices, flip(): return lambda x: lax.ppermute(x, 'seq', pairs)  52.1 us
    ppermute x46, waiting for transfers between devices, flip(): return lambda x: lax.ppermute(x, 'seq', pairs)  50.6 us
    ppermute x7, waiting for transfers between devices, up(): return lax.ppermute(x, 'section', [(source, target)])  18 us
    pallas_call x2, Pallas kernels, keep(): kernel_call(functools.partial(body, config), [pltpu.VMEM(x.shape, BF16) f...  13.4 us
    ppermute x7, starting transfers between devices, up(): return lax.ppermute(x, 'section', [(source, target)])  6.56 us
    pallas_call x2, Pallas kernels, shards(): kernel_call(functools.partial(only_in([step])(section_kernel), config), p...  5.69 us
    pallas_call x1, Pallas kernels, project_memory(): kernel_call(functools.partial(memory_kernel, config), [sds((length, both)...  4.15 us
    another operation x7, local copies, waits for them, and re-layouts  3.26 us
  transfers between devices with their start and end apart: 53, of which 29 were waited for; matrix products, arithmetic and copies ran while one was open for 0% of the time, Pallas kernels for 6%

profile of v4, /device:TPU:25, one launch (start us, length us, event | category | flops | bytes accessed | tf_op | source)
XLA Modules:
  0.0 159.6 jit_solution(5862137240804725280)
XLA Ops:
  0.7 29.0 %conditional.2 = (bf16[32,4096]{1,0:T(8,128)(2,1)S(1)}, bf16[4096,512]{1,0:T(8,128)(2,1)}, bf16[4096,512]{1,0:T(8,128)(2,1)}, bf16[512,4096]{1,0:T(8,128)(2,1)},...) conditional(s32[]{:T(128)} %clamp.3, (s32[3]{0:T(128)S(1)}, ...), branch_computations={%region_0.1_spmd, %region_1.2_spmd, %region_2.3_spmd} | conditional | bytes 135528864 | solution.py:463
  2.0 6.4 %collective-permute-done.10 = bf16[4096,512]{1,0:T(8,128)(2,1)S(1)} collective-permute-done((bf16[4096,512]{1,0:T(8,128)(2,1)}, bf16[4096,512]{1,0:T(8,128)(2,1)S(1)}, u32[]{:S(2)}, u32[]{:S(2)}) %collective-permute-start.10) | collective-permute-done | bytes 4194336 | tf_op jit(solution)/shard_map/cond/branch_2_fun/ppermute | solution.py:341
  8.5 6.0 %collective-permute-done.11 = bf16[512,4096]{1,0:T(8,128)(2,1)S(1)} collective-permute-done((bf16[512,4096]{1,0:T(8,128)(2,1)}, bf16[512,4096]{1,0:T(8,128)(2,1)S(1)}, u32[]{:S(2)}, u32[]{:S(2)}) %collective-permute-start.11) | collective-permute-done | bytes 4194336 | tf_op jit(solution)/shard_map/cond/branch_2_fun/ppermute | solution.py:341
  14.5 6.0 %collective-permute-done.12 = bf16[4096,512]{1,0:T(8,128)(2,1)S(1)} collective-permute-done((bf16[4096,512]{1,0:T(8,128)(2,1)}, bf16[4096,512]{1,0:T(8,128)(2,1)S(1)}, u32[]{:S(2)}, u32[]{:S(2)}) %collective-permute-start.12) | collective-permute-done | bytes 4194336 | tf_op jit(solution)/shard_map/cond/branch_2_fun/ppermute | solution.py:341
  20.5 6.0 %collective-permute-done.9 = bf16[4096,512]{1,0:T(8,128)(2,1)S(1)} collective-permute-done((bf16[4096,512]{1,0:T(8,128)(2,1)}, bf16[4096,512]{1,0:T(8,128)(2,1)S(1)}, u32[]{:S(2)}, u32[]{:S(2)}) %collective-permute-start.9) | collective-permute-done | bytes 4194336 | tf_op jit(solution)/shard_map/cond/branch_2_fun/ppermute | solution.py:341
  31.7 36.4 %conditional.3 = (bf16[128,1024]{1,0:T(8,128)(2,1)}, bf16[128,1024]{1,0:T(8,128)(2,1)}, bf16[16,4096]{1,0:T(8,128)(2,1)S(1)}, bf16[16,4096]{1,0:T(8,128)(2,1)S(1)}) conditional(s32[]{:T(128)} %convert_element_type.3, (s32[]{:T(128)}, bf16[32,4096]{1,0:T(8,128)(2,1)S(1)}, s32[3]{0:T(128)S(1)}, bf16[4096,512]{1,0:T(8,128)(2,1)}, ...), branch_computations={%region_3.4_spmd, %region_4.5_spmd} | conditional | flops 131073 | bytes 58720760 | solution.py:526
  33.6 16.3 %collective-permute-done.23 = bf16[32,4096]{1,0:T(8,128)(2,1)S(1)} collective-permute-done((bf16[32,4096]{1,0:T(8,128)(2,1)S(1)}, bf16[32,4096]{1,0:T(8,128)(2,1)S(1)}, u32[]{:S(2)}, u32[]{:S(2)}) %collective-permute-start.23) | collective-permute-done | bytes 262176 | tf_op jit(solution)/shard_map/cond/branch_0_fun/ppermute | solution.py:344
  50.0 1.9 %collective-permute-start.24 = (bf16[32,4096]{1,0:T(8,128)(2,1)S(1)}, bf16[32,4096]{1,0:T(8,128)(2,1)S(1)}, u32[]{:S(2)}, u32[]{:S(2)}) collective-permute-start(bf16[32,4096]{1,0:T(8,128)(2,1)S(1)} %broadcast_select_fusion.refs_0_), channel_id=1, source_target_pairs={{0,2},{1,3},{2,0},{3,1},{4,6},{5,7},{6,4},{7,5},{8,10},{9,11},{10,... | collective-permute-start | bytes 786440 | tf_op jit(solution)/shard_map/cond/branch_0_fun/ppermute | solution.py:341
  53.4 7.0 %branch_0_fun.10 = (bf16[4096,512]{1,0:T(8,128)(2,1)S(1)}, bf16[4096,512]{1,0:T(8,128)(2,1)S(1)}, bf16[4096,512]{1,0:T(8,128)(2,1)S(1)}, bf16[4096,512]{1,0:T(8,128)(2,1)S(1)}, bf16[8,128]{1,0:T(8,128)(2,1)}) custom-call(s32[3]{0:T(128)S(1)} %get-tuple-element.131.place, bf16[4096,512]{1,0:T(8,128)(2,1)} %get-tuple-element.132.refs_0_, ...), custom_call_target="tpu_custom_call" | custom-call | bytes 33554432 | tf_op jit(solution)/shard_map/cond/branch_0_fun/pallas_call | solution.py:476
  60.4 3.3 %collective-permute-done.26.refs_3_ = bf16[32,4096]{1,0:T(8,128)(2,1)S(1)} collective-permute-done((bf16[32,4096]{1,0:T(8,128)(2,1)S(1)}, bf16[32,4096]{1,0:T(8,128)(2,1)S(1)}, u32[]{:S(2)}, u32[]{:S(2)}) %collective-permute-start.26) | collective-permute-done | bytes 262176 | tf_op jit(solution)/shard_map/cond/branch_0_fun/ppermute | solution.py:341
  63.7 4.1 %branch_0_fun.11 = (bf16[128,1024]{1,0:T(8,128)(2,1)}, bf16[128,1024]{1,0:T(8,128)(2,1)}) custom-call(s32[3]{0:T(128)S(1)} %get-tuple-element.131.place, f32[1,4096]{1,0:T(1,128)S(1)} %get-tuple-element.128.gain, bf16[32,4096]{1,0:T(8,128)(2,1)S(1)} %broadcast_select_fusion.refs_0_, bf16[32,4096]{1,0:T(8,128)(2,1)S(1)} %collective-permute-done.24.refs_1_, ...), custom_call_target="tpu_custom_call" | custom-call | tf_op jit(solution)/shard_map/cond/branch_0_fun/pallas_call | solution.py:486
  68.1 6.4 %shard_map.93 = (bf16[4096,512]{1,0:T(8,128)(2,1)S(1)}, bf16[4096,512]{1,0:T(8,128)(2,1)S(1)}, bf16[512,4096]{1,0:T(8,128)(2,1)S(1)}, bf16[512,4096]{1,0:T(8,128)(2,1)S(1)}, bf16[8,128]{1,0:T(8,128)(2,1)S(1)}) custom-call(s32[3]{0:T(128)S(1)} %pad_add_fusion.place, bf16[4096,512]{1,0:T(8,128)(2,1)} %bitcast.14, ...), custom_call_target="tpu_custom_call" | custom-call | bytes 33554432 | tf_op jit(solution)/shard_map/pallas_call | solution.py:476
  82.1 1.9 %collective-permute-done.31.refs_5_ = bf16[16,4096]{1,0:T(8,128)(2,1)S(1)} collective-permute-done((bf16[16,4096]{1,0:T(8,128)(2,1)S(1)}, bf16[16,4096]{1,0:T(8,128)(2,1)S(1)}, u32[]{:S(2)}, u32[]{:S(2)}) %collective-permute-start.31) | collective-permute-done | bytes 131104 | tf_op jit(solution)/shard_map/ppermute | solution.py:341
  84.7 3.0 %collective-permute-done.35.refs_9_ = bf16[16,4096]{1,0:T(8,128)(2,1)S(1)} collective-permute-done((bf16[16,4096]{1,0:T(8,128)(2,1)S(1)}, bf16[16,4096]{1,0:T(8,128)(2,1)S(1)}, u32[]{:S(2)}, u32[]{:S(2)}) %collective-permute-start.35) | collective-permute-done | bytes 131104 | tf_op jit(solution)/shard_map/ppermute | solution.py:341
  88.8 1.9 %collective-permute-start.37 = (bf16[16,4096]{1,0:T(8,128)(2,1)S(1)}, bf16[16,4096]{1,0:T(8,128)(2,1)S(1)}, u32[]{:S(2)}, u32[]{:S(2)}) collective-permute-start(bf16[16,4096]{1,0:T(8,128)(2,1)S(1)} %get-tuple-element.229), channel_id=1, source_target_pairs={{0,6},{1,7},{2,4},{3,5},{4,2},{5,3},{6,0},{7,1},{8,14},{9,15},{10,... | collective-permute-start | bytes 393224 | tf_op jit(solution)/shard_map/ppermute | solution.py:341
  91.5 1.9 %collective-permute-start.41 = (bf16[16,4096]{1,0:T(8,128)(2,1)S(1)}, bf16[16,4096]{1,0:T(8,128)(2,1)S(1)}, u32[]{:S(2)}, u32[]{:S(2)}) collective-permute-start(bf16[16,4096]{1,0:T(8,128)(2,1)S(1)} %get-tuple-element.233), channel_id=1, source_target_pairs={{0,6},{1,7},{2,4},{3,5},{4,2},{5,3},{6,0},{7,1},{8,14},{9,15},{10,... | collective-permute-start | bytes 393224 | tf_op jit(solution)/shard_map/ppermute | solution.py:341
  98.6 2.9 %collective-permute-done.42.refs_3_ = bf16[16,4096]{1,0:T(8,128)(2,1)S(1)} collective-permute-done((bf16[16,4096]{1,0:T(8,128)(2,1)S(1)}, bf16[16,4096]{1,0:T(8,128)(2,1)S(1)}, u32[]{:S(2)}, u32[]{:S(2)}) %collective-permute-start.42) | collective-permute-done | bytes 131104 | tf_op jit(solution)/shard_map/ppermute | solution.py:341
  108.4 2.1 %collective-permute-start.50 = (bf16[16,4096]{1,0:T(8,128)(2,1)S(1)}, bf16[16,4096]{1,0:T(8,128)(2,1)S(1)}, u32[]{:S(2)}, u32[]{:S(2)}) collective-permute-start(bf16[16,4096]{1,0:T(8,128)(2,1)S(1)} %collective-permute-done.44.refs_4_.refs_0_), channel_id=1, source_target_pairs={{0,6},{1,7},{2,4},{3,5},{4,2},{5,3},{6,0},{7,1},{8,14},{9,15},{10,... | collective-permute-start | bytes 393224 | tf_op jit(solution)/shard_map/ppermute | solution.py:341
  113.1 4.6 %shard_map.98 = (bf16[16,4096]{1,0:T(8,128)(2,1)S(1)}, bf16[16,4096]{1,0:T(8,128)(2,1)S(1)}, bf16[16,4096]{1,0:T(8,128)(2,1)S(1)}, bf16[16,4096]{1,0:T(8,128)(2,...) custom-call(s32[3]{0:T(128)S(1)} %pad_add_fusion.place, ...), custom_call_target="tpu_custom_call" | custom-call | tf_op jit(solution)/shard_map/pallas_call | solution.py:542
  117.7 2.4 %collective-permute-start.51 = (bf16[16,4096]{1,0:T(8,128)(2,1)S(1)}, bf16[16,4096]{1,0:T(8,128)(2,1)S(1)}, u32[]{:S(2)}, u32[]{:S(2)}) collective-permute-start(bf16[16,4096]{1,0:T(8,128)(2,1)S(1)} %get-tuple-element.237), channel_id=1, source_target_pairs={{0,6},{1,7},{2,4},{3,5},{4,2},{5,3},{6,0},{7,1},{8,14},{9,15},{10,... | collective-permute-start | bytes 393224 | tf_op jit(solution)/shard_map/ppermute | solution.py:341
  120.7 2.0 %collective-permute-start.54 = (bf16[16,4096]{1,0:T(8,128)(2,1)S(1)}, bf16[16,4096]{1,0:T(8,128)(2,1)S(1)}, u32[]{:S(2)}, u32[]{:S(2)}) collective-permute-start(bf16[16,4096]{1,0:T(8,128)(2,1)S(1)} %get-tuple-element.241), channel_id=1, source_target_pairs={{0,6},{1,7},{2,4},{3,5},{4,2},{5,3},{6,0},{7,1},{8,14},{9,15},{10,... | collective-permute-start | bytes 393224 | tf_op jit(solution)/shard_map/ppermute | solution.py:341
  136.4 14.6 %collective-permute-start.63 = (bf16[16,4096]{1,0:T(8,128)(2,1)S(1)}, bf16[16,4096]{1,0:T(8,128)(2,1)S(1)}, u32[]{:S(2)}, u32[]{:S(2)}) collective-permute-start(bf16[16,4096]{1,0:T(8,128)(2,1)S(1)} %get-tuple-element.249.refs_0_), channel_id=1, source_target_pairs={{0,1},{1,0},{2,3},{3,2},{4,5},{5,4},{6,7},{7,6},{8,9},{9,8},{10,11... | collective-permute-start | bytes 393224 | tf_op jit(solution)/shard_map/ppermute | solution.py:341
  153.9 1.8 %collective-permute-start.67 = (bf16[16,4096]{1,0:T(8,128)(2,1)S(1)}, bf16[16,4096]{1,0:T(8,128)(2,1)S(1)}, u32[]{:S(2)}, u32[]{:S(2)}) collective-permute-start(bf16[16,4096]{1,0:T(8,128)(2,1)S(1)} %collective-permute-done.59.refs_4_), channel_id=1, source_target_pairs={{0,1},{1,0},{2,3},{3,2},{4,5},{5,4},{6,7},{7,6},{8,9},{9,8},{10,11... | collective-permute-start | bytes 393224 | tf_op jit(solution)/shard_map/ppermute | solution.py:341
  157.6 2.0 %shard_map.101 = bf16[2,128,4096]{2,1,0:T(8,128)(2,1)} custom-call(s32[3]{0:T(128)S(1)} %pad_add_fusion.place, bf16[16,4096]{1,0:T(8,128)(2,1)S(1)} %get-tuple-element.249.refs_0_, bf16[16,4096]{1,0:T(8,128)(2,1)S(1)} %get-tuple-element.248.refs_1_, bf16[16,4096]{1,0:T(8,128)(2,1)S(1)} %collective-permute-done.57.refs_2_, ...), custom_call_target="tpu_custom_call" | custom-call | tf_op jit(solution)/shard_map/pallas_call | solution.py:554
  (118 shorter events, 54.5 us)
Async XLA Ops:
  0.7 7.7 %collective-permute-start.10 = (bf16[4096,512]{1,0:T(8,128)(2,1)}, bf16[4096,512]{1,0:T(8,128)(2,1)S(1)}, u32[]{:S(2)}, u32[]{:S(2)}) collective-permute-start(bf16[4096,512]{1,0:T(8,128)(2,1)} %get-tuple-element.124), channel_id=1, source_target_pairs={{0,1},{1,0},{2,3},{3,2},{4,5},{5,4},{6,7},{7,6},{8,9},{9,8},{10,11... | collective-permute-start | bytes 12582920 | tf_op jit(solution)/shard_map/cond/branch_2_fun/ppermute | solution.py:341
  1.5 13.0 %collective-permute-start.11 = (bf16[512,4096]{1,0:T(8,128)(2,1)}, bf16[512,4096]{1,0:T(8,128)(2,1)S(1)}, u32[]{:S(2)}, u32[]{:S(2)}) collective-permute-start(bf16[512,4096]{1,0:T(8,128)(2,1)} %get-tuple-element.125), channel_id=1, source_target_pairs={{0,1},{1,0},{2,3},{3,2},{4,5},{5,4},{6,7},{7,6},{8,9},{9,8},{10,11... | collective-permute-start | bytes 12582920 | tf_op jit(solution)/shard_map/cond/branch_2_fun/ppermute | solution.py:341
  1.5 18.9 %collective-permute-start.12 = (bf16[4096,512]{1,0:T(8,128)(2,1)}, bf16[4096,512]{1,0:T(8,128)(2,1)S(1)}, u32[]{:S(2)}, u32[]{:S(2)}) collective-permute-start(bf16[4096,512]{1,0:T(8,128)(2,1)} %get-tuple-element.126), channel_id=1, source_target_pairs={{0,1},{1,0},{2,3},{3,2},{4,5},{5,4},{6,7},{7,6},{8,9},{9,8},{10,11... | collective-permute-start | bytes 12582920 | tf_op jit(solution)/shard_map/cond/branch_2_fun/ppermute | solution.py:341
  2.0 24.5 %collective-permute-start.9 = (bf16[4096,512]{1,0:T(8,128)(2,1)}, bf16[4096,512]{1,0:T(8,128)(2,1)S(1)}, u32[]{:S(2)}, u32[]{:S(2)}) collective-permute-start(bf16[4096,512]{1,0:T(8,128)(2,1)} %get-tuple-element.123), channel_id=1, source_target_pairs={{0,1},{1,0},{2,3},{3,2},{4,5},{5,4},{6,7},{7,6},{8,9},{9,8},{10,11... | collective-permute-start | bytes 12582920 | tf_op jit(solution)/shard_map/cond/branch_2_fun/ppermute | solution.py:341
  32.3 17.6 %collective-permute-start.23 = (bf16[32,4096]{1,0:T(8,128)(2,1)S(1)}, bf16[32,4096]{1,0:T(8,128)(2,1)S(1)}, u32[]{:S(2)}, u32[]{:S(2)}) collective-permute-start(bf16[32,4096]{1,0:T(8,128)(2,1)S(1)} %get-tuple-element.130), channel_id=1, source_target_pairs={{0,24},{1,25},{2,26},{3,27},{4,28},{5,29},{6,30},{7,31}} | collective-permute-start | bytes 786440 | tf_op jit(solution)/shard_map/cond/branch_0_fun/ppermute | solution.py:344
  50.0 10.4 %collective-permute-start.24 = (bf16[32,4096]{1,0:T(8,128)(2,1)S(1)}, bf16[32,4096]{1,0:T(8,128)(2,1)S(1)}, u32[]{:S(2)}, u32[]{:S(2)}) collective-permute-start(bf16[32,4096]{1,0:T(8,128)(2,1)S(1)} %broadcast_select_fusion.refs_0_), channel_id=1, source_target_pairs={{0,2},{1,3},{2,0},{3,1},{4,6},{5,7},{6,4},{7,5},{8,10},{9,11},{10,... | collective-permute-start | bytes 786440 | tf_op jit(solution)/shard_map/cond/branch_0_fun/ppermute | solution.py:341
  51.9 8.5 %collective-permute-start.25 = (bf16[32,4096]{1,0:T(8,128)(2,1)S(1)}, bf16[32,4096]{1,0:T(8,128)(2,1)S(1)}, u32[]{:S(2)}, u32[]{:S(2)}) collective-permute-start(bf16[32,4096]{1,0:T(8,128)(2,1)S(1)} %broadcast_select_fusion.refs_0_), channel_id=1, source_target_pairs={{0,4},{1,5},{2,6},{3,7},{4,0},{5,1},{6,2},{7,3},{8,12},{9,13},{10,... | collective-permute-start | bytes 786440 | tf_op jit(solution)/shard_map/cond/branch_0_fun/ppermute | solution.py:341
  52.3 11.4 %collective-permute-start.26 = (bf16[32,4096]{1,0:T(8,128)(2,1)S(1)}, bf16[32,4096]{1,0:T(8,128)(2,1)S(1)}, u32[]{:S(2)}, u32[]{:S(2)}) collective-permute-start(bf16[32,4096]{1,0:T(8,128)(2,1)S(1)} %broadcast_select_fusion.refs_0_), channel_id=1, source_target_pairs={{0,6},{1,7},{2,4},{3,5},{4,2},{5,3},{6,0},{7,1},{8,14},{9,15},{10,... | collective-permute-start | bytes 786440 | tf_op jit(solution)/shard_map/cond/branch_0_fun/ppermute | solution.py:341
  78.8 5.9 %collective-permute-start.33 = (bf16[16,4096]{1,0:T(8,128)(2,1)S(1)}, bf16[16,4096]{1,0:T(8,128)(2,1)S(1)}, u32[]{:S(2)}, u32[]{:S(2)}) collective-permute-start(bf16[16,4096]{1,0:T(8,128)(2,1)S(1)} %collective-permute-done.29.refs_3_.refs_0_), channel_id=1, source_target_pairs={{0,4},{1,5},{2,6},{3,7},{4,0},{5,1},{6,2},{7,3},{8,12},{9,13},{10,... | collective-permute-start | bytes 393224 | tf_op jit(solution)/shard_map/ppermute | solution.py:341
  79.8 7.9 %collective-permute-start.35 = (bf16[16,4096]{1,0:T(8,128)(2,1)S(1)}, bf16[16,4096]{1,0:T(8,128)(2,1)S(1)}, u32[]{:S(2)}, u32[]{:S(2)}) collective-permute-start(bf16[16,4096]{1,0:T(8,128)(2,1)S(1)} %collective-permute-done.29.refs_3_.refs_0_), channel_id=1, source_target_pairs={{0,6},{1,7},{2,4},{3,5},{4,2},{5,3},{6,0},{7,1},{8,14},{9,15},{10,... | collective-permute-start | bytes 393224 | tf_op jit(solution)/shard_map/ppermute | solution.py:341
  91.5 7.1 %collective-permute-start.41 = (bf16[16,4096]{1,0:T(8,128)(2,1)S(1)}, bf16[16,4096]{1,0:T(8,128)(2,1)S(1)}, u32[]{:S(2)}, u32[]{:S(2)}) collective-permute-start(bf16[16,4096]{1,0:T(8,128)(2,1)S(1)} %get-tuple-element.233), channel_id=1, source_target_pairs={{0,6},{1,7},{2,4},{3,5},{4,2},{5,3},{6,0},{7,1},{8,14},{9,15},{10,... | collective-permute-start | bytes 393224 | tf_op jit(solution)/shard_map/ppermute | solution.py:341
  93.3 8.2 %collective-permute-start.42 = (bf16[16,4096]{1,0:T(8,128)(2,1)S(1)}, bf16[16,4096]{1,0:T(8,128)(2,1)S(1)}, u32[]{:S(2)}, u32[]{:S(2)}) collective-permute-start(bf16[16,4096]{1,0:T(8,128)(2,1)S(1)} %get-tuple-element.234), channel_id=1, source_target_pairs={{0,4},{1,5},{2,6},{3,7},{4,0},{5,1},{6,2},{7,3},{8,12},{9,13},{10,... | collective-permute-start | bytes 393224 | tf_op jit(solution)/shard_map/ppermute | solution.py:341
  93.6 7.9 %collective-permute-start.43 = (bf16[16,4096]{1,0:T(8,128)(2,1)S(1)}, bf16[16,4096]{1,0:T(8,128)(2,1)S(1)}, u32[]{:S(2)}, u32[]{:S(2)}) collective-permute-start(bf16[16,4096]{1,0:T(8,128)(2,1)S(1)} %get-tuple-element.235), channel_id=1, source_target_pairs={{0,2},{1,3},{2,0},{3,1},{4,6},{5,7},{6,4},{7,5},{8,10},{9,11},{10,... | collective-permute-start | bytes 393224 | tf_op jit(solution)/shard_map/ppermute | solution.py:341
  95.6 7.9 %collective-permute-start.40 = (bf16[16,4096]{1,0:T(8,128)(2,1)S(1)}, bf16[16,4096]{1,0:T(8,128)(2,1)S(1)}, u32[]{:S(2)}, u32[]{:S(2)}) collective-permute-start(bf16[16,4096]{1,0:T(8,128)(2,1)S(1)} %shard_map.96), channel_id=1, source_target_pairs={{16,24},{17,25},{18,26},{19,27},{20,28},{21,29},{22,30},{23,31}} | collective-permute-start | bytes 393224 | tf_op jit(solution)/shard_map/ppermute | solution.py:344
  103.7 6.8 %collective-permute-start.47 = (bf16[16,4096]{1,0:T(8,128)(2,1)S(1)}, bf16[16,4096]{1,0:T(8,128)(2,1)S(1)}, u32[]{:S(2)}, u32[]{:S(2)}) collective-permute-start(bf16[16,4096]{1,0:T(8,128)(2,1)S(1)} %collective-permute-done.40.refs_3_.refs_0_), channel_id=1, source_target_pairs={{0,4},{1,5},{2,6},{3,7},{4,0},{5,1},{6,2},{7,3},{8,12},{9,13},{10,... | collective-permute-start | bytes 393224 | tf_op jit(solution)/shard_map/ppermute | solution.py:341
  104.6 5.9 %collective-permute-start.49 = (bf16[16,4096]{1,0:T(8,128)(2,1)S(1)}, bf16[16,4096]{1,0:T(8,128)(2,1)S(1)}, u32[]{:S(2)}, u32[]{:S(2)}) collective-permute-start(bf16[16,4096]{1,0:T(8,128)(2,1)S(1)} %collective-permute-done.40.refs_3_.refs_0_), channel_id=1, source_target_pairs={{0,6},{1,7},{2,4},{3,5},{4,2},{5,3},{6,0},{7,1},{8,14},{9,15},{10,... | collective-permute-start | bytes 393224 | tf_op jit(solution)/shard_map/ppermute | solution.py:341
  117.7 6.1 %collective-permute-start.51 = (bf16[16,4096]{1,0:T(8,128)(2,1)S(1)}, bf16[16,4096]{1,0:T(8,128)(2,1)S(1)}, u32[]{:S(2)}, u32[]{:S(2)}) collective-permute-start(bf16[16,4096]{1,0:T(8,128)(2,1)S(1)} %get-tuple-element.237), channel_id=1, source_target_pairs={{0,6},{1,7},{2,4},{3,5},{4,2},{5,3},{6,0},{7,1},{8,14},{9,15},{10,... | collective-permute-start | bytes 393224 | tf_op jit(solution)/shard_map/ppermute | solution.py:341
  120.7 5.9 %collective-permute-start.54 = (bf16[16,4096]{1,0:T(8,128)(2,1)S(1)}, bf16[16,4096]{1,0:T(8,128)(2,1)S(1)}, u32[]{:S(2)}, u32[]{:S(2)}) collective-permute-start(bf16[16,4096]{1,0:T(8,128)(2,1)S(1)} %get-tuple-element.241), channel_id=1, source_target_pairs={{0,6},{1,7},{2,4},{3,5},{4,2},{5,3},{6,0},{7,1},{8,14},{9,15},{10,... | collective-permute-start | bytes 393224 | tf_op jit(solution)/shard_map/ppermute | solution.py:341
  129.2 7.2 %collective-permute-start.58 = (bf16[16,4096]{1,0:T(8,128)(2,1)S(1)}, bf16[16,4096]{1,0:T(8,128)(2,1)S(1)}, u32[]{:S(2)}, u32[]{:S(2)}) collective-permute-start(bf16[16,4096]{1,0:T(8,128)(2,1)S(1)} %get-tuple-element.248.refs_1_), channel_id=1, source_target_pairs={{0,2},{1,3},{2,0},{3,1},{4,6},{5,7},{6,4},{7,5},{8,10},{9,11},{10,... | collective-permute-start | bytes 393224 | tf_op jit(solution)/shard_map/ppermute | solution.py:341
  130.1 20.9 %collective-permute-start.59 = (bf16[16,4096]{1,0:T(8,128)(2,1)S(1)}, bf16[16,4096]{1,0:T(8,128)(2,1)S(1)}, u32[]{:S(2)}, u32[]{:S(2)}) collective-permute-start(bf16[16,4096]{1,0:T(8,128)(2,1)S(1)} %get-tuple-element.249.refs_0_), channel_id=1, source_target_pairs={{0,4},{1,5},{2,6},{3,7},{4,0},{5,1},{6,2},{7,3},{8,12},{9,13},{10,... | collective-permute-start | bytes 393224 | tf_op jit(solution)/shard_map/ppermute | solution.py:341
  130.8 20.3 %collective-permute-start.60 = (bf16[16,4096]{1,0:T(8,128)(2,1)S(1)}, bf16[16,4096]{1,0:T(8,128)(2,1)S(1)}, u32[]{:S(2)}, u32[]{:S(2)}) collective-permute-start(bf16[16,4096]{1,0:T(8,128)(2,1)S(1)} %get-tuple-element.248.refs_1_), channel_id=1, source_target_pairs={{0,4},{1,5},{2,6},{3,7},{4,0},{5,1},{6,2},{7,3},{8,12},{9,13},{10,... | collective-permute-start | bytes 393224 | tf_op jit(solution)/shard_map/ppermute | solution.py:341
  131.6 20.8 %collective-permute-start.61 = (bf16[16,4096]{1,0:T(8,128)(2,1)S(1)}, bf16[16,4096]{1,0:T(8,128)(2,1)S(1)}, u32[]{:S(2)}, u32[]{:S(2)}) collective-permute-start(bf16[16,4096]{1,0:T(8,128)(2,1)S(1)} %get-tuple-element.249.refs_0_), channel_id=1, source_target_pairs={{0,6},{1,7},{2,4},{3,5},{4,2},{5,3},{6,0},{7,1},{8,14},{9,15},{10,... | collective-permute-start | bytes 393224 | tf_op jit(solution)/shard_map/ppermute | solution.py:341
  133.6 20.4 %collective-permute-start.62 = (bf16[16,4096]{1,0:T(8,128)(2,1)S(1)}, bf16[16,4096]{1,0:T(8,128)(2,1)S(1)}, u32[]{:S(2)}, u32[]{:S(2)}) collective-permute-start(bf16[16,4096]{1,0:T(8,128)(2,1)S(1)} %get-tuple-element.248.refs_1_), channel_id=1, source_target_pairs={{0,6},{1,7},{2,4},{3,5},{4,2},{5,3},{6,0},{7,1},{8,14},{9,15},{10,... | collective-permute-start | bytes 393224 | tf_op jit(solution)/shard_map/ppermute | solution.py:341
  136.4 19.4 %collective-permute-start.63 = (bf16[16,4096]{1,0:T(8,128)(2,1)S(1)}, bf16[16,4096]{1,0:T(8,128)(2,1)S(1)}, u32[]{:S(2)}, u32[]{:S(2)}) collective-permute-start(bf16[16,4096]{1,0:T(8,128)(2,1)S(1)} %get-tuple-element.249.refs_0_), channel_id=1, source_target_pairs={{0,1},{1,0},{2,3},{3,2},{4,5},{5,4},{6,7},{7,6},{8,9},{9,8},{10,11... | collective-permute-start | bytes 393224 | tf_op jit(solution)/shard_map/ppermute | solution.py:341
  (35 other events, 209.9 us)

commit v5 on v4

--- a/solution.py
+++ b/solution.py
@@ -111,7 +111,7 @@
         scales = []
         for i in range(per):
             index = group * per + i
-            scales.append(sharps[index // each][index % each])
+            scales.append(sharps[index // each][index % each] * (head ** -0.5))
         mixture[:, lanes] = attend(uq[:, lanes], uk[:, lanes], v[:, lanes], scales, head)
 
 
@@ -351,7 +351,7 @@
     )
     gain = layer_rescale_weights
     last_gain = last_rescale_weights.reshape(1, width)
-    sharp = logit_sharpness[0] * (head ** -0.5)
+    sharp = logit_sharpness[0]
     sharp_other = to_core(sharp)
     stay = pltpu.with_memory_space_constraint
 
@@ -370,10 +370,19 @@
         return pltpu.SemaphoreType.DMA((n,))
 
     def gather(shares):
-        by_group = []
-        for share in shares:
-            others = {j: to_chip[j](share) for j in reversed(range(1, blocks))}
-            by_group.append([share] + [others[j] for j in range(1, blocks)])
+        if blocks == 4 and len(shares) == 2:
+            first, second = shares
+            x_first, y_second = to_chip[1](first), to_chip[2](second)
+            y_first, x_second = to_chip[2](first), to_chip[1](second)
+            by_group = [
+                [first, x_first, y_first, to_chip[2](x_first)],
+                [second, x_second, y_second, to_chip[1](y_second)],
+            ]
+        else:
+            by_group = []
+            for share in shares:
+                others = {j: to_chip[j](share) for j in reversed(range(1, blocks))}
+                by_group.append([share] + [others[j] for j in range(1, blocks)])
         return [group[j] for j in range(blocks) for group in by_group]
 
     def finish(parts, residuals):

time: 160 us -> 157 us (0.981)
  starting transfers between devices: 58.7 us -> 55.1 us
  waiting for transfers between devices: 68.6 us -> 70.2 us
    ppermute x7, waiting for transfers between devices: 18 us -> 22.9 us  [up(): return lax.ppermute(x, 'section', [(source, target)])]
    ppermute x46, starting transfers between devices: 52.1 us -> 48.5 us  [flip(): return lambda x: lax.ppermute(x, 'seq', pairs)]
    ppermute x46, waiting for transfers between devices: 50.6 us -> 47.3 us  [flip(): return lambda x: lax.ppermute(x, 'seq', pairs)]
where the time goes in v5:
time: 157 us
  waiting for transfers between devices  70.2 us (45%)
  starting transfers between devices  55.1 us (35%)
  Pallas kernels  27.8 us (18%)
  local copies, waits for them, and re-layouts  3.27 us (2%)
    ppermute x46, starting transfers between devices, flip(): return lambda x: lax.ppermute(x, 'seq', pairs)  48.5 us
    ppermute x46, waiting for transfers between devices, flip(): return lambda x: lax.ppermute(x, 'seq', pairs)  47.3 us
    ppermute x7, waiting for transfers between devices, up(): return lax.ppermute(x, 'section', [(source, target)])  22.9 us
    pallas_call x2, Pallas kernels, keep(): kernel_call(functools.partial(body, config), [pltpu.VMEM(x.shape, BF16) f...  13.4 us
    ppermute x7, starting transfers between devices, up(): return lax.ppermute(x, 'section', [(source, target)])  6.57 us
    pallas_call x2, Pallas kernels, shards(): kernel_call(functools.partial(only_in([step])(section_kernel), config), p...  5.69 us
    pallas_call x1, Pallas kernels, project_memory(): kernel_call(functools.partial(memory_kernel, config), [sds((length, both)...  4.16 us
    another operation x7, local copies, waits for them, and re-layouts  3.24 us
  transfers between devices with their start and end apart: 53, of which 29 were waited for; matrix products, arithmetic and copies ran while one was open for 0% of the time, Pallas kernels for 6%

profile of v5, /device:TPU:25, one launch (start us, length us, event | category | flops | bytes accessed | tf_op | source)
XLA Modules:
  0.0 157.0 jit_solution(17152728166311803949)
XLA Ops:
  0.1 29.0 %conditional.2 = (bf16[32,4096]{1,0:T(8,128)(2,1)S(1)}, bf16[4096,512]{1,0:T(8,128)(2,1)}, bf16[4096,512]{1,0:T(8,128)(2,1)}, bf16[512,4096]{1,0:T(8,128)(2,1)},...) conditional(s32[]{:T(128)} %clamp.3, (s32[3]{0:T(128)S(1)}, ...), branch_computations={%region_0.1_spmd, %region_1.2_spmd, %region_2.3_spmd} | conditional | bytes 135528864 | solution.py:472
  1.4 6.4 %collective-permute-done.10 = bf16[4096,512]{1,0:T(8,128)(2,1)S(1)} collective-permute-done((bf16[4096,512]{1,0:T(8,128)(2,1)}, bf16[4096,512]{1,0:T(8,128)(2,1)S(1)}, u32[]{:S(2)}, u32[]{:S(2)}) %collective-permute-start.10) | collective-permute-done | bytes 4194336 | tf_op jit(solution)/shard_map/cond/branch_2_fun/ppermute | solution.py:341
  7.8 6.0 %collective-permute-done.11 = bf16[512,4096]{1,0:T(8,128)(2,1)S(1)} collective-permute-done((bf16[512,4096]{1,0:T(8,128)(2,1)}, bf16[512,4096]{1,0:T(8,128)(2,1)S(1)}, u32[]{:S(2)}, u32[]{:S(2)}) %collective-permute-start.11) | collective-permute-done | bytes 4194336 | tf_op jit(solution)/shard_map/cond/branch_2_fun/ppermute | solution.py:341
  13.8 6.0 %collective-permute-done.12 = bf16[4096,512]{1,0:T(8,128)(2,1)S(1)} collective-permute-done((bf16[4096,512]{1,0:T(8,128)(2,1)}, bf16[4096,512]{1,0:T(8,128)(2,1)S(1)}, u32[]{:S(2)}, u32[]{:S(2)}) %collective-permute-start.12) | collective-permute-done | bytes 4194336 | tf_op jit(solution)/shard_map/cond/branch_2_fun/ppermute | solution.py:341
  19.8 6.0 %collective-permute-done.9 = bf16[4096,512]{1,0:T(8,128)(2,1)S(1)} collective-permute-done((bf16[4096,512]{1,0:T(8,128)(2,1)}, bf16[4096,512]{1,0:T(8,128)(2,1)S(1)}, u32[]{:S(2)}, u32[]{:S(2)}) %collective-permute-start.9) | collective-permute-done | bytes 4194336 | tf_op jit(solution)/shard_map/cond/branch_2_fun/ppermute | solution.py:341
  31.1 36.4 %conditional.3 = (bf16[128,1024]{1,0:T(8,128)(2,1)}, bf16[128,1024]{1,0:T(8,128)(2,1)}, bf16[16,4096]{1,0:T(8,128)(2,1)S(1)}, bf16[16,4096]{1,0:T(8,128)(2,1)S(1)}) conditional(s32[]{:T(128)} %convert_element_type.3, (s32[]{:T(128)}, bf16[32,4096]{1,0:T(8,128)(2,1)S(1)}, s32[3]{0:T(128)S(1)}, bf16[4096,512]{1,0:T(8,128)(2,1)}, ...), branch_computations={%region_3.4_spmd, %region_4.5_spmd} | conditional | flops 131073 | bytes 58720760 | solution.py:535
  33.1 16.2 %collective-permute-done.23 = bf16[32,4096]{1,0:T(8,128)(2,1)S(1)} collective-permute-done((bf16[32,4096]{1,0:T(8,128)(2,1)S(1)}, bf16[32,4096]{1,0:T(8,128)(2,1)S(1)}, u32[]{:S(2)}, u32[]{:S(2)}) %collective-permute-start.23) | collective-permute-done | bytes 262176 | tf_op jit(solution)/shard_map/cond/branch_0_fun/ppermute | solution.py:344
  49.4 1.9 %collective-permute-start.24 = (bf16[32,4096]{1,0:T(8,128)(2,1)S(1)}, bf16[32,4096]{1,0:T(8,128)(2,1)S(1)}, u32[]{:S(2)}, u32[]{:S(2)}) collective-permute-start(bf16[32,4096]{1,0:T(8,128)(2,1)S(1)} %broadcast_select_fusion.refs_0_), channel_id=1, source_target_pairs={{0,2},{1,3},{2,0},{3,1},{4,6},{5,7},{6,4},{7,5},{8,10},{9,11},{10,... | collective-permute-start | bytes 786440 | tf_op jit(solution)/shard_map/cond/branch_0_fun/ppermute | solution.py:341
  52.8 7.0 %branch_0_fun.10 = (bf16[4096,512]{1,0:T(8,128)(2,1)S(1)}, bf16[4096,512]{1,0:T(8,128)(2,1)S(1)}, bf16[4096,512]{1,0:T(8,128)(2,1)S(1)}, bf16[4096,512]{1,0:T(8,128)(2,1)S(1)}, bf16[8,128]{1,0:T(8,128)(2,1)}) custom-call(s32[3]{0:T(128)S(1)} %get-tuple-element.131.place, bf16[4096,512]{1,0:T(8,128)(2,1)} %get-tuple-element.132.refs_0_, ...), custom_call_target="tpu_custom_call" | custom-call | bytes 33554432 | tf_op jit(solution)/shard_map/cond/branch_0_fun/pallas_call | solution.py:485
  59.8 3.3 %collective-permute-done.26.refs_3_ = bf16[32,4096]{1,0:T(8,128)(2,1)S(1)} collective-permute-done((bf16[32,4096]{1,0:T(8,128)(2,1)S(1)}, bf16[32,4096]{1,0:T(8,128)(2,1)S(1)}, u32[]{:S(2)}, u32[]{:S(2)}) %collective-permute-start.26) | collective-permute-done | bytes 262176 | tf_op jit(solution)/shard_map/cond/branch_0_fun/ppermute | solution.py:341
  63.1 4.2 %branch_0_fun.11 = (bf16[128,1024]{1,0:T(8,128)(2,1)}, bf16[128,1024]{1,0:T(8,128)(2,1)}) custom-call(s32[3]{0:T(128)S(1)} %get-tuple-element.131.place, f32[1,4096]{1,0:T(1,128)S(1)} %get-tuple-element.128.gain, bf16[32,4096]{1,0:T(8,128)(2,1)S(1)} %broadcast_select_fusion.refs_0_, bf16[32,4096]{1,0:T(8,128)(2,1)S(1)} %collective-permute-done.24.refs_1_, ...), custom_call_target="tpu_custom_call" | custom-call | tf_op jit(solution)/shard_map/cond/branch_0_fun/pallas_call | solution.py:495
  67.5 6.4 %shard_map.93 = (bf16[4096,512]{1,0:T(8,128)(2,1)S(1)}, bf16[4096,512]{1,0:T(8,128)(2,1)S(1)}, bf16[512,4096]{1,0:T(8,128)(2,1)S(1)}, bf16[512,4096]{1,0:T(8,128)(2,1)S(1)}, bf16[8,128]{1,0:T(8,128)(2,1)S(1)}) custom-call(s32[3]{0:T(128)S(1)} %pad_add_fusion.place, bf16[4096,512]{1,0:T(8,128)(2,1)} %bitcast.13, ...), custom_call_target="tpu_custom_call" | custom-call | bytes 33554432 | tf_op jit(solution)/shard_map/pallas_call | solution.py:485
  77.0 1.4 collective-permute-start.33
  81.3 3.4 %collective-permute-done.36.refs_10_ = bf16[16,4096]{1,0:T(8,128)(2,1)S(1)} collective-permute-done((bf16[16,4096]{1,0:T(8,128)(2,1)S(1)}, bf16[16,4096]{1,0:T(8,128)(2,1)S(1)}, u32[]{:S(2)}, u32[]{:S(2)}) %collective-permute-start.36) | collective-permute-done | bytes 131104 | tf_op jit(solution)/shard_map/ppermute | solution.py:341
  87.2 1.3 collective-permute-start.39
  97.2 4.6 %collective-permute-done.40.refs_3_.refs_0_ = bf16[16,4096]{1,0:T(8,128)(2,1)S(1)} collective-permute-done((bf16[16,4096]{1,0:T(8,128)(2,1)S(1)}, bf16[16,4096]{1,0:T(8,128)(2,1)S(1)}, u32[]{:S(2)}, u32[]{:S(2)}) %collective-permute-start.40) | collective-permute-done | bytes 131104 | tf_op jit(solution)/shard_map/ppermute | solution.py:344
  102.2 2.1 %collective-permute-done.44.refs_4_.refs_0_ = bf16[16,4096]{1,0:T(8,128)(2,1)S(1)} collective-permute-done((bf16[16,4096]{1,0:T(8,128)(2,1)S(1)}, bf16[16,4096]{1,0:T(8,128)(2,1)S(1)}, u32[]{:S(2)}, u32[]{:S(2)}) %collective-permute-start.44) | collective-permute-done | bytes 131104 | tf_op jit(solution)/shard_map/ppermute | solution.py:344
  109.6 1.3 collective-permute-done.49.refs_9_
  110.9 1.6 %collective-permute-done.50.refs_10_ = bf16[16,4096]{1,0:T(8,128)(2,1)S(1)} collective-permute-done((bf16[16,4096]{1,0:T(8,128)(2,1)S(1)}, bf16[16,4096]{1,0:T(8,128)(2,1)S(1)}, u32[]{:S(2)}, u32[]{:S(2)}) %collective-permute-start.50) | collective-permute-done | bytes 131104 | tf_op jit(solution)/shard_map/ppermute | solution.py:341
  112.5 4.6 %shard_map.98 = (bf16[16,4096]{1,0:T(8,128)(2,1)S(1)}, bf16[16,4096]{1,0:T(8,128)(2,1)S(1)}, bf16[16,4096]{1,0:T(8,128)(2,1)S(1)}, bf16[16,4096]{1,0:T(8,128)(2,...) custom-call(s32[3]{0:T(128)S(1)} %pad_add_fusion.place, ...), custom_call_target="tpu_custom_call" | custom-call | tf_op jit(solution)/shard_map/pallas_call | solution.py:551
  130.9 14.8 %collective-permute-start.63 = (bf16[16,4096]{1,0:T(8,128)(2,1)S(1)}, bf16[16,4096]{1,0:T(8,128)(2,1)S(1)}, u32[]{:S(2)}, u32[]{:S(2)}) collective-permute-start(bf16[16,4096]{1,0:T(8,128)(2,1)S(1)} %get-tuple-element.249.refs_0_), channel_id=1, source_target_pairs={{0,1},{1,0},{2,3},{3,2},{4,5},{5,4},{6,7},{7,6},{8,9},{9,8},{10,11... | collective-permute-start | bytes 393224 | tf_op jit(solution)/shard_map/ppermute | solution.py:341
  148.2 1.6 collective-permute-start.65
  150.4 2.1 %collective-permute-start.67 = (bf16[16,4096]{1,0:T(8,128)(2,1)S(1)}, bf16[16,4096]{1,0:T(8,128)(2,1)S(1)}, u32[]{:S(2)}, u32[]{:S(2)}) collective-permute-start(bf16[16,4096]{1,0:T(8,128)(2,1)S(1)} %collective-permute-done.59.refs_4_), channel_id=1, source_target_pairs={{0,1},{1,0},{2,3},{3,2},{4,5},{5,4},{6,7},{7,6},{8,9},{9,8},{10,11... | collective-permute-start | bytes 393224 | tf_op jit(solution)/shard_map/ppermute | solution.py:341
  155.0 2.0 %shard_map.101 = bf16[2,128,4096]{2,1,0:T(8,128)(2,1)} custom-call(s32[3]{0:T(128)S(1)} %pad_add_fusion.place, bf16[16,4096]{1,0:T(8,128)(2,1)S(1)} %get-tuple-element.249.refs_0_, bf16[16,4096]{1,0:T(8,128)(2,1)S(1)} %get-tuple-element.248.refs_1_, bf16[16,4096]{1,0:T(8,128)(2,1)S(1)} %collective-permute-done.57.refs_2_, ...), custom_call_target="tpu_custom_call" | custom-call | tf_op jit(solution)/shard_map/pallas_call | solution.py:563
  (119 shorter events, 52.2 us)
Async XLA Ops:
  0.1 7.7 %collective-permute-start.10 = (bf16[4096,512]{1,0:T(8,128)(2,1)}, bf16[4096,512]{1,0:T(8,128)(2,1)S(1)}, u32[]{:S(2)}, u32[]{:S(2)}) collective-permute-start(bf16[4096,512]{1,0:T(8,128)(2,1)} %get-tuple-element.124), channel_id=1, source_target_pairs={{0,1},{1,0},{2,3},{3,2},{4,5},{5,4},{6,7},{7,6},{8,9},{9,8},{10,11... | collective-permute-start | bytes 12582920 | tf_op jit(solution)/shard_map/cond/branch_2_fun/ppermute | solution.py:341
  0.8 13.0 %collective-permute-start.11 = (bf16[512,4096]{1,0:T(8,128)(2,1)}, bf16[512,4096]{1,0:T(8,128)(2,1)S(1)}, u32[]{:S(2)}, u32[]{:S(2)}) collective-permute-start(bf16[512,4096]{1,0:T(8,128)(2,1)} %get-tuple-element.125), channel_id=1, source_target_pairs={{0,1},{1,0},{2,3},{3,2},{4,5},{5,4},{6,7},{7,6},{8,9},{9,8},{10,11... | collective-permute-start | bytes 12582920 | tf_op jit(solution)/shard_map/cond/branch_2_fun/ppermute | solution.py:341
  0.9 18.9 %collective-permute-start.12 = (bf16[4096,512]{1,0:T(8,128)(2,1)}, bf16[4096,512]{1,0:T(8,128)(2,1)S(1)}, u32[]{:S(2)}, u32[]{:S(2)}) collective-permute-start(bf16[4096,512]{1,0:T(8,128)(2,1)} %get-tuple-element.126), channel_id=1, source_target_pairs={{0,1},{1,0},{2,3},{3,2},{4,5},{5,4},{6,7},{7,6},{8,9},{9,8},{10,11... | collective-permute-start | bytes 12582920 | tf_op jit(solution)/shard_map/cond/branch_2_fun/ppermute | solution.py:341
  1.3 24.5 %collective-permute-start.9 = (bf16[4096,512]{1,0:T(8,128)(2,1)}, bf16[4096,512]{1,0:T(8,128)(2,1)S(1)}, u32[]{:S(2)}, u32[]{:S(2)}) collective-permute-start(bf16[4096,512]{1,0:T(8,128)(2,1)} %get-tuple-element.123), channel_id=1, source_target_pairs={{0,1},{1,0},{2,3},{3,2},{4,5},{5,4},{6,7},{7,6},{8,9},{9,8},{10,11... | collective-permute-start | bytes 12582920 | tf_op jit(solution)/shard_map/cond/branch_2_fun/ppermute | solution.py:341
  31.8 17.6 %collective-permute-start.23 = (bf16[32,4096]{1,0:T(8,128)(2,1)S(1)}, bf16[32,4096]{1,0:T(8,128)(2,1)S(1)}, u32[]{:S(2)}, u32[]{:S(2)}) collective-permute-start(bf16[32,4096]{1,0:T(8,128)(2,1)S(1)} %get-tuple-element.130), channel_id=1, source_target_pairs={{0,24},{1,25},{2,26},{3,27},{4,28},{5,29},{6,30},{7,31}} | collective-permute-start | bytes 786440 | tf_op jit(solution)/shard_map/cond/branch_0_fun/ppermute | solution.py:344
  49.4 10.4 %collective-permute-start.24 = (bf16[32,4096]{1,0:T(8,128)(2,1)S(1)}, bf16[32,4096]{1,0:T(8,128)(2,1)S(1)}, u32[]{:S(2)}, u32[]{:S(2)}) collective-permute-start(bf16[32,4096]{1,0:T(8,128)(2,1)S(1)} %broadcast_select_fusion.refs_0_), channel_id=1, source_target_pairs={{0,2},{1,3},{2,0},{3,1},{4,6},{5,7},{6,4},{7,5},{8,10},{9,11},{10,... | collective-permute-start | bytes 786440 | tf_op jit(solution)/shard_map/cond/branch_0_fun/ppermute | solution.py:341
  51.3 8.5 %collective-permute-start.25 = (bf16[32,4096]{1,0:T(8,128)(2,1)S(1)}, bf16[32,4096]{1,0:T(8,128)(2,1)S(1)}, u32[]{:S(2)}, u32[]{:S(2)}) collective-permute-start(bf16[32,4096]{1,0:T(8,128)(2,1)S(1)} %broadcast_select_fusion.refs_0_), channel_id=1, source_target_pairs={{0,4},{1,5},{2,6},{3,7},{4,0},{5,1},{6,2},{7,3},{8,12},{9,13},{10,... | collective-permute-start | bytes 786440 | tf_op jit(solution)/shard_map/cond/branch_0_fun/ppermute | solution.py:341
  51.7 11.4 %collective-permute-start.26 = (bf16[32,4096]{1,0:T(8,128)(2,1)S(1)}, bf16[32,4096]{1,0:T(8,128)(2,1)S(1)}, u32[]{:S(2)}, u32[]{:S(2)}) collective-permute-start(bf16[32,4096]{1,0:T(8,128)(2,1)S(1)} %broadcast_select_fusion.refs_0_), channel_id=1, source_target_pairs={{0,6},{1,7},{2,4},{3,5},{4,2},{5,3},{6,0},{7,1},{8,14},{9,15},{10,... | collective-permute-start | bytes 786440 | tf_op jit(solution)/shard_map/cond/branch_0_fun/ppermute | solution.py:341
  79.2 5.5 %collective-permute-start.36 = (bf16[16,4096]{1,0:T(8,128)(2,1)S(1)}, bf16[16,4096]{1,0:T(8,128)(2,1)S(1)}, u32[]{:S(2)}, u32[]{:S(2)}) collective-permute-start(bf16[16,4096]{1,0:T(8,128)(2,1)S(1)} %collective-permute-done.34.refs_8_), channel_id=1, source_target_pairs={{0,2},{1,3},{2,0},{3,1},{4,6},{5,7},{6,4},{7,5},{8,10},{9,11},{10,... | collective-permute-start | bytes 393224 | tf_op jit(solution)/shard_map/ppermute | solution.py:341
  79.5 5.3 %collective-permute-start.35 = (bf16[16,4096]{1,0:T(8,128)(2,1)S(1)}, bf16[16,4096]{1,0:T(8,128)(2,1)S(1)}, u32[]{:S(2)}, u32[]{:S(2)}) collective-permute-start(bf16[16,4096]{1,0:T(8,128)(2,1)S(1)} %collective-permute-done.31.refs_5_), channel_id=1, source_target_pairs={{0,4},{1,5},{2,6},{3,7},{4,0},{5,1},{6,2},{7,3},{8,12},{9,13},{10,... | collective-permute-start | bytes 393224 | tf_op jit(solution)/shard_map/ppermute | solution.py:341
  88.5 5.4 %collective-permute-start.41 = (bf16[16,4096]{1,0:T(8,128)(2,1)S(1)}, bf16[16,4096]{1,0:T(8,128)(2,1)S(1)}, u32[]{:S(2)}, u32[]{:S(2)}) collective-permute-start(bf16[16,4096]{1,0:T(8,128)(2,1)S(1)} %get-tuple-element.233), channel_id=1, source_target_pairs={{0,6},{1,7},{2,4},{3,5},{4,2},{5,3},{6,0},{7,1},{8,14},{9,15},{10,... | collective-permute-start | bytes 393224 | tf_op jit(solution)/shard_map/ppermute | solution.py:341
  89.6 5.6 %collective-permute-start.42 = (bf16[16,4096]{1,0:T(8,128)(2,1)S(1)}, bf16[16,4096]{1,0:T(8,128)(2,1)S(1)}, u32[]{:S(2)}, u32[]{:S(2)}) collective-permute-start(bf16[16,4096]{1,0:T(8,128)(2,1)S(1)} %get-tuple-element.234), channel_id=1, source_target_pairs={{0,4},{1,5},{2,6},{3,7},{4,0},{5,1},{6,2},{7,3},{8,12},{9,13},{10,... | collective-permute-start | bytes 393224 | tf_op jit(solution)/shard_map/ppermute | solution.py:341
  92.6 9.1 %collective-permute-start.40 = (bf16[16,4096]{1,0:T(8,128)(2,1)S(1)}, bf16[16,4096]{1,0:T(8,128)(2,1)S(1)}, u32[]{:S(2)}, u32[]{:S(2)}) collective-permute-start(bf16[16,4096]{1,0:T(8,128)(2,1)S(1)} %shard_map.96), channel_id=1, source_target_pairs={{16,24},{17,25},{18,26},{19,27},{20,28},{21,29},{22,30},{23,31}} | collective-permute-start | bytes 393224 | tf_op jit(solution)/shard_map/ppermute | solution.py:344
  95.9 8.4 %collective-permute-start.44 = (bf16[16,4096]{1,0:T(8,128)(2,1)S(1)}, bf16[16,4096]{1,0:T(8,128)(2,1)S(1)}, u32[]{:S(2)}, u32[]{:S(2)}) collective-permute-start(bf16[16,4096]{1,0:T(8,128)(2,1)S(1)} %shard_map.97), channel_id=1, source_target_pairs={{16,24},{17,25},{18,26},{19,27},{20,28},{21,29},{22,30},{23,31}} | collective-permute-start | bytes 393224 | tf_op jit(solution)/shard_map/ppermute | solution.py:344
  118.4 5.7 %collective-permute-start.52 = (bf16[16,4096]{1,0:T(8,128)(2,1)S(1)}, bf16[16,4096]{1,0:T(8,128)(2,1)S(1)}, u32[]{:S(2)}, u32[]{:S(2)}) collective-permute-start(bf16[16,4096]{1,0:T(8,128)(2,1)S(1)} %get-tuple-element.238), channel_id=1, source_target_pairs={{0,4},{1,5},{2,6},{3,7},{4,0},{5,1},{6,2},{7,3},{8,12},{9,13},{10,... | collective-permute-start | bytes 393224 | tf_op jit(solution)/shard_map/ppermute | solution.py:341
  118.8 5.7 %collective-permute-start.53 = (bf16[16,4096]{1,0:T(8,128)(2,1)S(1)}, bf16[16,4096]{1,0:T(8,128)(2,1)S(1)}, u32[]{:S(2)}, u32[]{:S(2)}) collective-permute-start(bf16[16,4096]{1,0:T(8,128)(2,1)S(1)} %get-tuple-element.239), channel_id=1, source_target_pairs={{0,2},{1,3},{2,0},{3,1},{4,6},{5,7},{6,4},{7,5},{8,10},{9,11},{10,... | collective-permute-start | bytes 393224 | tf_op jit(solution)/shard_map/ppermute | solution.py:341
  119.9 6.4 %collective-permute-start.54 = (bf16[16,4096]{1,0:T(8,128)(2,1)S(1)}, bf16[16,4096]{1,0:T(8,128)(2,1)S(1)}, u32[]{:S(2)}, u32[]{:S(2)}) collective-permute-start(bf16[16,4096]{1,0:T(8,128)(2,1)S(1)} %get-tuple-element.241), channel_id=1, source_target_pairs={{0,6},{1,7},{2,4},{3,5},{4,2},{5,3},{6,0},{7,1},{8,14},{9,15},{10,... | collective-permute-start | bytes 393224 | tf_op jit(solution)/shard_map/ppermute | solution.py:341
  121.1 5.5 %collective-permute-start.55 = (bf16[16,4096]{1,0:T(8,128)(2,1)S(1)}, bf16[16,4096]{1,0:T(8,128)(2,1)S(1)}, u32[]{:S(2)}, u32[]{:S(2)}) collective-permute-start(bf16[16,4096]{1,0:T(8,128)(2,1)S(1)} %get-tuple-element.242), channel_id=1, source_target_pairs={{0,4},{1,5},{2,6},{3,7},{4,0},{5,1},{6,2},{7,3},{8,12},{9,13},{10,... | collective-permute-start | bytes 393224 | tf_op jit(solution)/shard_map/ppermute | solution.py:341
  127.9 17.8 %collective-permute-start.57 = (bf16[16,4096]{1,0:T(8,128)(2,1)S(1)}, bf16[16,4096]{1,0:T(8,128)(2,1)S(1)}, u32[]{:S(2)}, u32[]{:S(2)}) collective-permute-start(bf16[16,4096]{1,0:T(8,128)(2,1)S(1)} %get-tuple-element.249.refs_0_), channel_id=1, source_target_pairs={{0,2},{1,3},{2,0},{3,1},{4,6},{5,7},{6,4},{7,5},{8,10},{9,11},{10,... | collective-permute-start | bytes 393224 | tf_op jit(solution)/shard_map/ppermute | solution.py:341
  128.7 17.9 %collective-permute-start.60 = (bf16[16,4096]{1,0:T(8,128)(2,1)S(1)}, bf16[16,4096]{1,0:T(8,128)(2,1)S(1)}, u32[]{:S(2)}, u32[]{:S(2)}) collective-permute-start(bf16[16,4096]{1,0:T(8,128)(2,1)S(1)} %get-tuple-element.248.refs_1_), channel_id=1, source_target_pairs={{0,4},{1,5},{2,6},{3,7},{4,0},{5,1},{6,2},{7,3},{8,12},{9,13},{10,... | collective-permute-start | bytes 393224 | tf_op jit(solution)/shard_map/ppermute | solution.py:341
  129.5 17.9 %collective-permute-start.58 = (bf16[16,4096]{1,0:T(8,128)(2,1)S(1)}, bf16[16,4096]{1,0:T(8,128)(2,1)S(1)}, u32[]{:S(2)}, u32[]{:S(2)}) collective-permute-start(bf16[16,4096]{1,0:T(8,128)(2,1)S(1)} %get-tuple-element.248.refs_1_), channel_id=1, source_target_pairs={{0,2},{1,3},{2,0},{3,1},{4,6},{5,7},{6,4},{7,5},{8,10},{9,11},{10,... | collective-permute-start | bytes 393224 | tf_op jit(solution)/shard_map/ppermute | solution.py:341
  130.2 18.0 %collective-permute-start.59 = (bf16[16,4096]{1,0:T(8,128)(2,1)S(1)}, bf16[16,4096]{1,0:T(8,128)(2,1)S(1)}, u32[]{:S(2)}, u32[]{:S(2)}) collective-permute-start(bf16[16,4096]{1,0:T(8,128)(2,1)S(1)} %get-tuple-element.249.refs_0_), channel_id=1, source_target_pairs={{0,4},{1,5},{2,6},{3,7},{4,0},{5,1},{6,2},{7,3},{8,12},{9,13},{10,... | collective-permute-start | bytes 393224 | tf_op jit(solution)/shard_map/ppermute | solution.py:341
  130.9 18.8 %collective-permute-start.63 = (bf16[16,4096]{1,0:T(8,128)(2,1)S(1)}, bf16[16,4096]{1,0:T(8,128)(2,1)S(1)}, u32[]{:S(2)}, u32[]{:S(2)}) collective-permute-start(bf16[16,4096]{1,0:T(8,128)(2,1)S(1)} %get-tuple-element.249.refs_0_), channel_id=1, source_target_pairs={{0,1},{1,0},{2,3},{3,2},{4,5},{5,4},{6,7},{7,6},{8,9},{9,8},{10,11... | collective-permute-start | bytes 393224 | tf_op jit(solution)/shard_map/ppermute | solution.py:341
  148.2 5.5 %collective-permute-start.65 = (bf16[16,4096]{1,0:T(8,128)(2,1)S(1)}, bf16[16,4096]{1,0:T(8,128)(2,1)S(1)}, u32[]{:S(2)}, u32[]{:S(2)}) collective-permute-start(bf16[16,4096]{1,0:T(8,128)(2,1)S(1)} %collective-permute-done.57.refs_2_), channel_id=1, source_target_pairs={{0,1},{1,0},{2,3},{3,2},{4,5},{5,4},{6,7},{7,6},{8,9},{9,8},{10,11... | collective-permute-start | bytes 393224 | tf_op jit(solution)/shard_map/ppermute | solution.py:341
  (36 other events, 235.3 us)

commit v6 on v5

--- a/solution.py
+++ b/solution.py
@@ -220,6 +220,17 @@
     for term in terms[1:]:
         total = total + term[...].astype(F32)
     out[...] = total.astype(BF16)
+
+
+def join_halves_kernel(config, place, residual, *refs):
+    terms, out = refs[:-1], refs[-1]
+    each, height = len(terms) // 2, terms[0].shape[0]
+    for half in range(2):
+        at = pl.ds(half * height, height)
+        total = residual[at, :].astype(F32)
+        for term in terms[half * each : (half + 1) * each]:
+            total = total + term[...].astype(F32)
+        out[at, :] = total.astype(BF16)
 
 
 def stream_out(copies, pairs):
@@ -400,8 +411,35 @@
             )
         return shares
 
+    def add(*terms):
+        return kernel_call(
+            functools.partial(finish_kernel, config),
+            sds((piece, width)),
+            [IN_SMEM] + [IN_VMEM] * len(terms),
+            [],
+            4,
+        )(place, *terms)
+
+    def relayed(parts):
+        (own_a, own_b), (x_a, x_b), (y_a, y_b), (d_a, d_b) = (parts[i : i + 2] for i in (0, 2, 4, 6))
+        through_a, through_b = to_chip[2](d_a), to_chip[1](d_b)
+        far_b, far_a = to_chip[1](x_b), to_chip[2](y_a)
+        near_a, near_b = to_chip[1](add(x_a, through_a)), to_chip[2](add(y_b, through_b))
+        return [own_a, far_a, near_a], [own_b, far_b, near_b]
+
+    two_ways = blocks == 4 and groups == 2
+
     def finish_whole(parts, residual):
-        arrived = [to_chip[j](parts[j]) for j in reversed(range(1, blocks))]
+        if two_ways:
+            terms = relayed(parts)
+            return kernel_call(
+                functools.partial(join_halves_kernel, config),
+                sds((height, width)),
+                [IN_SMEM] + [IN_VMEM] * 7,
+                [],
+                6,
+            )(place, residual, *terms[0], *terms[1])
+        arrived = [to_chip[j](parts[j]) for j in range(1, blocks)]
         return kernel_call(
             functools.partial(finish_kernel, config),
             sds((height, width)),
@@ -435,7 +473,7 @@
         )
         parts = kernel_call(
             functools.partial(join_kernel, config),
-            [sds((height, width))] * blocks,
+            partials if two_ways else [sds((height, width))] * blocks,
             [IN_SMEM] + [IN_VMEM] * 2,
             [],
             8,

time: 157 us -> 156 us (level)
  waiting for transfers between devices: 70.2 us -> 65.7 us
  starting transfers between devices: 55.1 us -> 58.6 us
    ppermute x46, waiting for transfers between devices: 47.3 us -> 42.9 us  [flip(): return lambda x: lax.ppermute(x, 'seq', pairs)]
    ppermute x46, starting transfers between devices: 48.5 us -> 52 us  [flip(): return lambda x: lax.ppermute(x, 'seq', pairs)]
  transfers between devices with their start and end apart: 53 -> 53, of which waited for: 29 -> 28; matrix products, arithmetic and copies ran while one was open for 0% -> 0% of each run, Pallas kernels for 6% -> 6%
where the time goes in v6:
time: 156 us
  waiting for transfers between devices  65.7 us (42%)
  starting transfers between devices  58.6 us (38%)
  Pallas kernels  27.8 us (18%)
  local copies, waits for them, and re-layouts  3.25 us (2%)
    ppermute x46, starting transfers between devices, flip(): return lambda x: lax.ppermute(x, 'seq', pairs)  52 us
    ppermute x46, waiting for transfers between devices, flip(): return lambda x: lax.ppermute(x, 'seq', pairs)  42.9 us
    ppermute x7, waiting for transfers between devices, up(): return lax.ppermute(x, 'section', [(source, target)])  22.8 us
    pallas_call x2, Pallas kernels, keep(): kernel_call(functools.partial(body, config), [pltpu.VMEM(x.shape, BF16) f...  13.4 us
    ppermute x7, starting transfers between devices, up(): return lax.ppermute(x, 'section', [(source, target)])  6.57 us
    pallas_call x2, Pallas kernels, shards(): kernel_call(functools.partial(only_in([step])(section_kernel), config), p...  5.69 us
    pallas_call x1, Pallas kernels, project_memory(): kernel_call(functools.partial(memory_kernel, config), [sds((length, both)...  4.17 us
    another operation x7, local copies, waits for them, and re-layouts  3.22 us
  transfers between devices with their start and end apart: 53, of which 28 were waited for; matrix products, arithmetic and copies ran while one was open for 0% of the time, Pallas kernels for 6%

profile of v6, /device:TPU:25, one launch (start us, length us, event | category | flops | bytes accessed | tf_op | source)
XLA Modules:
  0.0 156.0 jit_solution(8628213888550412764)
XLA Ops:
  0.1 28.9 %conditional.2 = (bf16[32,4096]{1,0:T(8,128)(2,1)S(1)}, bf16[4096,512]{1,0:T(8,128)(2,1)}, bf16[4096,512]{1,0:T(8,128)(2,1)}, bf16[512,4096]{1,0:T(8,128)(2,1)},...) conditional(s32[]{:T(128)} %clamp.3, (s32[3]{0:T(128)S(1)}, ...), branch_computations={%region_0.1_spmd, %region_1.2_spmd, %region_2.3_spmd} | conditional | bytes 135528864 | solution.py:510
  1.4 6.4 %collective-permute-done.12 = bf16[4096,512]{1,0:T(8,128)(2,1)S(1)} collective-permute-done((bf16[4096,512]{1,0:T(8,128)(2,1)}, bf16[4096,512]{1,0:T(8,128)(2,1)S(1)}, u32[]{:S(2)}, u32[]{:S(2)}) %collective-permute-start.12) | collective-permute-done | bytes 4194336 | tf_op jit(solution)/shard_map/cond/branch_2_fun/ppermute | solution.py:352
  7.8 6.0 %collective-permute-done.13 = bf16[4096,512]{1,0:T(8,128)(2,1)S(1)} collective-permute-done((bf16[4096,512]{1,0:T(8,128)(2,1)}, bf16[4096,512]{1,0:T(8,128)(2,1)S(1)}, u32[]{:S(2)}, u32[]{:S(2)}) %collective-permute-start.13) | collective-permute-done | bytes 4194336 | tf_op jit(solution)/shard_map/cond/branch_2_fun/ppermute | solution.py:352
  13.8 6.0 %collective-permute-done.14 = bf16[512,4096]{1,0:T(8,128)(2,1)S(1)} collective-permute-done((bf16[512,4096]{1,0:T(8,128)(2,1)}, bf16[512,4096]{1,0:T(8,128)(2,1)S(1)}, u32[]{:S(2)}, u32[]{:S(2)}) %collective-permute-start.14) | collective-permute-done | bytes 4194336 | tf_op jit(solution)/shard_map/cond/branch_2_fun/ppermute | solution.py:352
  19.8 6.0 %collective-permute-done.15 = bf16[4096,512]{1,0:T(8,128)(2,1)S(1)} collective-permute-done((bf16[4096,512]{1,0:T(8,128)(2,1)}, bf16[4096,512]{1,0:T(8,128)(2,1)S(1)}, u32[]{:S(2)}, u32[]{:S(2)}) %collective-permute-start.15) | collective-permute-done | bytes 4194336 | tf_op jit(solution)/shard_map/cond/branch_2_fun/ppermute | solution.py:352
  31.1 34.7 %conditional.3 = (bf16[128,1024]{1,0:T(8,128)(2,1)}, bf16[128,1024]{1,0:T(8,128)(2,1)}, bf16[16,4096]{1,0:T(8,128)(2,1)S(1)}, bf16[16,4096]{1,0:T(8,128)(2,1)S(1)}) conditional(s32[]{:T(128)} %convert_element_type.3, (s32[]{:T(128)}, bf16[32,4096]{1,0:T(8,128)(2,1)S(1)}, s32[3]{0:T(128)S(1)}, bf16[4096,512]{1,0:T(8,128)(2,1)}, ...), branch_computations={%region_3.4_spmd, %region_4.5_spmd} | conditional | flops 131073 | bytes 58720760 | solution.py:573
  33.1 15.7 %collective-permute-done.26 = bf16[32,4096]{1,0:T(8,128)(2,1)S(1)} collective-permute-done((bf16[32,4096]{1,0:T(8,128)(2,1)S(1)}, bf16[32,4096]{1,0:T(8,128)(2,1)S(1)}, u32[]{:S(2)}, u32[]{:S(2)}) %collective-permute-start.26) | collective-permute-done | bytes 262176 | tf_op jit(solution)/shard_map/cond/branch_0_fun/ppermute | solution.py:355
  49.8 1.6 %collective-permute-start.28 = (bf16[32,4096]{1,0:T(8,128)(2,1)S(1)}, bf16[32,4096]{1,0:T(8,128)(2,1)S(1)}, u32[]{:S(2)}, u32[]{:S(2)}) collective-permute-start(bf16[32,4096]{1,0:T(8,128)(2,1)S(1)} %broadcast_select_fusion.refs_0_), channel_id=1, source_target_pairs={{0,4},{1,5},{2,6},{3,7},{4,0},{5,1},{6,2},{7,3},{8,12},{9,13},{10,... | collective-permute-start | bytes 786440 | tf_op jit(solution)/shard_map/cond/branch_0_fun/ppermute | solution.py:352
  51.6 7.0 %branch_0_fun.14 = (bf16[4096,512]{1,0:T(8,128)(2,1)S(1)}, bf16[4096,512]{1,0:T(8,128)(2,1)S(1)}, bf16[4096,512]{1,0:T(8,128)(2,1)S(1)}, bf16[4096,512]{1,0:T(8,128)(2,1)S(1)}, bf16[8,128]{1,0:T(8,128)(2,1)}) custom-call(s32[3]{0:T(128)S(1)} %get-tuple-element.135.place, bf16[4096,512]{1,0:T(8,128)(2,1)} %get-tuple-element.136.refs_0_, ...), custom_call_target="tpu_custom_call" | custom-call | bytes 33554432 | tf_op jit(solution)/shard_map/cond/branch_0_fun/pallas_call | solution.py:523
  58.6 2.9 %collective-permute-done.29.refs_3_ = bf16[32,4096]{1,0:T(8,128)(2,1)S(1)} collective-permute-done((bf16[32,4096]{1,0:T(8,128)(2,1)S(1)}, bf16[32,4096]{1,0:T(8,128)(2,1)S(1)}, u32[]{:S(2)}, u32[]{:S(2)}) %collective-permute-start.29) | collective-permute-done | bytes 262176 | tf_op jit(solution)/shard_map/cond/branch_0_fun/ppermute | solution.py:352
  61.5 4.2 %branch_0_fun.15 = (bf16[128,1024]{1,0:T(8,128)(2,1)}, bf16[128,1024]{1,0:T(8,128)(2,1)}) custom-call(s32[3]{0:T(128)S(1)} %get-tuple-element.135.place, f32[1,4096]{1,0:T(1,128)S(1)} %get-tuple-element.132.gain, bf16[32,4096]{1,0:T(8,128)(2,1)S(1)} %broadcast_select_fusion.refs_0_, bf16[32,4096]{1,0:T(8,128)(2,1)S(1)} %collective-permute-done.27.refs_1_, ...), custom_call_target="tpu_custom_call" | custom-call | tf_op jit(solution)/shard_map/cond/branch_0_fun/pallas_call | solution.py:533
  65.9 6.4 %shard_map.93 = (bf16[4096,512]{1,0:T(8,128)(2,1)S(1)}, bf16[4096,512]{1,0:T(8,128)(2,1)S(1)}, bf16[512,4096]{1,0:T(8,128)(2,1)S(1)}, bf16[512,4096]{1,0:T(8,128)(2,1)S(1)}, bf16[8,128]{1,0:T(8,128)(2,1)S(1)}) custom-call(s32[3]{0:T(128)S(1)} %pad_add_fusion.place, bf16[4096,512]{1,0:T(8,128)(2,1)} %bitcast.13, ...), custom_call_target="tpu_custom_call" | custom-call | bytes 33554432 | tf_op jit(solution)/shard_map/pallas_call | solution.py:523
  79.3 2.6 %collective-permute-done.39.refs_10_ = bf16[16,4096]{1,0:T(8,128)(2,1)S(1)} collective-permute-done((bf16[16,4096]{1,0:T(8,128)(2,1)S(1)}, bf16[16,4096]{1,0:T(8,128)(2,1)S(1)}, u32[]{:S(2)}, u32[]{:S(2)}) %collective-permute-start.39) | collective-permute-done | bytes 131104 | tf_op jit(solution)/shard_map/ppermute | solution.py:352
  84.0 1.8 %collective-permute-start.40 = (bf16[16,4096]{1,0:T(8,128)(2,1)S(1)}, bf16[16,4096]{1,0:T(8,128)(2,1)S(1)}, u32[]{:S(2)}, u32[]{:S(2)}) collective-permute-start(bf16[16,4096]{1,0:T(8,128)(2,1)S(1)} %get-tuple-element.233), channel_id=1, source_target_pairs={{0,6},{1,7},{2,4},{3,5},{4,2},{5,3},{6,0},{7,1},{8,14},{9,15},{10,... | collective-permute-start | bytes 393224 | tf_op jit(solution)/shard_map/ppermute | solution.py:352
  86.7 1.7 %collective-permute-start.44 = (bf16[16,4096]{1,0:T(8,128)(2,1)S(1)}, bf16[16,4096]{1,0:T(8,128)(2,1)S(1)}, u32[]{:S(2)}, u32[]{:S(2)}) collective-permute-start(bf16[16,4096]{1,0:T(8,128)(2,1)S(1)} %get-tuple-element.237), channel_id=1, source_target_pairs={{0,6},{1,7},{2,4},{3,5},{4,2},{5,3},{6,0},{7,1},{8,14},{9,15},{10,... | collective-permute-start | bytes 393224 | tf_op jit(solution)/shard_map/ppermute | solution.py:352
  95.5 4.9 %collective-permute-done.43.refs_3_.refs_0_ = bf16[16,4096]{1,0:T(8,128)(2,1)S(1)} collective-permute-done((bf16[16,4096]{1,0:T(8,128)(2,1)S(1)}, bf16[16,4096]{1,0:T(8,128)(2,1)S(1)}, u32[]{:S(2)}, u32[]{:S(2)}) %collective-permute-start.43) | collective-permute-done | bytes 131104 | tf_op jit(solution)/shard_map/ppermute | solution.py:355
  100.8 2.2 %collective-permute-done.47.refs_4_.refs_0_ = bf16[16,4096]{1,0:T(8,128)(2,1)S(1)} collective-permute-done((bf16[16,4096]{1,0:T(8,128)(2,1)S(1)}, bf16[16,4096]{1,0:T(8,128)(2,1)S(1)}, u32[]{:S(2)}, u32[]{:S(2)}) %collective-permute-start.47) | collective-permute-done | bytes 131104 | tf_op jit(solution)/shard_map/ppermute | solution.py:355
  109.6 1.6 %collective-permute-done.53.refs_10_ = bf16[16,4096]{1,0:T(8,128)(2,1)S(1)} collective-permute-done((bf16[16,4096]{1,0:T(8,128)(2,1)S(1)}, bf16[16,4096]{1,0:T(8,128)(2,1)S(1)}, u32[]{:S(2)}, u32[]{:S(2)}) %collective-permute-start.53) | collective-permute-done | bytes 131104 | tf_op jit(solution)/shard_map/ppermute | solution.py:352
  111.2 4.6 %shard_map.98 = (bf16[16,4096]{1,0:T(8,128)(2,1)S(1)}, bf16[16,4096]{1,0:T(8,128)(2,1)S(1)}, bf16[16,4096]{1,0:T(8,128)(2,1)S(1)}, bf16[16,4096]{1,0:T(8,128)(2,...) custom-call(s32[3]{0:T(128)S(1)} %pad_add_fusion.place, ...), custom_call_target="tpu_custom_call" | custom-call | tf_op jit(solution)/shard_map/pallas_call | solution.py:589
  121.3 1.6 %collective-permute-start.59 = (bf16[16,4096]{1,0:T(8,128)(2,1)S(1)}, bf16[16,4096]{1,0:T(8,128)(2,1)S(1)}, u32[]{:S(2)}, u32[]{:S(2)}) collective-permute-start(bf16[16,4096]{1,0:T(8,128)(2,1)S(1)} %get-tuple-element.247), channel_id=1, source_target_pairs={{0,2},{1,3},{2,0},{3,1},{4,6},{5,7},{6,4},{7,5},{8,10},{9,11},{10,... | collective-permute-start | bytes 393224 | tf_op jit(solution)/shard_map/ppermute | solution.py:352
  129.8 14.8 %collective-permute-start.66 = (bf16[16,4096]{1,0:T(8,128)(2,1)S(1)}, bf16[16,4096]{1,0:T(8,128)(2,1)S(1)}, u32[]{:S(2)}, u32[]{:S(2)}) collective-permute-start(bf16[16,4096]{1,0:T(8,128)(2,1)S(1)} %get-tuple-element.253.refs_0_), channel_id=1, source_target_pairs={{0,1},{1,0},{2,3},{3,2},{4,5},{5,4},{6,7},{7,6},{8,9},{9,8},{10,11... | collective-permute-start | bytes 393224 | tf_op jit(solution)/shard_map/ppermute | solution.py:352
  147.1 2.3 %collective-permute-start.68 = (bf16[16,4096]{1,0:T(8,128)(2,1)S(1)}, bf16[16,4096]{1,0:T(8,128)(2,1)S(1)}, u32[]{:S(2)}, u32[]{:S(2)}) collective-permute-start(bf16[16,4096]{1,0:T(8,128)(2,1)S(1)} %collective-permute-done.60.refs_2_), channel_id=1, source_target_pairs={{0,1},{1,0},{2,3},{3,2},{4,5},{5,4},{6,7},{7,6},{8,9},{9,8},{10,11... | collective-permute-start | bytes 393224 | tf_op jit(solution)/shard_map/ppermute | solution.py:352
  149.9 2.0 %collective-permute-start.70 = (bf16[16,4096]{1,0:T(8,128)(2,1)S(1)}, bf16[16,4096]{1,0:T(8,128)(2,1)S(1)}, u32[]{:S(2)}, u32[]{:S(2)}) collective-permute-start(bf16[16,4096]{1,0:T(8,128)(2,1)S(1)} %collective-permute-done.62.refs_4_), channel_id=1, source_target_pairs={{0,1},{1,0},{2,3},{3,2},{4,5},{5,4},{6,7},{7,6},{8,9},{9,8},{10,11... | collective-permute-start | bytes 393224 | tf_op jit(solution)/shard_map/ppermute | solution.py:352
  154.0 2.0 %shard_map.101 = bf16[2,128,4096]{2,1,0:T(8,128)(2,1)} custom-call(s32[3]{0:T(128)S(1)} %pad_add_fusion.place, bf16[16,4096]{1,0:T(8,128)(2,1)S(1)} %get-tuple-element.253.refs_0_, bf16[16,4096]{1,0:T(8,128)(2,1)S(1)} %get-tuple-element.252.refs_1_, bf16[16,4096]{1,0:T(8,128)(2,1)S(1)} %collective-permute-done.60.refs_2_, ...), custom_call_target="tpu_custom_call" | custom-call | tf_op jit(solution)/shard_map/pallas_call | solution.py:601
  (119 shorter events, 51.1 us)
Async XLA Ops:
  0.1 7.7 %collective-permute-start.12 = (bf16[4096,512]{1,0:T(8,128)(2,1)}, bf16[4096,512]{1,0:T(8,128)(2,1)S(1)}, u32[]{:S(2)}, u32[]{:S(2)}) collective-permute-start(bf16[4096,512]{1,0:T(8,128)(2,1)} %get-tuple-element.127), channel_id=1, source_target_pairs={{0,1},{1,0},{2,3},{3,2},{4,5},{5,4},{6,7},{7,6},{8,9},{9,8},{10,11... | collective-permute-start | bytes 12582920 | tf_op jit(solution)/shard_map/cond/branch_2_fun/ppermute | solution.py:352
  0.8 13.0 %collective-permute-start.13 = (bf16[4096,512]{1,0:T(8,128)(2,1)}, bf16[4096,512]{1,0:T(8,128)(2,1)S(1)}, u32[]{:S(2)}, u32[]{:S(2)}) collective-permute-start(bf16[4096,512]{1,0:T(8,128)(2,1)} %get-tuple-element.128), channel_id=1, source_target_pairs={{0,1},{1,0},{2,3},{3,2},{4,5},{5,4},{6,7},{7,6},{8,9},{9,8},{10,11... | collective-permute-start | bytes 12582920 | tf_op jit(solution)/shard_map/cond/branch_2_fun/ppermute | solution.py:352
  0.9 18.9 %collective-permute-start.14 = (bf16[512,4096]{1,0:T(8,128)(2,1)}, bf16[512,4096]{1,0:T(8,128)(2,1)S(1)}, u32[]{:S(2)}, u32[]{:S(2)}) collective-permute-start(bf16[512,4096]{1,0:T(8,128)(2,1)} %get-tuple-element.129), channel_id=1, source_target_pairs={{0,1},{1,0},{2,3},{3,2},{4,5},{5,4},{6,7},{7,6},{8,9},{9,8},{10,11... | collective-permute-start | bytes 12582920 | tf_op jit(solution)/shard_map/cond/branch_2_fun/ppermute | solution.py:352
  1.3 24.5 %collective-permute-start.15 = (bf16[4096,512]{1,0:T(8,128)(2,1)}, bf16[4096,512]{1,0:T(8,128)(2,1)S(1)}, u32[]{:S(2)}, u32[]{:S(2)}) collective-permute-start(bf16[4096,512]{1,0:T(8,128)(2,1)} %get-tuple-element.130), channel_id=1, source_target_pairs={{0,1},{1,0},{2,3},{3,2},{4,5},{5,4},{6,7},{7,6},{8,9},{9,8},{10,11... | collective-permute-start | bytes 12582920 | tf_op jit(solution)/shard_map/cond/branch_2_fun/ppermute | solution.py:352
  31.8 17.0 %collective-permute-start.26 = (bf16[32,4096]{1,0:T(8,128)(2,1)S(1)}, bf16[32,4096]{1,0:T(8,128)(2,1)S(1)}, u32[]{:S(2)}, u32[]{:S(2)}) collective-permute-start(bf16[32,4096]{1,0:T(8,128)(2,1)S(1)} %get-tuple-element.134), channel_id=1, source_target_pairs={{0,24},{1,25},{2,26},{3,27},{4,28},{5,29},{6,30},{7,31}} | collective-permute-start | bytes 786440 | tf_op jit(solution)/shard_map/cond/branch_0_fun/ppermute | solution.py:355
  48.8 9.7 %collective-permute-start.27 = (bf16[32,4096]{1,0:T(8,128)(2,1)S(1)}, bf16[32,4096]{1,0:T(8,128)(2,1)S(1)}, u32[]{:S(2)}, u32[]{:S(2)}) collective-permute-start(bf16[32,4096]{1,0:T(8,128)(2,1)S(1)} %broadcast_select_fusion.refs_0_), channel_id=1, source_target_pairs={{0,2},{1,3},{2,0},{3,1},{4,6},{5,7},{6,4},{7,5},{8,10},{9,11},{10,... | collective-permute-start | bytes 786440 | tf_op jit(solution)/shard_map/cond/branch_0_fun/ppermute | solution.py:352
  49.8 8.8 %collective-permute-start.28 = (bf16[32,4096]{1,0:T(8,128)(2,1)S(1)}, bf16[32,4096]{1,0:T(8,128)(2,1)S(1)}, u32[]{:S(2)}, u32[]{:S(2)}) collective-permute-start(bf16[32,4096]{1,0:T(8,128)(2,1)S(1)} %broadcast_select_fusion.refs_0_), channel_id=1, source_target_pairs={{0,4},{1,5},{2,6},{3,7},{4,0},{5,1},{6,2},{7,3},{8,12},{9,13},{10,... | collective-permute-start | bytes 786440 | tf_op jit(solution)/shard_map/cond/branch_0_fun/ppermute | solution.py:352
  51.4 10.1 %collective-permute-start.29 = (bf16[32,4096]{1,0:T(8,128)(2,1)S(1)}, bf16[32,4096]{1,0:T(8,128)(2,1)S(1)}, u32[]{:S(2)}, u32[]{:S(2)}) collective-permute-start(bf16[32,4096]{1,0:T(8,128)(2,1)S(1)} %broadcast_select_fusion.refs_0_), channel_id=1, source_target_pairs={{0,6},{1,7},{2,4},{3,5},{4,2},{5,3},{6,0},{7,1},{8,14},{9,15},{10,... | collective-permute-start | bytes 786440 | tf_op jit(solution)/shard_map/cond/branch_0_fun/ppermute | solution.py:352
  84.0 5.3 %collective-permute-start.40 = (bf16[16,4096]{1,0:T(8,128)(2,1)S(1)}, bf16[16,4096]{1,0:T(8,128)(2,1)S(1)}, u32[]{:S(2)}, u32[]{:S(2)}) collective-permute-start(bf16[16,4096]{1,0:T(8,128)(2,1)S(1)} %get-tuple-element.233), channel_id=1, source_target_pairs={{0,6},{1,7},{2,4},{3,5},{4,2},{5,3},{6,0},{7,1},{8,14},{9,15},{10,... | collective-permute-start | bytes 393224 | tf_op jit(solution)/shard_map/ppermute | solution.py:352
  86.7 5.8 %collective-permute-start.44 = (bf16[16,4096]{1,0:T(8,128)(2,1)S(1)}, bf16[16,4096]{1,0:T(8,128)(2,1)S(1)}, u32[]{:S(2)}, u32[]{:S(2)}) collective-permute-start(bf16[16,4096]{1,0:T(8,128)(2,1)S(1)} %get-tuple-element.237), channel_id=1, source_target_pairs={{0,6},{1,7},{2,4},{3,5},{4,2},{5,3},{6,0},{7,1},{8,14},{9,15},{10,... | collective-permute-start | bytes 393224 | tf_op jit(solution)/shard_map/ppermute | solution.py:352
  88.4 5.2 %collective-permute-start.45 = (bf16[16,4096]{1,0:T(8,128)(2,1)S(1)}, bf16[16,4096]{1,0:T(8,128)(2,1)S(1)}, u32[]{:S(2)}, u32[]{:S(2)}) collective-permute-start(bf16[16,4096]{1,0:T(8,128)(2,1)S(1)} %get-tuple-element.238), channel_id=1, source_target_pairs={{0,4},{1,5},{2,6},{3,7},{4,0},{5,1},{6,2},{7,3},{8,12},{9,13},{10,... | collective-permute-start | bytes 393224 | tf_op jit(solution)/shard_map/ppermute | solution.py:352
  91.2 9.2 %collective-permute-start.43 = (bf16[16,4096]{1,0:T(8,128)(2,1)S(1)}, bf16[16,4096]{1,0:T(8,128)(2,1)S(1)}, u32[]{:S(2)}, u32[]{:S(2)}) collective-permute-start(bf16[16,4096]{1,0:T(8,128)(2,1)S(1)} %shard_map.96), channel_id=1, source_target_pairs={{16,24},{17,25},{18,26},{19,27},{20,28},{21,29},{22,30},{23,31}} | collective-permute-start | bytes 393224 | tf_op jit(solution)/shard_map/ppermute | solution.py:355
  94.2 8.8 %collective-permute-start.47 = (bf16[16,4096]{1,0:T(8,128)(2,1)S(1)}, bf16[16,4096]{1,0:T(8,128)(2,1)S(1)}, u32[]{:S(2)}, u32[]{:S(2)}) collective-permute-start(bf16[16,4096]{1,0:T(8,128)(2,1)S(1)} %shard_map.97), channel_id=1, source_target_pairs={{16,24},{17,25},{18,26},{19,27},{20,28},{21,29},{22,30},{23,31}} | collective-permute-start | bytes 393224 | tf_op jit(solution)/shard_map/ppermute | solution.py:355
  115.9 5.4 %collective-permute-start.54 = (bf16[16,4096]{1,0:T(8,128)(2,1)S(1)}, bf16[16,4096]{1,0:T(8,128)(2,1)S(1)}, u32[]{:S(2)}, u32[]{:S(2)}) collective-permute-start(bf16[16,4096]{1,0:T(8,128)(2,1)S(1)} %get-tuple-element.241), channel_id=1, source_target_pairs={{0,6},{1,7},{2,4},{3,5},{4,2},{5,3},{6,0},{7,1},{8,14},{9,15},{10,... | collective-permute-start | bytes 393224 | tf_op jit(solution)/shard_map/ppermute | solution.py:352
  117.1 5.8 %collective-permute-start.55 = (bf16[16,4096]{1,0:T(8,128)(2,1)S(1)}, bf16[16,4096]{1,0:T(8,128)(2,1)S(1)}, u32[]{:S(2)}, u32[]{:S(2)}) collective-permute-start(bf16[16,4096]{1,0:T(8,128)(2,1)S(1)} %get-tuple-element.242), channel_id=1, source_target_pairs={{0,4},{1,5},{2,6},{3,7},{4,0},{5,1},{6,2},{7,3},{8,12},{9,13},{10,... | collective-permute-start | bytes 393224 | tf_op jit(solution)/shard_map/ppermute | solution.py:352
  118.6 6.6 %collective-permute-start.57 = (bf16[16,4096]{1,0:T(8,128)(2,1)S(1)}, bf16[16,4096]{1,0:T(8,128)(2,1)S(1)}, u32[]{:S(2)}, u32[]{:S(2)}) collective-permute-start(bf16[16,4096]{1,0:T(8,128)(2,1)S(1)} %get-tuple-element.245), channel_id=1, source_target_pairs={{0,6},{1,7},{2,4},{3,5},{4,2},{5,3},{6,0},{7,1},{8,14},{9,15},{10,... | collective-permute-start | bytes 393224 | tf_op jit(solution)/shard_map/ppermute | solution.py:352
  119.8 5.8 %collective-permute-start.58 = (bf16[16,4096]{1,0:T(8,128)(2,1)S(1)}, bf16[16,4096]{1,0:T(8,128)(2,1)S(1)}, u32[]{:S(2)}, u32[]{:S(2)}) collective-permute-start(bf16[16,4096]{1,0:T(8,128)(2,1)S(1)} %get-tuple-element.246), channel_id=1, source_target_pairs={{0,4},{1,5},{2,6},{3,7},{4,0},{5,1},{6,2},{7,3},{8,12},{9,13},{10,... | collective-permute-start | bytes 393224 | tf_op jit(solution)/shard_map/ppermute | solution.py:352
  126.8 17.8 %collective-permute-start.60 = (bf16[16,4096]{1,0:T(8,128)(2,1)S(1)}, bf16[16,4096]{1,0:T(8,128)(2,1)S(1)}, u32[]{:S(2)}, u32[]{:S(2)}) collective-permute-start(bf16[16,4096]{1,0:T(8,128)(2,1)S(1)} %get-tuple-element.253.refs_0_), channel_id=1, source_target_pairs={{0,2},{1,3},{2,0},{3,1},{4,6},{5,7},{6,4},{7,5},{8,10},{9,11},{10,... | collective-permute-start | bytes 393224 | tf_op jit(solution)/shard_map/ppermute | solution.py:352
  127.6 17.9 %collective-permute-start.63 = (bf16[16,4096]{1,0:T(8,128)(2,1)S(1)}, bf16[16,4096]{1,0:T(8,128)(2,1)S(1)}, u32[]{:S(2)}, u32[]{:S(2)}) collective-permute-start(bf16[16,4096]{1,0:T(8,128)(2,1)S(1)} %get-tuple-element.252.refs_1_), channel_id=1, source_target_pairs={{0,4},{1,5},{2,6},{3,7},{4,0},{5,1},{6,2},{7,3},{8,12},{9,13},{10,... | collective-permute-start | bytes 393224 | tf_op jit(solution)/shard_map/ppermute | solution.py:352
  128.8 17.9 %collective-permute-start.61 = (bf16[16,4096]{1,0:T(8,128)(2,1)S(1)}, bf16[16,4096]{1,0:T(8,128)(2,1)S(1)}, u32[]{:S(2)}, u32[]{:S(2)}) collective-permute-start(bf16[16,4096]{1,0:T(8,128)(2,1)S(1)} %get-tuple-element.252.refs_1_), channel_id=1, source_target_pairs={{0,2},{1,3},{2,0},{3,1},{4,6},{5,7},{6,4},{7,5},{8,10},{9,11},{10,... | collective-permute-start | bytes 393224 | tf_op jit(solution)/shard_map/ppermute | solution.py:352
  129.1 17.9 %collective-permute-start.62 = (bf16[16,4096]{1,0:T(8,128)(2,1)S(1)}, bf16[16,4096]{1,0:T(8,128)(2,1)S(1)}, u32[]{:S(2)}, u32[]{:S(2)}) collective-permute-start(bf16[16,4096]{1,0:T(8,128)(2,1)S(1)} %get-tuple-element.253.refs_0_), channel_id=1, source_target_pairs={{0,4},{1,5},{2,6},{3,7},{4,0},{5,1},{6,2},{7,3},{8,12},{9,13},{10,... | collective-permute-start | bytes 393224 | tf_op jit(solution)/shard_map/ppermute | solution.py:352
  129.8 19.6 %collective-permute-start.66 = (bf16[16,4096]{1,0:T(8,128)(2,1)S(1)}, bf16[16,4096]{1,0:T(8,128)(2,1)S(1)}, u32[]{:S(2)}, u32[]{:S(2)}) collective-permute-start(bf16[16,4096]{1,0:T(8,128)(2,1)S(1)} %get-tuple-element.253.refs_0_), channel_id=1, source_target_pairs={{0,1},{1,0},{2,3},{3,2},{4,5},{5,4},{6,7},{7,6},{8,9},{9,8},{10,11... | collective-permute-start | bytes 393224 | tf_op jit(solution)/shard_map/ppermute | solution.py:352
  146.7 5.2 %collective-permute-start.65 = (bf16[16,4096]{1,0:T(8,128)(2,1)S(1)}, bf16[16,4096]{1,0:T(8,128)(2,1)S(1)}, u32[]{:S(2)}, u32[]{:S(2)}) collective-permute-start(bf16[16,4096]{1,0:T(8,128)(2,1)S(1)} %collective-permute-done.63.refs_5_), channel_id=1, source_target_pairs={{0,2},{1,3},{2,0},{3,1},{4,6},{5,7},{6,4},{7,5},{8,10},{9,11},{10,... | collective-permute-start | bytes 393224 | tf_op jit(solution)/shard_map/ppermute | solution.py:352
  147.1 5.6 %collective-permute-start.68 = (bf16[16,4096]{1,0:T(8,128)(2,1)S(1)}, bf16[16,4096]{1,0:T(8,128)(2,1)S(1)}, u32[]{:S(2)}, u32[]{:S(2)}) collective-permute-start(bf16[16,4096]{1,0:T(8,128)(2,1)S(1)} %collective-permute-done.60.refs_2_), channel_id=1, source_target_pairs={{0,1},{1,0},{2,3},{3,2},{4,5},{5,4},{6,7},{7,6},{8,9},{9,8},{10,11... | collective-permute-start | bytes 393224 | tf_op jit(solution)/shard_map/ppermute | solution.py:352
  (36 other events, 231.0 us)

commit v7 on v6

--- a/solution.py
+++ b/solution.py
@@ -577,7 +577,12 @@
             )
         else:
             if step in (1, encoders + 1):
-                *near, mark = keep((wq, wq_other, wo, wo_other), unit_keys, range(step, sections))
+                arrays = (wq, wq_other, wo, wo_other)
+                if step > encoders:
+                    arrays += (unit_keys, values)
+                *near, mark = keep(arrays, unit_keys, range(step, sections))
+                if step > encoders:
+                    *near, unit_keys, values = near
                 shares[-1] = kernel_call(
                     pass_kernel, sds((piece, width)), [IN_VMEM] * 2, [], 4
                 )(shares[-1], mark)

time: 156 us -> 157 us (level)
  waiting for transfers between devices: 65.7 us -> 67.7 us
    ppermute x46, waiting for transfers between devices: 42.9 us -> 45 us  [flip(): return lambda x: lax.ppermute(x, 'seq', pairs)]
  transfers between devices with their start and end apart: 53 -> 53, of which waited for: 28 -> 27; matrix products, arithmetic and copies ran while one was open for 0% -> 0% of each run, Pallas kernels for 6% -> 6%
where the time goes in v7:
time: 157 us; the launch traced here: 156 us
  waiting for transfers between devices  67.7 us (43%)
  starting transfers between devices  57.9 us (37%)
  Pallas kernels  26.9 us (17%)
  local copies, waits for them, and re-layouts  3.25 us (2%)
    ppermute x46, starting transfers between devices, flip(): return lambda x: lax.ppermute(x, 'seq', pairs)  51.3 us
    ppermute x46, waiting for transfers between devices, flip(): return lambda x: lax.ppermute(x, 'seq', pairs)  45 us
    ppermute x7, waiting for transfers between devices, up(): return lax.ppermute(x, 'section', [(source, target)])  22.6 us
    pallas_call x2, Pallas kernels, keep(): kernel_call(functools.partial(body, config), [pltpu.VMEM(x.shape, BF16) f...  13.5 us
    ppermute x7, starting transfers between devices, up(): return lax.ppermute(x, 'section', [(source, target)])  6.57 us
    pallas_call x2, Pallas kernels, shards(): kernel_call(functools.partial(only_in([step])(section_kernel), config), p...  4.71 us
    pallas_call x1, Pallas kernels, project_memory(): kernel_call(functools.partial(memory_kernel, config), [sds((length, both)...  4.17 us
    another operation x7, local copies, waits for them, and re-layouts  3.22 us
  transfers between devices with their start and end apart: 53, of which 27 were waited for; matrix products, arithmetic and copies ran while one was open for 0% of the time, Pallas kernels for 6%

profile of v7, /device:TPU:25, one launch (start us, length us, event | category | flops | bytes accessed | tf_op | source)
XLA Modules:
  0.0 156.3 jit_solution(4076544154634170643)
XLA Ops:
  0.1 28.9 %conditional.2 = (bf16[32,4096]{1,0:T(8,128)(2,1)S(1)}, bf16[4096,512]{1,0:T(8,128)(2,1)}, bf16[4096,512]{1,0:T(8,128)(2,1)}, bf16[512,4096]{1,0:T(8,128)(2,1)},...) conditional(s32[]{:T(128)} %clamp.3, (s32[3]{0:T(128)S(1)}, ...), branch_computations={%region_0.1_spmd, %region_1.2_spmd, %region_2.3_spmd} | conditional | bytes 135528864 | solution.py:510
  1.4 6.4 %collective-permute-done.12 = bf16[4096,512]{1,0:T(8,128)(2,1)S(1)} collective-permute-done((bf16[4096,512]{1,0:T(8,128)(2,1)}, bf16[4096,512]{1,0:T(8,128)(2,1)S(1)}, u32[]{:S(2)}, u32[]{:S(2)}) %collective-permute-start.12) | collective-permute-done | bytes 4194336 | tf_op jit(solution)/shard_map/cond/branch_2_fun/ppermute | solution.py:352
  7.8 6.0 %collective-permute-done.13 = bf16[4096,512]{1,0:T(8,128)(2,1)S(1)} collective-permute-done((bf16[4096,512]{1,0:T(8,128)(2,1)}, bf16[4096,512]{1,0:T(8,128)(2,1)S(1)}, u32[]{:S(2)}, u32[]{:S(2)}) %collective-permute-start.13) | collective-permute-done | bytes 4194336 | tf_op jit(solution)/shard_map/cond/branch_2_fun/ppermute | solution.py:352
  13.8 6.0 %collective-permute-done.14 = bf16[512,4096]{1,0:T(8,128)(2,1)S(1)} collective-permute-done((bf16[512,4096]{1,0:T(8,128)(2,1)}, bf16[512,4096]{1,0:T(8,128)(2,1)S(1)}, u32[]{:S(2)}, u32[]{:S(2)}) %collective-permute-start.14) | collective-permute-done | bytes 4194336 | tf_op jit(solution)/shard_map/cond/branch_2_fun/ppermute | solution.py:352
  19.8 6.0 %collective-permute-done.15 = bf16[4096,512]{1,0:T(8,128)(2,1)S(1)} collective-permute-done((bf16[4096,512]{1,0:T(8,128)(2,1)}, bf16[4096,512]{1,0:T(8,128)(2,1)S(1)}, u32[]{:S(2)}, u32[]{:S(2)}) %collective-permute-start.15) | collective-permute-done | bytes 4194336 | tf_op jit(solution)/shard_map/cond/branch_2_fun/ppermute | solution.py:352
  31.1 34.7 %conditional.3 = (bf16[128,1024]{1,0:T(8,128)(2,1)}, bf16[128,1024]{1,0:T(8,128)(2,1)}, bf16[16,4096]{1,0:T(8,128)(2,1)S(1)}, bf16[16,4096]{1,0:T(8,128)(2,1)S(1)}) conditional(s32[]{:T(128)} %convert_element_type.3, (s32[]{:T(128)}, bf16[32,4096]{1,0:T(8,128)(2,1)S(1)}, s32[3]{0:T(128)S(1)}, bf16[4096,512]{1,0:T(8,128)(2,1)}, ...), branch_computations={%region_3.4_spmd, %region_4.5_spmd} | conditional | flops 131073 | bytes 58720760 | solution.py:573
  33.1 15.7 %collective-permute-done.26 = bf16[32,4096]{1,0:T(8,128)(2,1)S(1)} collective-permute-done((bf16[32,4096]{1,0:T(8,128)(2,1)S(1)}, bf16[32,4096]{1,0:T(8,128)(2,1)S(1)}, u32[]{:S(2)}, u32[]{:S(2)}) %collective-permute-start.26) | collective-permute-done | bytes 262176 | tf_op jit(solution)/shard_map/cond/branch_0_fun/ppermute | solution.py:355
  49.8 1.6 %collective-permute-start.28 = (bf16[32,4096]{1,0:T(8,128)(2,1)S(1)}, bf16[32,4096]{1,0:T(8,128)(2,1)S(1)}, u32[]{:S(2)}, u32[]{:S(2)}) collective-permute-start(bf16[32,4096]{1,0:T(8,128)(2,1)S(1)} %broadcast_select_fusion.refs_0_), channel_id=1, source_target_pairs={{0,4},{1,5},{2,6},{3,7},{4,0},{5,1},{6,2},{7,3},{8,12},{9,13},{10,... | collective-permute-start | bytes 786440 | tf_op jit(solution)/shard_map/cond/branch_0_fun/ppermute | solution.py:352
  51.6 7.0 %branch_0_fun.14 = (bf16[4096,512]{1,0:T(8,128)(2,1)S(1)}, bf16[4096,512]{1,0:T(8,128)(2,1)S(1)}, bf16[4096,512]{1,0:T(8,128)(2,1)S(1)}, bf16[4096,512]{1,0:T(8,128)(2,1)S(1)}, bf16[8,128]{1,0:T(8,128)(2,1)}) custom-call(s32[3]{0:T(128)S(1)} %get-tuple-element.135.place, bf16[4096,512]{1,0:T(8,128)(2,1)} %get-tuple-element.136.refs_0_, ...), custom_call_target="tpu_custom_call" | custom-call | bytes 33554432 | tf_op jit(solution)/shard_map/cond/branch_0_fun/pallas_call | solution.py:523
  58.6 2.9 %collective-permute-done.29.refs_3_ = bf16[32,4096]{1,0:T(8,128)(2,1)S(1)} collective-permute-done((bf16[32,4096]{1,0:T(8,128)(2,1)S(1)}, bf16[32,4096]{1,0:T(8,128)(2,1)S(1)}, u32[]{:S(2)}, u32[]{:S(2)}) %collective-permute-start.29) | collective-permute-done | bytes 262176 | tf_op jit(solution)/shard_map/cond/branch_0_fun/ppermute | solution.py:352
  61.5 4.2 %branch_0_fun.15 = (bf16[128,1024]{1,0:T(8,128)(2,1)}, bf16[128,1024]{1,0:T(8,128)(2,1)}) custom-call(s32[3]{0:T(128)S(1)} %get-tuple-element.135.place, f32[1,4096]{1,0:T(1,128)S(1)} %get-tuple-element.132.gain, bf16[32,4096]{1,0:T(8,128)(2,1)S(1)} %broadcast_select_fusion.refs_0_, bf16[32,4096]{1,0:T(8,128)(2,1)S(1)} %collective-permute-done.27.refs_1_, ...), custom_call_target="tpu_custom_call" | custom-call | tf_op jit(solution)/shard_map/cond/branch_0_fun/pallas_call | solution.py:533
  65.9 6.5 %shard_map.93 = (bf16[4096,512]{1,0:T(8,128)(2,1)S(1)}, bf16[4096,512]{1,0:T(8,128)(2,1)S(1)}, bf16[512,4096]{1,0:T(8,128)(2,1)S(1)}, bf16[512,4096]{1,0:T(8,128...) custom-call(s32[3]{0:T(128)S(1)} %pad_add_fusion.place, ...), custom_call_target="tpu_custom_call" | custom-call | bytes 50331648 | tf_op jit(solution)/shard_map/pallas_call | solution.py:523
  79.3 2.6 %collective-permute-done.39.refs_10_ = bf16[16,4096]{1,0:T(8,128)(2,1)S(1)} collective-permute-done((bf16[16,4096]{1,0:T(8,128)(2,1)S(1)}, bf16[16,4096]{1,0:T(8,128)(2,1)S(1)}, u32[]{:S(2)}, u32[]{:S(2)}) %collective-permute-start.39) | collective-permute-done | bytes 131104 | tf_op jit(solution)/shard_map/ppermute | solution.py:352
  83.5 1.8 %collective-permute-start.40 = (bf16[16,4096]{1,0:T(8,128)(2,1)S(1)}, bf16[16,4096]{1,0:T(8,128)(2,1)S(1)}, u32[]{:S(2)}, u32[]{:S(2)}) collective-permute-start(bf16[16,4096]{1,0:T(8,128)(2,1)S(1)} %get-tuple-element.237), channel_id=1, source_target_pairs={{0,6},{1,7},{2,4},{3,5},{4,2},{5,3},{6,0},{7,1},{8,14},{9,15},{10,... | collective-permute-start | bytes 393224 | tf_op jit(solution)/shard_map/ppermute | solution.py:352
  86.3 1.7 %collective-permute-start.44 = (bf16[16,4096]{1,0:T(8,128)(2,1)S(1)}, bf16[16,4096]{1,0:T(8,128)(2,1)S(1)}, u32[]{:S(2)}, u32[]{:S(2)}) collective-permute-start(bf16[16,4096]{1,0:T(8,128)(2,1)S(1)} %get-tuple-element.241), channel_id=1, source_target_pairs={{0,6},{1,7},{2,4},{3,5},{4,2},{5,3},{6,0},{7,1},{8,14},{9,15},{10,... | collective-permute-start | bytes 393224 | tf_op jit(solution)/shard_map/ppermute | solution.py:352
  95.4 4.5 %collective-permute-done.43.refs_3_.refs_0_ = bf16[16,4096]{1,0:T(8,128)(2,1)S(1)} collective-permute-done((bf16[16,4096]{1,0:T(8,128)(2,1)S(1)}, bf16[16,4096]{1,0:T(8,128)(2,1)S(1)}, u32[]{:S(2)}, u32[]{:S(2)}) %collective-permute-start.43) | collective-permute-done | bytes 131104 | tf_op jit(solution)/shard_map/ppermute | solution.py:355
  100.3 2.5 %collective-permute-done.47.refs_4_.refs_0_ = bf16[16,4096]{1,0:T(8,128)(2,1)S(1)} collective-permute-done((bf16[16,4096]{1,0:T(8,128)(2,1)S(1)}, bf16[16,4096]{1,0:T(8,128)(2,1)S(1)}, u32[]{:S(2)}, u32[]{:S(2)}) %collective-permute-start.47) | collective-permute-done | bytes 131104 | tf_op jit(solution)/shard_map/ppermute | solution.py:355
  109.4 1.6 %collective-permute-done.53.refs_10_ = bf16[16,4096]{1,0:T(8,128)(2,1)S(1)} collective-permute-done((bf16[16,4096]{1,0:T(8,128)(2,1)S(1)}, bf16[16,4096]{1,0:T(8,128)(2,1)S(1)}, u32[]{:S(2)}, u32[]{:S(2)}) %collective-permute-start.53) | collective-permute-done | bytes 131104 | tf_op jit(solution)/shard_map/ppermute | solution.py:352
  111.1 4.2 %shard_map.98 = (bf16[16,4096]{1,0:T(8,128)(2,1)S(1)}, bf16[16,4096]{1,0:T(8,128)(2,1)S(1)}, bf16[16,4096]{1,0:T(8,128)(2,1)S(1)}, bf16[16,4096]{1,0:T(8,128)(2,...) custom-call(s32[3]{0:T(128)S(1)} %pad_add_fusion.place, ...), custom_call_target="tpu_custom_call" | custom-call | tf_op jit(solution)/shard_map/pallas_call | solution.py:594
  123.5 2.1 %collective-permute-done.57.refs_2_ = bf16[16,4096]{1,0:T(8,128)(2,1)S(1)} collective-permute-done((bf16[16,4096]{1,0:T(8,128)(2,1)S(1)}, bf16[16,4096]{1,0:T(8,128)(2,1)S(1)}, u32[]{:S(2)}, u32[]{:S(2)}) %collective-permute-start.57) | collective-permute-done | bytes 131104 | tf_op jit(solution)/shard_map/ppermute | solution.py:352
  129.5 15.4 %collective-permute-start.66 = (bf16[16,4096]{1,0:T(8,128)(2,1)S(1)}, bf16[16,4096]{1,0:T(8,128)(2,1)S(1)}, u32[]{:S(2)}, u32[]{:S(2)}) collective-permute-start(bf16[16,4096]{1,0:T(8,128)(2,1)S(1)} %get-tuple-element.257.refs_0_), channel_id=1, source_target_pairs={{0,1},{1,0},{2,3},{3,2},{4,5},{5,4},{6,7},{7,6},{8,9},{9,8},{10,11... | collective-permute-start | bytes 393224 | tf_op jit(solution)/shard_map/ppermute | solution.py:352
  147.4 1.6 %collective-permute-start.68 = (bf16[16,4096]{1,0:T(8,128)(2,1)S(1)}, bf16[16,4096]{1,0:T(8,128)(2,1)S(1)}, u32[]{:S(2)}, u32[]{:S(2)}) collective-permute-start(bf16[16,4096]{1,0:T(8,128)(2,1)S(1)} %collective-permute-done.60.refs_2_), channel_id=1, source_target_pairs={{0,1},{1,0},{2,3},{3,2},{4,5},{5,4},{6,7},{7,6},{8,9},{9,8},{10,11... | collective-permute-start | bytes 393224 | tf_op jit(solution)/shard_map/ppermute | solution.py:352
  149.8 2.2 %collective-permute-start.70 = (bf16[16,4096]{1,0:T(8,128)(2,1)S(1)}, bf16[16,4096]{1,0:T(8,128)(2,1)S(1)}, u32[]{:S(2)}, u32[]{:S(2)}) collective-permute-start(bf16[16,4096]{1,0:T(8,128)(2,1)S(1)} %collective-permute-done.62.refs_4_), channel_id=1, source_target_pairs={{0,1},{1,0},{2,3},{3,2},{4,5},{5,4},{6,7},{7,6},{8,9},{9,8},{10,11... | collective-permute-start | bytes 393224 | tf_op jit(solution)/shard_map/ppermute | solution.py:352
  154.3 2.0 %shard_map.101 = bf16[2,128,4096]{2,1,0:T(8,128)(2,1)} custom-call(s32[3]{0:T(128)S(1)} %pad_add_fusion.place, bf16[16,4096]{1,0:T(8,128)(2,1)S(1)} %get-tuple-element.257.refs_0_, bf16[16,4096]{1,0:T(8,128)(2,1)S(1)} %get-tuple-element.256.refs_1_, bf16[16,4096]{1,0:T(8,128)(2,1)S(1)} %collective-permute-done.60.refs_2_, ...), custom_call_target="tpu_custom_call" | custom-call | tf_op jit(solution)/shard_map/pallas_call | solution.py:606
  (119 shorter events, 51.3 us)
Async XLA Ops:
  0.1 7.7 %collective-permute-start.12 = (bf16[4096,512]{1,0:T(8,128)(2,1)}, bf16[4096,512]{1,0:T(8,128)(2,1)S(1)}, u32[]{:S(2)}, u32[]{:S(2)}) collective-permute-start(bf16[4096,512]{1,0:T(8,128)(2,1)} %get-tuple-element.127), channel_id=1, source_target_pairs={{0,1},{1,0},{2,3},{3,2},{4,5},{5,4},{6,7},{7,6},{8,9},{9,8},{10,11... | collective-permute-start | bytes 12582920 | tf_op jit(solution)/shard_map/cond/branch_2_fun/ppermute | solution.py:352
  0.8 13.0 %collective-permute-start.13 = (bf16[4096,512]{1,0:T(8,128)(2,1)}, bf16[4096,512]{1,0:T(8,128)(2,1)S(1)}, u32[]{:S(2)}, u32[]{:S(2)}) collective-permute-start(bf16[4096,512]{1,0:T(8,128)(2,1)} %get-tuple-element.128), channel_id=1, source_target_pairs={{0,1},{1,0},{2,3},{3,2},{4,5},{5,4},{6,7},{7,6},{8,9},{9,8},{10,11... | collective-permute-start | bytes 12582920 | tf_op jit(solution)/shard_map/cond/branch_2_fun/ppermute | solution.py:352
  0.9 18.9 %collective-permute-start.14 = (bf16[512,4096]{1,0:T(8,128)(2,1)}, bf16[512,4096]{1,0:T(8,128)(2,1)S(1)}, u32[]{:S(2)}, u32[]{:S(2)}) collective-permute-start(bf16[512,4096]{1,0:T(8,128)(2,1)} %get-tuple-element.129), channel_id=1, source_target_pairs={{0,1},{1,0},{2,3},{3,2},{4,5},{5,4},{6,7},{7,6},{8,9},{9,8},{10,11... | collective-permute-start | bytes 12582920 | tf_op jit(solution)/shard_map/cond/branch_2_fun/ppermute | solution.py:352
  1.3 24.5 %collective-permute-start.15 = (bf16[4096,512]{1,0:T(8,128)(2,1)}, bf16[4096,512]{1,0:T(8,128)(2,1)S(1)}, u32[]{:S(2)}, u32[]{:S(2)}) collective-permute-start(bf16[4096,512]{1,0:T(8,128)(2,1)} %get-tuple-element.130), channel_id=1, source_target_pairs={{0,1},{1,0},{2,3},{3,2},{4,5},{5,4},{6,7},{7,6},{8,9},{9,8},{10,11... | collective-permute-start | bytes 12582920 | tf_op jit(solution)/shard_map/cond/branch_2_fun/ppermute | solution.py:352
  31.8 17.0 %collective-permute-start.26 = (bf16[32,4096]{1,0:T(8,128)(2,1)S(1)}, bf16[32,4096]{1,0:T(8,128)(2,1)S(1)}, u32[]{:S(2)}, u32[]{:S(2)}) collective-permute-start(bf16[32,4096]{1,0:T(8,128)(2,1)S(1)} %get-tuple-element.134), channel_id=1, source_target_pairs={{0,24},{1,25},{2,26},{3,27},{4,28},{5,29},{6,30},{7,31}} | collective-permute-start | bytes 786440 | tf_op jit(solution)/shard_map/cond/branch_0_fun/ppermute | solution.py:355
  48.8 9.7 %collective-permute-start.27 = (bf16[32,4096]{1,0:T(8,128)(2,1)S(1)}, bf16[32,4096]{1,0:T(8,128)(2,1)S(1)}, u32[]{:S(2)}, u32[]{:S(2)}) collective-permute-start(bf16[32,4096]{1,0:T(8,128)(2,1)S(1)} %broadcast_select_fusion.refs_0_), channel_id=1, source_target_pairs={{0,2},{1,3},{2,0},{3,1},{4,6},{5,7},{6,4},{7,5},{8,10},{9,11},{10,... | collective-permute-start | bytes 786440 | tf_op jit(solution)/shard_map/cond/branch_0_fun/ppermute | solution.py:352
  49.8 8.8 %collective-permute-start.28 = (bf16[32,4096]{1,0:T(8,128)(2,1)S(1)}, bf16[32,4096]{1,0:T(8,128)(2,1)S(1)}, u32[]{:S(2)}, u32[]{:S(2)}) collective-permute-start(bf16[32,4096]{1,0:T(8,128)(2,1)S(1)} %broadcast_select_fusion.refs_0_), channel_id=1, source_target_pairs={{0,4},{1,5},{2,6},{3,7},{4,0},{5,1},{6,2},{7,3},{8,12},{9,13},{10,... | collective-permute-start | bytes 786440 | tf_op jit(solution)/shard_map/cond/branch_0_fun/ppermute | solution.py:352
  51.4 10.1 %collective-permute-start.29 = (bf16[32,4096]{1,0:T(8,128)(2,1)S(1)}, bf16[32,4096]{1,0:T(8,128)(2,1)S(1)}, u32[]{:S(2)}, u32[]{:S(2)}) collective-permute-start(bf16[32,4096]{1,0:T(8,128)(2,1)S(1)} %broadcast_select_fusion.refs_0_), channel_id=1, source_target_pairs={{0,6},{1,7},{2,4},{3,5},{4,2},{5,3},{6,0},{7,1},{8,14},{9,15},{10,... | collective-permute-start | bytes 786440 | tf_op jit(solution)/shard_map/cond/branch_0_fun/ppermute | solution.py:352
  83.5 5.8 %collective-permute-start.40 = (bf16[16,4096]{1,0:T(8,128)(2,1)S(1)}, bf16[16,4096]{1,0:T(8,128)(2,1)S(1)}, u32[]{:S(2)}, u32[]{:S(2)}) collective-permute-start(bf16[16,4096]{1,0:T(8,128)(2,1)S(1)} %get-tuple-element.237), channel_id=1, source_target_pairs={{0,6},{1,7},{2,4},{3,5},{4,2},{5,3},{6,0},{7,1},{8,14},{9,15},{10,... | collective-permute-start | bytes 393224 | tf_op jit(solution)/shard_map/ppermute | solution.py:352
  85.4 5.8 %collective-permute-start.41 = (bf16[16,4096]{1,0:T(8,128)(2,1)S(1)}, bf16[16,4096]{1,0:T(8,128)(2,1)S(1)}, u32[]{:S(2)}, u32[]{:S(2)}) collective-permute-start(bf16[16,4096]{1,0:T(8,128)(2,1)S(1)} %get-tuple-element.238), channel_id=1, source_target_pairs={{0,4},{1,5},{2,6},{3,7},{4,0},{5,1},{6,2},{7,3},{8,12},{9,13},{10,... | collective-permute-start | bytes 393224 | tf_op jit(solution)/shard_map/ppermute | solution.py:352
  86.3 6.8 %collective-permute-start.44 = (bf16[16,4096]{1,0:T(8,128)(2,1)S(1)}, bf16[16,4096]{1,0:T(8,128)(2,1)S(1)}, u32[]{:S(2)}, u32[]{:S(2)}) collective-permute-start(bf16[16,4096]{1,0:T(8,128)(2,1)S(1)} %get-tuple-element.241), channel_id=1, source_target_pairs={{0,6},{1,7},{2,4},{3,5},{4,2},{5,3},{6,0},{7,1},{8,14},{9,15},{10,... | collective-permute-start | bytes 393224 | tf_op jit(solution)/shard_map/ppermute | solution.py:352
  91.8 8.1 %collective-permute-start.43 = (bf16[16,4096]{1,0:T(8,128)(2,1)S(1)}, bf16[16,4096]{1,0:T(8,128)(2,1)S(1)}, u32[]{:S(2)}, u32[]{:S(2)}) collective-permute-start(bf16[16,4096]{1,0:T(8,128)(2,1)S(1)} %shard_map.96), channel_id=1, source_target_pairs={{16,24},{17,25},{18,26},{19,27},{20,28},{21,29},{22,30},{23,31}} | collective-permute-start | bytes 393224 | tf_op jit(solution)/shard_map/ppermute | solution.py:355
  94.1 8.7 %collective-permute-start.47 = (bf16[16,4096]{1,0:T(8,128)(2,1)S(1)}, bf16[16,4096]{1,0:T(8,128)(2,1)S(1)}, u32[]{:S(2)}, u32[]{:S(2)}) collective-permute-start(bf16[16,4096]{1,0:T(8,128)(2,1)S(1)} %shard_map.97), channel_id=1, source_target_pairs={{16,24},{17,25},{18,26},{19,27},{20,28},{21,29},{22,30},{23,31}} | collective-permute-start | bytes 393224 | tf_op jit(solution)/shard_map/ppermute | solution.py:355
  99.9 5.5 %collective-permute-start.48 = (bf16[16,4096]{1,0:T(8,128)(2,1)S(1)}, bf16[16,4096]{1,0:T(8,128)(2,1)S(1)}, u32[]{:S(2)}, u32[]{:S(2)}) collective-permute-start(bf16[16,4096]{1,0:T(8,128)(2,1)S(1)} %collective-permute-done.43.refs_3_.refs_0_), channel_id=1, source_target_pairs={{0,2},{1,3},{2,0},{3,1},{4,6},{5,7},{6,4},{7,5},{8,10},{9,11},{10,... | collective-permute-start | bytes 393224 | tf_op jit(solution)/shard_map/ppermute | solution.py:352
  115.2 6.2 %collective-permute-start.54 = (bf16[16,4096]{1,0:T(8,128)(2,1)S(1)}, bf16[16,4096]{1,0:T(8,128)(2,1)S(1)}, u32[]{:S(2)}, u32[]{:S(2)}) collective-permute-start(bf16[16,4096]{1,0:T(8,128)(2,1)S(1)} %get-tuple-element.245), channel_id=1, source_target_pairs={{0,6},{1,7},{2,4},{3,5},{4,2},{5,3},{6,0},{7,1},{8,14},{9,15},{10,... | collective-permute-start | bytes 393224 | tf_op jit(solution)/shard_map/ppermute | solution.py:352
  116.2 6.7 %collective-permute-start.55 = (bf16[16,4096]{1,0:T(8,128)(2,1)S(1)}, bf16[16,4096]{1,0:T(8,128)(2,1)S(1)}, u32[]{:S(2)}, u32[]{:S(2)}) collective-permute-start(bf16[16,4096]{1,0:T(8,128)(2,1)S(1)} %get-tuple-element.246), channel_id=1, source_target_pairs={{0,4},{1,5},{2,6},{3,7},{4,0},{5,1},{6,2},{7,3},{8,12},{9,13},{10,... | collective-permute-start | bytes 393224 | tf_op jit(solution)/shard_map/ppermute | solution.py:352
  117.9 7.7 %collective-permute-start.57 = (bf16[16,4096]{1,0:T(8,128)(2,1)S(1)}, bf16[16,4096]{1,0:T(8,128)(2,1)S(1)}, u32[]{:S(2)}, u32[]{:S(2)}) collective-permute-start(bf16[16,4096]{1,0:T(8,128)(2,1)S(1)} %get-tuple-element.249), channel_id=1, source_target_pairs={{0,6},{1,7},{2,4},{3,5},{4,2},{5,3},{6,0},{7,1},{8,14},{9,15},{10,... | collective-permute-start | bytes 393224 | tf_op jit(solution)/shard_map/ppermute | solution.py:352
  118.8 6.8 %collective-permute-start.58 = (bf16[16,4096]{1,0:T(8,128)(2,1)S(1)}, bf16[16,4096]{1,0:T(8,128)(2,1)S(1)}, u32[]{:S(2)}, u32[]{:S(2)}) collective-permute-start(bf16[16,4096]{1,0:T(8,128)(2,1)S(1)} %get-tuple-element.250), channel_id=1, source_target_pairs={{0,4},{1,5},{2,6},{3,7},{4,0},{5,1},{6,2},{7,3},{8,12},{9,13},{10,... | collective-permute-start | bytes 393224 | tf_op jit(solution)/shard_map/ppermute | solution.py:352
  126.4 18.6 %collective-permute-start.60 = (bf16[16,4096]{1,0:T(8,128)(2,1)S(1)}, bf16[16,4096]{1,0:T(8,128)(2,1)S(1)}, u32[]{:S(2)}, u32[]{:S(2)}) collective-permute-start(bf16[16,4096]{1,0:T(8,128)(2,1)S(1)} %get-tuple-element.257.refs_0_), channel_id=1, source_target_pairs={{0,2},{1,3},{2,0},{3,1},{4,6},{5,7},{6,4},{7,5},{8,10},{9,11},{10,... | collective-permute-start | bytes 393224 | tf_op jit(solution)/shard_map/ppermute | solution.py:352
  127.8 18.1 %collective-permute-start.63 = (bf16[16,4096]{1,0:T(8,128)(2,1)S(1)}, bf16[16,4096]{1,0:T(8,128)(2,1)S(1)}, u32[]{:S(2)}, u32[]{:S(2)}) collective-permute-start(bf16[16,4096]{1,0:T(8,128)(2,1)S(1)} %get-tuple-element.256.refs_1_), channel_id=1, source_target_pairs={{0,4},{1,5},{2,6},{3,7},{4,0},{5,1},{6,2},{7,3},{8,12},{9,13},{10,... | collective-permute-start | bytes 393224 | tf_op jit(solution)/shard_map/ppermute | solution.py:352
  128.9 17.9 %collective-permute-start.61 = (bf16[16,4096]{1,0:T(8,128)(2,1)S(1)}, bf16[16,4096]{1,0:T(8,128)(2,1)S(1)}, u32[]{:S(2)}, u32[]{:S(2)}) collective-permute-start(bf16[16,4096]{1,0:T(8,128)(2,1)S(1)} %get-tuple-element.256.refs_1_), channel_id=1, source_target_pairs={{0,2},{1,3},{2,0},{3,1},{4,6},{5,7},{6,4},{7,5},{8,10},{9,11},{10,... | collective-permute-start | bytes 393224 | tf_op jit(solution)/shard_map/ppermute | solution.py:352
  129.5 17.9 %collective-permute-start.62 = (bf16[16,4096]{1,0:T(8,128)(2,1)S(1)}, bf16[16,4096]{1,0:T(8,128)(2,1)S(1)}, u32[]{:S(2)}, u32[]{:S(2)}) collective-permute-start(bf16[16,4096]{1,0:T(8,128)(2,1)S(1)} %get-tuple-element.257.refs_0_), channel_id=1, source_target_pairs={{0,4},{1,5},{2,6},{3,7},{4,0},{5,1},{6,2},{7,3},{8,12},{9,13},{10,... | collective-permute-start | bytes 393224 | tf_op jit(solution)/shard_map/ppermute | solution.py:352
  129.5 19.5 %collective-permute-start.66 = (bf16[16,4096]{1,0:T(8,128)(2,1)S(1)}, bf16[16,4096]{1,0:T(8,128)(2,1)S(1)}, u32[]{:S(2)}, u32[]{:S(2)}) collective-permute-start(bf16[16,4096]{1,0:T(8,128)(2,1)S(1)} %get-tuple-element.257.refs_0_), channel_id=1, source_target_pairs={{0,1},{1,0},{2,3},{3,2},{4,5},{5,4},{6,7},{7,6},{8,9},{9,8},{10,11... | collective-permute-start | bytes 393224 | tf_op jit(solution)/shard_map/ppermute | solution.py:352
  147.4 5.5 %collective-permute-start.68 = (bf16[16,4096]{1,0:T(8,128)(2,1)S(1)}, bf16[16,4096]{1,0:T(8,128)(2,1)S(1)}, u32[]{:S(2)}, u32[]{:S(2)}) collective-permute-start(bf16[16,4096]{1,0:T(8,128)(2,1)S(1)} %collective-permute-done.60.refs_2_), channel_id=1, source_target_pairs={{0,1},{1,0},{2,3},{3,2},{4,5},{5,4},{6,7},{7,6},{8,9},{9,8},{10,11... | collective-permute-start | bytes 393224 | tf_op jit(solution)/shard_map/ppermute | solution.py:352
  (36 other events, 233.3 us)

commit v8 on v6

--- a/solution.py
+++ b/solution.py
@@ -383,8 +383,8 @@
     def gather(shares):
         if blocks == 4 and len(shares) == 2:
             first, second = shares
-            x_first, y_second = to_chip[1](first), to_chip[2](second)
-            y_first, x_second = to_chip[2](first), to_chip[1](second)
+            x_first, y_first = to_chip[1](first), to_chip[2](first)
+            y_second, x_second = to_chip[2](second), to_chip[1](second)
             by_group = [
                 [first, x_first, y_first, to_chip[2](x_first)],
                 [second, x_second, y_second, to_chip[1](y_second)],

time: 156 us -> 156 us (level)
  no operation moved by 1% of the time
where the time goes in v8:
time: 156 us
  waiting for transfers between devices  65.7 us (42%)
  starting transfers between devices  58.6 us (38%)
  Pallas kernels  27.8 us (18%)
  local copies, waits for them, and re-layouts  3.25 us (2%)
    ppermute x46, starting transfers between devices, flip(): return lambda x: lax.ppermute(x, 'seq', pairs)  52 us
    ppermute x46, waiting for transfers between devices, flip(): return lambda x: lax.ppermute(x, 'seq', pairs)  42.9 us
    ppermute x7, waiting for transfers between devices, up(): return lax.ppermute(x, 'section', [(source, target)])  22.8 us
    pallas_call x2, Pallas kernels, keep(): kernel_call(functools.partial(body, config), [pltpu.VMEM(x.shape, BF16) f...  13.4 us
    ppermute x7, starting transfers between devices, up(): return lax.ppermute(x, 'section', [(source, target)])  6.57 us
    pallas_call x2, Pallas kernels, shards(): kernel_call(functools.partial(only_in([step])(section_kernel), config), p...  5.69 us
    pallas_call x1, Pallas kernels, project_memory(): kernel_call(functools.partial(memory_kernel, config), [sds((length, both)...  4.17 us
    another operation x7, local copies, waits for them, and re-layouts  3.22 us
  transfers between devices with their start and end apart: 53, of which 28 were waited for; matrix products, arithmetic and copies ran while one was open for 0% of the time, Pallas kernels for 6%

profile of v8, /device:TPU:25, one launch (start us, length us, event | category | flops | bytes accessed | tf_op | source)
XLA Modules:
  0.0 156.0 jit_solution(8628213888550412764)
XLA Ops:
  0.1 28.9 %conditional.2 = (bf16[32,4096]{1,0:T(8,128)(2,1)S(1)}, bf16[4096,512]{1,0:T(8,128)(2,1)}, bf16[4096,512]{1,0:T(8,128)(2,1)}, bf16[512,4096]{1,0:T(8,128)(2,1)},...) conditional(s32[]{:T(128)} %clamp.3, (s32[3]{0:T(128)S(1)}, ...), branch_computations={%region_0.1_spmd, %region_1.2_spmd, %region_2.3_spmd} | conditional | bytes 135528864 | solution.py:510
  1.4 6.4 %collective-permute-done.12 = bf16[4096,512]{1,0:T(8,128)(2,1)S(1)} collective-permute-done((bf16[4096,512]{1,0:T(8,128)(2,1)}, bf16[4096,512]{1,0:T(8,128)(2,1)S(1)}, u32[]{:S(2)}, u32[]{:S(2)}) %collective-permute-start.12) | collective-permute-done | bytes 4194336 | tf_op jit(solution)/shard_map/cond/branch_2_fun/ppermute | solution.py:352
  7.8 6.0 %collective-permute-done.13 = bf16[4096,512]{1,0:T(8,128)(2,1)S(1)} collective-permute-done((bf16[4096,512]{1,0:T(8,128)(2,1)}, bf16[4096,512]{1,0:T(8,128)(2,1)S(1)}, u32[]{:S(2)}, u32[]{:S(2)}) %collective-permute-start.13) | collective-permute-done | bytes 4194336 | tf_op jit(solution)/shard_map/cond/branch_2_fun/ppermute | solution.py:352
  13.8 6.0 %collective-permute-done.14 = bf16[512,4096]{1,0:T(8,128)(2,1)S(1)} collective-permute-done((bf16[512,4096]{1,0:T(8,128)(2,1)}, bf16[512,4096]{1,0:T(8,128)(2,1)S(1)}, u32[]{:S(2)}, u32[]{:S(2)}) %collective-permute-start.14) | collective-permute-done | bytes 4194336 | tf_op jit(solution)/shard_map/cond/branch_2_fun/ppermute | solution.py:352
  19.8 6.0 %collective-permute-done.15 = bf16[4096,512]{1,0:T(8,128)(2,1)S(1)} collective-permute-done((bf16[4096,512]{1,0:T(8,128)(2,1)}, bf16[4096,512]{1,0:T(8,128)(2,1)S(1)}, u32[]{:S(2)}, u32[]{:S(2)}) %collective-permute-start.15) | collective-permute-done | bytes 4194336 | tf_op jit(solution)/shard_map/cond/branch_2_fun/ppermute | solution.py:352
  31.1 34.7 %conditional.3 = (bf16[128,1024]{1,0:T(8,128)(2,1)}, bf16[128,1024]{1,0:T(8,128)(2,1)}, bf16[16,4096]{1,0:T(8,128)(2,1)S(1)}, bf16[16,4096]{1,0:T(8,128)(2,1)S(1)}) conditional(s32[]{:T(128)} %convert_element_type.3, (s32[]{:T(128)}, bf16[32,4096]{1,0:T(8,128)(2,1)S(1)}, s32[3]{0:T(128)S(1)}, bf16[4096,512]{1,0:T(8,128)(2,1)}, ...), branch_computations={%region_3.4_spmd, %region_4.5_spmd} | conditional | flops 131073 | bytes 58720760 | solution.py:573
  33.1 15.7 %collective-permute-done.26 = bf16[32,4096]{1,0:T(8,128)(2,1)S(1)} collective-permute-done((bf16[32,4096]{1,0:T(8,128)(2,1)S(1)}, bf16[32,4096]{1,0:T(8,128)(2,1)S(1)}, u32[]{:S(2)}, u32[]{:S(2)}) %collective-permute-start.26) | collective-permute-done | bytes 262176 | tf_op jit(solution)/shard_map/cond/branch_0_fun/ppermute | solution.py:355
  49.8 1.6 %collective-permute-start.28 = (bf16[32,4096]{1,0:T(8,128)(2,1)S(1)}, bf16[32,4096]{1,0:T(8,128)(2,1)S(1)}, u32[]{:S(2)}, u32[]{:S(2)}) collective-permute-start(bf16[32,4096]{1,0:T(8,128)(2,1)S(1)} %broadcast_select_fusion.refs_0_), channel_id=1, source_target_pairs={{0,4},{1,5},{2,6},{3,7},{4,0},{5,1},{6,2},{7,3},{8,12},{9,13},{10,... | collective-permute-start | bytes 786440 | tf_op jit(solution)/shard_map/cond/branch_0_fun/ppermute | solution.py:352
  51.6 7.0 %branch_0_fun.14 = (bf16[4096,512]{1,0:T(8,128)(2,1)S(1)}, bf16[4096,512]{1,0:T(8,128)(2,1)S(1)}, bf16[4096,512]{1,0:T(8,128)(2,1)S(1)}, bf16[4096,512]{1,0:T(8,128)(2,1)S(1)}, bf16[8,128]{1,0:T(8,128)(2,1)}) custom-call(s32[3]{0:T(128)S(1)} %get-tuple-element.135.place, bf16[4096,512]{1,0:T(8,128)(2,1)} %get-tuple-element.136.refs_0_, ...), custom_call_target="tpu_custom_call" | custom-call | bytes 33554432 | tf_op jit(solution)/shard_map/cond/branch_0_fun/pallas_call | solution.py:523
  58.6 2.9 %collective-permute-done.29.refs_3_ = bf16[32,4096]{1,0:T(8,128)(2,1)S(1)} collective-permute-done((bf16[32,4096]{1,0:T(8,128)(2,1)S(1)}, bf16[32,4096]{1,0:T(8,128)(2,1)S(1)}, u32[]{:S(2)}, u32[]{:S(2)}) %collective-permute-start.29) | collective-permute-done | bytes 262176 | tf_op jit(solution)/shard_map/cond/branch_0_fun/ppermute | solution.py:352
  61.5 4.2 %branch_0_fun.15 = (bf16[128,1024]{1,0:T(8,128)(2,1)}, bf16[128,1024]{1,0:T(8,128)(2,1)}) custom-call(s32[3]{0:T(128)S(1)} %get-tuple-element.135.place, f32[1,4096]{1,0:T(1,128)S(1)} %get-tuple-element.132.gain, bf16[32,4096]{1,0:T(8,128)(2,1)S(1)} %broadcast_select_fusion.refs_0_, bf16[32,4096]{1,0:T(8,128)(2,1)S(1)} %collective-permute-done.27.refs_1_, ...), custom_call_target="tpu_custom_call" | custom-call | tf_op jit(solution)/shard_map/cond/branch_0_fun/pallas_call | solution.py:533
  65.9 6.4 %shard_map.93 = (bf16[4096,512]{1,0:T(8,128)(2,1)S(1)}, bf16[4096,512]{1,0:T(8,128)(2,1)S(1)}, bf16[512,4096]{1,0:T(8,128)(2,1)S(1)}, bf16[512,4096]{1,0:T(8,128)(2,1)S(1)}, bf16[8,128]{1,0:T(8,128)(2,1)S(1)}) custom-call(s32[3]{0:T(128)S(1)} %pad_add_fusion.place, bf16[4096,512]{1,0:T(8,128)(2,1)} %bitcast.13, ...), custom_call_target="tpu_custom_call" | custom-call | bytes 33554432 | tf_op jit(solution)/shard_map/pallas_call | solution.py:523
  79.3 2.6 %collective-permute-done.39.refs_10_ = bf16[16,4096]{1,0:T(8,128)(2,1)S(1)} collective-permute-done((bf16[16,4096]{1,0:T(8,128)(2,1)S(1)}, bf16[16,4096]{1,0:T(8,128)(2,1)S(1)}, u32[]{:S(2)}, u32[]{:S(2)}) %collective-permute-start.39) | collective-permute-done | bytes 131104 | tf_op jit(solution)/shard_map/ppermute | solution.py:352
  84.0 1.8 %collective-permute-start.40 = (bf16[16,4096]{1,0:T(8,128)(2,1)S(1)}, bf16[16,4096]{1,0:T(8,128)(2,1)S(1)}, u32[]{:S(2)}, u32[]{:S(2)}) collective-permute-start(bf16[16,4096]{1,0:T(8,128)(2,1)S(1)} %get-tuple-element.233), channel_id=1, source_target_pairs={{0,6},{1,7},{2,4},{3,5},{4,2},{5,3},{6,0},{7,1},{8,14},{9,15},{10,... | collective-permute-start | bytes 393224 | tf_op jit(solution)/shard_map/ppermute | solution.py:352
  86.7 1.7 %collective-permute-start.44 = (bf16[16,4096]{1,0:T(8,128)(2,1)S(1)}, bf16[16,4096]{1,0:T(8,128)(2,1)S(1)}, u32[]{:S(2)}, u32[]{:S(2)}) collective-permute-start(bf16[16,4096]{1,0:T(8,128)(2,1)S(1)} %get-tuple-element.237), channel_id=1, source_target_pairs={{0,6},{1,7},{2,4},{3,5},{4,2},{5,3},{6,0},{7,1},{8,14},{9,15},{10,... | collective-permute-start | bytes 393224 | tf_op jit(solution)/shard_map/ppermute | solution.py:352
  95.5 4.9 %collective-permute-done.43.refs_3_.refs_0_ = bf16[16,4096]{1,0:T(8,128)(2,1)S(1)} collective-permute-done((bf16[16,4096]{1,0:T(8,128)(2,1)S(1)}, bf16[16,4096]{1,0:T(8,128)(2,1)S(1)}, u32[]{:S(2)}, u32[]{:S(2)}) %collective-permute-start.43) | collective-permute-done | bytes 131104 | tf_op jit(solution)/shard_map/ppermute | solution.py:355
  100.8 2.2 %collective-permute-done.47.refs_4_.refs_0_ = bf16[16,4096]{1,0:T(8,128)(2,1)S(1)} collective-permute-done((bf16[16,4096]{1,0:T(8,128)(2,1)S(1)}, bf16[16,4096]{1,0:T(8,128)(2,1)S(1)}, u32[]{:S(2)}, u32[]{:S(2)}) %collective-permute-start.47) | collective-permute-done | bytes 131104 | tf_op jit(solution)/shard_map/ppermute | solution.py:355
  109.6 1.6 %collective-permute-done.53.refs_10_ = bf16[16,4096]{1,0:T(8,128)(2,1)S(1)} collective-permute-done((bf16[16,4096]{1,0:T(8,128)(2,1)S(1)}, bf16[16,4096]{1,0:T(8,128)(2,1)S(1)}, u32[]{:S(2)}, u32[]{:S(2)}) %collective-permute-start.53) | collective-permute-done | bytes 131104 | tf_op jit(solution)/shard_map/ppermute | solution.py:352
  111.2 4.6 %shard_map.98 = (bf16[16,4096]{1,0:T(8,128)(2,1)S(1)}, bf16[16,4096]{1,0:T(8,128)(2,1)S(1)}, bf16[16,4096]{1,0:T(8,128)(2,1)S(1)}, bf16[16,4096]{1,0:T(8,128)(2,...) custom-call(s32[3]{0:T(128)S(1)} %pad_add_fusion.place, ...), custom_call_target="tpu_custom_call" | custom-call | tf_op jit(solution)/shard_map/pallas_call | solution.py:589
  121.3 1.6 %collective-permute-start.59 = (bf16[16,4096]{1,0:T(8,128)(2,1)S(1)}, bf16[16,4096]{1,0:T(8,128)(2,1)S(1)}, u32[]{:S(2)}, u32[]{:S(2)}) collective-permute-start(bf16[16,4096]{1,0:T(8,128)(2,1)S(1)} %get-tuple-element.247), channel_id=1, source_target_pairs={{0,2},{1,3},{2,0},{3,1},{4,6},{5,7},{6,4},{7,5},{8,10},{9,11},{10,... | collective-permute-start | bytes 393224 | tf_op jit(solution)/shard_map/ppermute | solution.py:352
  129.8 14.8 %collective-permute-start.66 = (bf16[16,4096]{1,0:T(8,128)(2,1)S(1)}, bf16[16,4096]{1,0:T(8,128)(2,1)S(1)}, u32[]{:S(2)}, u32[]{:S(2)}) collective-permute-start(bf16[16,4096]{1,0:T(8,128)(2,1)S(1)} %get-tuple-element.253.refs_0_), channel_id=1, source_target_pairs={{0,1},{1,0},{2,3},{3,2},{4,5},{5,4},{6,7},{7,6},{8,9},{9,8},{10,11... | collective-permute-start | bytes 393224 | tf_op jit(solution)/shard_map/ppermute | solution.py:352
  147.1 2.3 %collective-permute-start.68 = (bf16[16,4096]{1,0:T(8,128)(2,1)S(1)}, bf16[16,4096]{1,0:T(8,128)(2,1)S(1)}, u32[]{:S(2)}, u32[]{:S(2)}) collective-permute-start(bf16[16,4096]{1,0:T(8,128)(2,1)S(1)} %collective-permute-done.60.refs_2_), channel_id=1, source_target_pairs={{0,1},{1,0},{2,3},{3,2},{4,5},{5,4},{6,7},{7,6},{8,9},{9,8},{10,11... | collective-permute-start | bytes 393224 | tf_op jit(solution)/shard_map/ppermute | solution.py:352
  149.9 2.0 %collective-permute-start.70 = (bf16[16,4096]{1,0:T(8,128)(2,1)S(1)}, bf16[16,4096]{1,0:T(8,128)(2,1)S(1)}, u32[]{:S(2)}, u32[]{:S(2)}) collective-permute-start(bf16[16,4096]{1,0:T(8,128)(2,1)S(1)} %collective-permute-done.62.refs_4_), channel_id=1, source_target_pairs={{0,1},{1,0},{2,3},{3,2},{4,5},{5,4},{6,7},{7,6},{8,9},{9,8},{10,11... | collective-permute-start | bytes 393224 | tf_op jit(solution)/shard_map/ppermute | solution.py:352
  154.0 2.0 %shard_map.101 = bf16[2,128,4096]{2,1,0:T(8,128)(2,1)} custom-call(s32[3]{0:T(128)S(1)} %pad_add_fusion.place, bf16[16,4096]{1,0:T(8,128)(2,1)S(1)} %get-tuple-element.253.refs_0_, bf16[16,4096]{1,0:T(8,128)(2,1)S(1)} %get-tuple-element.252.refs_1_, bf16[16,4096]{1,0:T(8,128)(2,1)S(1)} %collective-permute-done.60.refs_2_, ...), custom_call_target="tpu_custom_call" | custom-call | tf_op jit(solution)/shard_map/pallas_call | solution.py:601
  (119 shorter events, 51.1 us)
Async XLA Ops:
  0.1 7.7 %collective-permute-start.12 = (bf16[4096,512]{1,0:T(8,128)(2,1)}, bf16[4096,512]{1,0:T(8,128)(2,1)S(1)}, u32[]{:S(2)}, u32[]{:S(2)}) collective-permute-start(bf16[4096,512]{1,0:T(8,128)(2,1)} %get-tuple-element.127), channel_id=1, source_target_pairs={{0,1},{1,0},{2,3},{3,2},{4,5},{5,4},{6,7},{7,6},{8,9},{9,8},{10,11... | collective-permute-start | bytes 12582920 | tf_op jit(solution)/shard_map/cond/branch_2_fun/ppermute | solution.py:352
  0.8 13.0 %collective-permute-start.13 = (bf16[4096,512]{1,0:T(8,128)(2,1)}, bf16[4096,512]{1,0:T(8,128)(2,1)S(1)}, u32[]{:S(2)}, u32[]{:S(2)}) collective-permute-start(bf16[4096,512]{1,0:T(8,128)(2,1)} %get-tuple-element.128), channel_id=1, source_target_pairs={{0,1},{1,0},{2,3},{3,2},{4,5},{5,4},{6,7},{7,6},{8,9},{9,8},{10,11... | collective-permute-start | bytes 12582920 | tf_op jit(solution)/shard_map/cond/branch_2_fun/ppermute | solution.py:352
  0.9 18.9 %collective-permute-start.14 = (bf16[512,4096]{1,0:T(8,128)(2,1)}, bf16[512,4096]{1,0:T(8,128)(2,1)S(1)}, u32[]{:S(2)}, u32[]{:S(2)}) collective-permute-start(bf16[512,4096]{1,0:T(8,128)(2,1)} %get-tuple-element.129), channel_id=1, source_target_pairs={{0,1},{1,0},{2,3},{3,2},{4,5},{5,4},{6,7},{7,6},{8,9},{9,8},{10,11... | collective-permute-start | bytes 12582920 | tf_op jit(solution)/shard_map/cond/branch_2_fun/ppermute | solution.py:352
  1.3 24.5 %collective-permute-start.15 = (bf16[4096,512]{1,0:T(8,128)(2,1)}, bf16[4096,512]{1,0:T(8,128)(2,1)S(1)}, u32[]{:S(2)}, u32[]{:S(2)}) collective-permute-start(bf16[4096,512]{1,0:T(8,128)(2,1)} %get-tuple-element.130), channel_id=1, source_target_pairs={{0,1},{1,0},{2,3},{3,2},{4,5},{5,4},{6,7},{7,6},{8,9},{9,8},{10,11... | collective-permute-start | bytes 12582920 | tf_op jit(solution)/shard_map/cond/branch_2_fun/ppermute | solution.py:352
  31.8 17.0 %collective-permute-start.26 = (bf16[32,4096]{1,0:T(8,128)(2,1)S(1)}, bf16[32,4096]{1,0:T(8,128)(2,1)S(1)}, u32[]{:S(2)}, u32[]{:S(2)}) collective-permute-start(bf16[32,4096]{1,0:T(8,128)(2,1)S(1)} %get-tuple-element.134), channel_id=1, source_target_pairs={{0,24},{1,25},{2,26},{3,27},{4,28},{5,29},{6,30},{7,31}} | collective-permute-start | bytes 786440 | tf_op jit(solution)/shard_map/cond/branch_0_fun/ppermute | solution.py:355
  48.8 9.7 %collective-permute-start.27 = (bf16[32,4096]{1,0:T(8,128)(2,1)S(1)}, bf16[32,4096]{1,0:T(8,128)(2,1)S(1)}, u32[]{:S(2)}, u32[]{:S(2)}) collective-permute-start(bf16[32,4096]{1,0:T(8,128)(2,1)S(1)} %broadcast_select_fusion.refs_0_), channel_id=1, source_target_pairs={{0,2},{1,3},{2,0},{3,1},{4,6},{5,7},{6,4},{7,5},{8,10},{9,11},{10,... | collective-permute-start | bytes 786440 | tf_op jit(solution)/shard_map/cond/branch_0_fun/ppermute | solution.py:352
  49.8 8.8 %collective-permute-start.28 = (bf16[32,4096]{1,0:T(8,128)(2,1)S(1)}, bf16[32,4096]{1,0:T(8,128)(2,1)S(1)}, u32[]{:S(2)}, u32[]{:S(2)}) collective-permute-start(bf16[32,4096]{1,0:T(8,128)(2,1)S(1)} %broadcast_select_fusion.refs_0_), channel_id=1, source_target_pairs={{0,4},{1,5},{2,6},{3,7},{4,0},{5,1},{6,2},{7,3},{8,12},{9,13},{10,... | collective-permute-start | bytes 786440 | tf_op jit(solution)/shard_map/cond/branch_0_fun/ppermute | solution.py:352
  51.4 10.1 %collective-permute-start.29 = (bf16[32,4096]{1,0:T(8,128)(2,1)S(1)}, bf16[32,4096]{1,0:T(8,128)(2,1)S(1)}, u32[]{:S(2)}, u32[]{:S(2)}) collective-permute-start(bf16[32,4096]{1,0:T(8,128)(2,1)S(1)} %broadcast_select_fusion.refs_0_), channel_id=1, source_target_pairs={{0,6},{1,7},{2,4},{3,5},{4,2},{5,3},{6,0},{7,1},{8,14},{9,15},{10,... | collective-permute-start | bytes 786440 | tf_op jit(solution)/shard_map/cond/branch_0_fun/ppermute | solution.py:352
  84.0 5.3 %collective-permute-start.40 = (bf16[16,4096]{1,0:T(8,128)(2,1)S(1)}, bf16[16,4096]{1,0:T(8,128)(2,1)S(1)}, u32[]{:S(2)}, u32[]{:S(2)}) collective-permute-start(bf16[16,4096]{1,0:T(8,128)(2,1)S(1)} %get-tuple-element.233), channel_id=1, source_target_pairs={{0,6},{1,7},{2,4},{3,5},{4,2},{5,3},{6,0},{7,1},{8,14},{9,15},{10,... | collective-permute-start | bytes 393224 | tf_op jit(solution)/shard_map/ppermute | solution.py:352
  86.7 5.8 %collective-permute-start.44 = (bf16[16,4096]{1,0:T(8,128)(2,1)S(1)}, bf16[16,4096]{1,0:T(8,128)(2,1)S(1)}, u32[]{:S(2)}, u32[]{:S(2)}) collective-permute-start(bf16[16,4096]{1,0:T(8,128)(2,1)S(1)} %get-tuple-element.237), channel_id=1, source_target_pairs={{0,6},{1,7},{2,4},{3,5},{4,2},{5,3},{6,0},{7,1},{8,14},{9,15},{10,... | collective-permute-start | bytes 393224 | tf_op jit(solution)/shard_map/ppermute | solution.py:352
  88.4 5.2 %collective-permute-start.45 = (bf16[16,4096]{1,0:T(8,128)(2,1)S(1)}, bf16[16,4096]{1,0:T(8,128)(2,1)S(1)}, u32[]{:S(2)}, u32[]{:S(2)}) collective-permute-start(bf16[16,4096]{1,0:T(8,128)(2,1)S(1)} %get-tuple-element.238), channel_id=1, source_target_pairs={{0,4},{1,5},{2,6},{3,7},{4,0},{5,1},{6,2},{7,3},{8,12},{9,13},{10,... | collective-permute-start | bytes 393224 | tf_op jit(solution)/shard_map/ppermute | solution.py:352
  91.2 9.2 %collective-permute-start.43 = (bf16[16,4096]{1,0:T(8,128)(2,1)S(1)}, bf16[16,4096]{1,0:T(8,128)(2,1)S(1)}, u32[]{:S(2)}, u32[]{:S(2)}) collective-permute-start(bf16[16,4096]{1,0:T(8,128)(2,1)S(1)} %shard_map.96), channel_id=1, source_target_pairs={{16,24},{17,25},{18,26},{19,27},{20,28},{21,29},{22,30},{23,31}} | collective-permute-start | bytes 393224 | tf_op jit(solution)/shard_map/ppermute | solution.py:355
  94.2 8.8 %collective-permute-start.47 = (bf16[16,4096]{1,0:T(8,128)(2,1)S(1)}, bf16[16,4096]{1,0:T(8,128)(2,1)S(1)}, u32[]{:S(2)}, u32[]{:S(2)}) collective-permute-start(bf16[16,4096]{1,0:T(8,128)(2,1)S(1)} %shard_map.97), channel_id=1, source_target_pairs={{16,24},{17,25},{18,26},{19,27},{20,28},{21,29},{22,30},{23,31}} | collective-permute-start | bytes 393224 | tf_op jit(solution)/shard_map/ppermute | solution.py:355
  115.9 5.4 %collective-permute-start.54 = (bf16[16,4096]{1,0:T(8,128)(2,1)S(1)}, bf16[16,4096]{1,0:T(8,128)(2,1)S(1)}, u32[]{:S(2)}, u32[]{:S(2)}) collective-permute-start(bf16[16,4096]{1,0:T(8,128)(2,1)S(1)} %get-tuple-element.241), channel_id=1, source_target_pairs={{0,6},{1,7},{2,4},{3,5},{4,2},{5,3},{6,0},{7,1},{8,14},{9,15},{10,... | collective-permute-start | bytes 393224 | tf_op jit(solution)/shard_map/ppermute | solution.py:352
  117.1 5.8 %collective-permute-start.55 = (bf16[16,4096]{1,0:T(8,128)(2,1)S(1)}, bf16[16,4096]{1,0:T(8,128)(2,1)S(1)}, u32[]{:S(2)}, u32[]{:S(2)}) collective-permute-start(bf16[16,4096]{1,0:T(8,128)(2,1)S(1)} %get-tuple-element.242), channel_id=1, source_target_pairs={{0,4},{1,5},{2,6},{3,7},{4,0},{5,1},{6,2},{7,3},{8,12},{9,13},{10,... | collective-permute-start | bytes 393224 | tf_op jit(solution)/shard_map/ppermute | solution.py:352
  118.6 6.6 %collective-permute-start.57 = (bf16[16,4096]{1,0:T(8,128)(2,1)S(1)}, bf16[16,4096]{1,0:T(8,128)(2,1)S(1)}, u32[]{:S(2)}, u32[]{:S(2)}) collective-permute-start(bf16[16,4096]{1,0:T(8,128)(2,1)S(1)} %get-tuple-element.245), channel_id=1, source_target_pairs={{0,6},{1,7},{2,4},{3,5},{4,2},{5,3},{6,0},{7,1},{8,14},{9,15},{10,... | collective-permute-start | bytes 393224 | tf_op jit(solution)/shard_map/ppermute | solution.py:352
  119.8 5.8 %collective-permute-start.58 = (bf16[16,4096]{1,0:T(8,128)(2,1)S(1)}, bf16[16,4096]{1,0:T(8,128)(2,1)S(1)}, u32[]{:S(2)}, u32[]{:S(2)}) collective-permute-start(bf16[16,4096]{1,0:T(8,128)(2,1)S(1)} %get-tuple-element.246), channel_id=1, source_target_pairs={{0,4},{1,5},{2,6},{3,7},{4,0},{5,1},{6,2},{7,3},{8,12},{9,13},{10,... | collective-permute-start | bytes 393224 | tf_op jit(solution)/shard_map/ppermute | solution.py:352
  126.8 17.8 %collective-permute-start.60 = (bf16[16,4096]{1,0:T(8,128)(2,1)S(1)}, bf16[16,4096]{1,0:T(8,128)(2,1)S(1)}, u32[]{:S(2)}, u32[]{:S(2)}) collective-permute-start(bf16[16,4096]{1,0:T(8,128)(2,1)S(1)} %get-tuple-element.253.refs_0_), channel_id=1, source_target_pairs={{0,2},{1,3},{2,0},{3,1},{4,6},{5,7},{6,4},{7,5},{8,10},{9,11},{10,... | collective-permute-start | bytes 393224 | tf_op jit(solution)/shard_map/ppermute | solution.py:352
  127.6 17.9 %collective-permute-start.63 = (bf16[16,4096]{1,0:T(8,128)(2,1)S(1)}, bf16[16,4096]{1,0:T(8,128)(2,1)S(1)}, u32[]{:S(2)}, u32[]{:S(2)}) collective-permute-start(bf16[16,4096]{1,0:T(8,128)(2,1)S(1)} %get-tuple-element.252.refs_1_), channel_id=1, source_target_pairs={{0,4},{1,5},{2,6},{3,7},{4,0},{5,1},{6,2},{7,3},{8,12},{9,13},{10,... | collective-permute-start | bytes 393224 | tf_op jit(solution)/shard_map/ppermute | solution.py:352
  128.8 17.9 %collective-permute-start.61 = (bf16[16,4096]{1,0:T(8,128)(2,1)S(1)}, bf16[16,4096]{1,0:T(8,128)(2,1)S(1)}, u32[]{:S(2)}, u32[]{:S(2)}) collective-permute-start(bf16[16,4096]{1,0:T(8,128)(2,1)S(1)} %get-tuple-element.252.refs_1_), channel_id=1, source_target_pairs={{0,2},{1,3},{2,0},{3,1},{4,6},{5,7},{6,4},{7,5},{8,10},{9,11},{10,... | collective-permute-start | bytes 393224 | tf_op jit(solution)/shard_map/ppermute | solution.py:352
  129.1 17.9 %collective-permute-start.62 = (bf16[16,4096]{1,0:T(8,128)(2,1)S(1)}, bf16[16,4096]{1,0:T(8,128)(2,1)S(1)}, u32[]{:S(2)}, u32[]{:S(2)}) collective-permute-start(bf16[16,4096]{1,0:T(8,128)(2,1)S(1)} %get-tuple-element.253.refs_0_), channel_id=1, source_target_pairs={{0,4},{1,5},{2,6},{3,7},{4,0},{5,1},{6,2},{7,3},{8,12},{9,13},{10,... | collective-permute-start | bytes 393224 | tf_op jit(solution)/shard_map/ppermute | solution.py:352
  129.8 19.6 %collective-permute-start.66 = (bf16[16,4096]{1,0:T(8,128)(2,1)S(1)}, bf16[16,4096]{1,0:T(8,128)(2,1)S(1)}, u32[]{:S(2)}, u32[]{:S(2)}) collective-permute-start(bf16[16,4096]{1,0:T(8,128)(2,1)S(1)} %get-tuple-element.253.refs_0_), channel_id=1, source_target_pairs={{0,1},{1,0},{2,3},{3,2},{4,5},{5,4},{6,7},{7,6},{8,9},{9,8},{10,11... | collective-permute-start | bytes 393224 | tf_op jit(solution)/shard_map/ppermute | solution.py:352
  146.7 5.2 %collective-permute-start.65 = (bf16[16,4096]{1,0:T(8,128)(2,1)S(1)}, bf16[16,4096]{1,0:T(8,128)(2,1)S(1)}, u32[]{:S(2)}, u32[]{:S(2)}) collective-permute-start(bf16[16,4096]{1,0:T(8,128)(2,1)S(1)} %collective-permute-done.63.refs_5_), channel_id=1, source_target_pairs={{0,2},{1,3},{2,0},{3,1},{4,6},{5,7},{6,4},{7,5},{8,10},{9,11},{10,... | collective-permute-start | bytes 393224 | tf_op jit(solution)/shard_map/ppermute | solution.py:352
  147.1 5.6 %collective-permute-start.68 = (bf16[16,4096]{1,0:T(8,128)(2,1)S(1)}, bf16[16,4096]{1,0:T(8,128)(2,1)S(1)}, u32[]{:S(2)}, u32[]{:S(2)}) collective-permute-start(bf16[16,4096]{1,0:T(8,128)(2,1)S(1)} %collective-permute-done.60.refs_2_), channel_id=1, source_target_pairs={{0,1},{1,0},{2,3},{3,2},{4,5},{5,4},{6,7},{7,6},{8,9},{9,8},{10,11... | collective-permute-start | bytes 393224 | tf_op jit(solution)/shard_map/ppermute | solution.py:352
  (36 other events, 231.0 us)
